TPU v7x, 32 devices: a whole 2x2x4 slice. The times are simulated.
32 devices in a mesh: inner: 16 (over z, y, core), outer: 2 (over x).
Axes of the slice: x: 2, y: 2, z: 4, core: 2. Of those that a mesh axis runs over, the one named last changes fastest.
Arguments:
- queries: bfloat16 [4096, 1024], P(('outer', 'inner')), may hold values from -8 to 8
- key_rows: bfloat16 [4096, 128], P(('outer', 'inner')), may hold values from -8 to 8
- value_rows: bfloat16 [4096, 128], P(('outer', 'inner')), may hold values from -6 to 6
- grad_output: bfloat16 [4096, 1024], P(('outer', 'inner')), may hold values from -6 to 6
- doc_blocks: int32 [32], replicated, may hold values from 0 to 3, never falling along the last dimension, each value on 1 to 16 neighbouring positions
Outputs:
- grad_queries: bfloat16 [4096, 1024], P(('outer', 'inner'))
- grad_keys: bfloat16 [4096, 128], P(('outer', 'inner'))
- grad_values: bfloat16 [4096, 128], P(('outer', 'inner'))
All inputs are finite; a program needn't handle non-finite values.
Results may differ from a plain program's by a relative error of at most 0.019.
Values may be sent and summed in bfloat16 or wider, within the bound.
No kernel may reach another device: no remote copies, remote signals or barrier semaphores. Data moves between devices by JAX's collectives and lax.ppermute only.
A program may use at most 64 MiB of HBM per device.

v0:
```python
import jax
import jax.numpy as jnp
from jax import lax
from jax.sharding import PartitionSpec as P


def shifted(block, axis, distance):
    devices = range(lax.axis_size(axis))
    route = [(i - distance, i) for i in devices if i - distance in devices]
    return lax.ppermute(block, axis, route)


def shards(queries, key_rows, value_rows, grad_output, doc_blocks):
    token_count = queries.shape[0]
    width = key_rows.shape[1]
    head_count = queries.shape[1] // width
    inner_count = lax.axis_size("inner")
    outer_count = lax.axis_size("outer")
    inner_at = lax.axis_index("inner")
    outer_at = lax.axis_index("outer")
    blocks_dev = doc_blocks.shape[0] // (inner_count * outer_count)
    block_len = token_count // blocks_dev
    tile_blocks = 4
    span_blocks = inner_count * blocks_dev
    win_blocks = -(-(span_blocks + blocks_dev) // tile_blocks) * tile_blocks
    pad_blocks = max(0, (inner_count - 1) * blocks_dev + win_blocks - 2 * span_blocks)
    tile_count = win_blocks // tile_blocks
    tile_len = tile_blocks * block_len
    scaling = width ** (-0.5)
    earlier_k, earlier_v = shifted((key_rows, value_rows), "outer", 1)
    group_k, group_v, prior_k, prior_v = (
        lax.all_gather(key_rows, "inner", axis=0, tiled=True),
        lax.all_gather(value_rows, "inner", axis=0, tiled=True),
        lax.all_gather(earlier_k, "inner", axis=0, tiled=True),
        lax.all_gather(earlier_v, "inner", axis=0, tiled=True),
    )
    padding = jnp.zeros((pad_blocks * block_len, width), key_rows.dtype)
    keys_all = jnp.concatenate([prior_k, group_k, padding], axis=0)
    values_all = jnp.concatenate([prior_v, group_v, padding], axis=0)
    first_block = inner_at * blocks_dev
    key_win = lax.dynamic_slice_in_dim(keys_all, first_block * block_len, win_blocks * block_len, 0)
    value_win = lax.dynamic_slice_in_dim(
        values_all, first_block * block_len, win_blocks * block_len, 0
    )
    tags_pad = jnp.concatenate(
        [
            jnp.full((span_blocks,), -1, jnp.int32),
            doc_blocks,
            jnp.full((span_blocks + pad_blocks,), -1, jnp.int32),
        ]
    )
    key_tags = lax.dynamic_slice_in_dim(
        tags_pad, outer_at * span_blocks + first_block, win_blocks, 0
    )
    own_tags = lax.dynamic_slice_in_dim(
        doc_blocks, (outer_at * inner_count + inner_at) * blocks_dev, blocks_dev, 0
    )
    row_tags = jnp.repeat(jnp.repeat(own_tags, block_len), head_count)
    row_pos = (
        jnp.repeat(jnp.arange(token_count, dtype=jnp.int32), head_count) + span_blocks * block_len
    )
    key_tiles = key_win.reshape(tile_count, tile_len, width)
    value_tiles = value_win.reshape(tile_count, tile_len, width)
    tag_tiles = jnp.repeat(key_tags, block_len).reshape(tile_count, tile_len)
    pos_tiles = jnp.arange(win_blocks * block_len, dtype=jnp.int32).reshape(tile_count, tile_len)
    query_flat = queries.reshape(token_count * head_count, width)
    grad_flat = grad_output.reshape(token_count * head_count, width)
    row_total = token_count * head_count

    def allowed_of(tag_tile, pos_tile):
        return (row_tags[:, None] == tag_tile[None, :]) & (pos_tile[None, :] <= row_pos[:, None])

    def forward_tile(running, pieces):
        key_tile, value_tile, tag_tile, pos_tile = pieces
        allowed = allowed_of(tag_tile, pos_tile)
        row_max, row_sum, out_acc = running
        scores = (
            jnp.einsum("rd,kd->rk", query_flat, key_tile, preferred_element_type=jnp.float32)
            * scaling
        )
        masked = jnp.where(allowed, scores, -jnp.inf)
        new_max = jnp.maximum(row_max, jnp.max(masked, axis=1, keepdims=True))
        factor = jnp.exp(row_max - new_max)
        weights = jnp.exp(masked - new_max)
        new_sum = row_sum * factor + jnp.sum(weights, axis=1, keepdims=True)
        weights_high = weights.astype(jnp.bfloat16)
        weights_rest = (weights - weights_high.astype(jnp.float32)).astype(jnp.bfloat16)
        product = jnp.dot(weights_high, value_tile, preferred_element_type=jnp.float32)
        product = product + jnp.dot(weights_rest, value_tile, preferred_element_type=jnp.float32)
        new_out = out_acc * factor + product
        return ((new_max, new_sum, new_out), None)

    start_state = (
        jnp.full((row_total, 1), -1e30, jnp.float32),
        jnp.zeros((row_total, 1), jnp.float32),
        jnp.zeros((row_total, width), jnp.float32),
    )
    (row_max, row_sum, out_acc), unused_ys = lax.scan(
        forward_tile, start_state, (key_tiles, value_tiles, tag_tiles, pos_tiles)
    )
    attn_out = out_acc / row_sum
    delta = jnp.sum(grad_flat.astype(jnp.float32) * attn_out, axis=1, keepdims=True)

    def backward_tile(grad_q, pieces):
        key_tile, value_tile, tag_tile, pos_tile = pieces
        allowed = allowed_of(tag_tile, pos_tile)
        scores = (
            jnp.einsum("rd,kd->rk", query_flat, key_tile, preferred_element_type=jnp.float32)
            * scaling
        )
        probs = jnp.exp(jnp.where(allowed, scores - row_max, -jnp.inf)) / row_sum
        probs_low = probs.astype(jnp.bfloat16)
        value_part = jnp.einsum(
            "rk,rd->kd", probs_low, grad_flat, preferred_element_type=jnp.float32
        )
        dprobs = jnp.einsum("rd,kd->rk", grad_flat, value_tile, preferred_element_type=jnp.float32)
        dscores = (probs * (dprobs - delta) * scaling).astype(jnp.bfloat16)
        new_q = grad_q + jnp.dot(dscores, key_tile, preferred_element_type=jnp.float32)
        key_part = jnp.einsum("rk,rd->kd", dscores, query_flat, preferred_element_type=jnp.float32)
        return (new_q, (key_part, value_part))

    grad_q, (key_parts, value_parts) = lax.scan(
        backward_tile,
        jnp.zeros((row_total, width), jnp.float32),
        (key_tiles, value_tiles, tag_tiles, pos_tiles),
    )
    grads_win = jnp.concatenate(
        [
            key_parts.reshape(win_blocks * block_len, width),
            value_parts.reshape(win_blocks * block_len, width),
        ],
        axis=1,
    )
    canvas = jnp.zeros(((2 * span_blocks + pad_blocks) * block_len, 2 * width), jnp.float32)
    canvas = lax.dynamic_update_slice_in_dim(canvas, grads_win, first_block * block_len, 0)
    earlier_part = canvas[: span_blocks * block_len]
    group_part = canvas[span_blocks * block_len : 2 * span_blocks * block_len]
    combined = jnp.concatenate([group_part, earlier_part], axis=1)
    summed = lax.psum_scatter(
        combined.astype(jnp.bfloat16), "inner", scatter_dimension=0, tiled=True
    ).astype(jnp.float32)
    returned = shifted(summed[:, 2 * width :].astype(jnp.bfloat16), "outer", -1).astype(jnp.float32)
    grads_kv = summed[:, : 2 * width] + returned
    grad_queries = grad_q.reshape(token_count, head_count * width).astype(jnp.bfloat16)
    return (
        grad_queries,
        grads_kv[:, :width].astype(jnp.bfloat16),
        grads_kv[:, width:].astype(jnp.bfloat16),
    )


def solution(mesh):
    in_specs = (
        P(("outer", "inner"), None),
        P(("outer", "inner"), None),
        P(("outer", "inner"), None),
        P(("outer", "inner"), None),
        P(),
    )
    out_specs = (
        P(("outer", "inner"), None),
        P(("outer", "inner"), None),
        P(("outer", "inner"), None),
    )
    return jax.shard_map(shards, mesh=mesh, in_specs=in_specs, out_specs=out_specs, check_vma=False)
```

profile of v0, /device:TPU:0, one launch (start us, length us, event | category | flops | bytes accessed | tf_op | source)
XLA Modules:
  0.0 221.9 jit_solution(6269202917846839754)
XLA Ops:
  7.2 4.8 %collective-permute-start = (bf16[128,128]{1,0:T(8,128)(2,1)}, bf16[128,128]{1,0:T(8,128)(2,1)S(1)}, u32[]{:S(2)}, u32[]{:S(2)}) collective-permute-start(bf16[128,128]{1,0:T(8,128)(2,1)} %param.10), channel_id=1, source_target_pairs={{0,1},{2,3},{4,5},{6,7},{8,9},{10,11},{12,13},{14,15},{16,17},{18,... | collective-permute-start | bytes 98312 | tf_op jit(solution)/shard_map/ppermute | solution.py:10
  12.1 1.3 collective-permute-start.1
  13.4 23.4 %all_gather.13 = bf16[2048,128]{1,0:T(8,128)(2,1)S(1)} all-gather(bf16[128,128]{1,0:T(8,128)(2,1)} %param.10), channel_id=1, replica_groups=mesh['inner'=16,'outer'=2] {'inner'}, dimensions={0}, use_global_device_ids=true | all-gather | bytes 557056 | tf_op jit(solution)/shard_map/all_gather | solution.py:32
  36.7 20.5 %all_gather.15 = bf16[2048,128]{1,0:T(8,128)(2,1)} all-gather(bf16[128,128]{1,0:T(8,128)(2,1)} %param.11), channel_id=1, replica_groups=mesh['inner'=16,'outer'=2] {'inner'}, dimensions={0}, use_global_device_ids=true | all-gather | bytes 557056 | tf_op jit(solution)/shard_map/all_gather | solution.py:33
  58.3 1.2 dynamic_slice.40
  59.5 1.1 reshape.52
  60.6 1.1 reshape.54
  61.7 20.5 %all_gather.14 = bf16[2048,128]{1,0:T(8,128)(2,1)S(1)} all-gather(bf16[128,128]{1,0:T(8,128)(2,1)S(1)} %collective-permute-done.1), channel_id=1, replica_groups=mesh['inner'=16,'outer'=2] {'inner'}, dimensions={0}, use_global_device_ids=true | all-gather | bytes 557056 | tf_op jit(solution)/shard_map/all_gather | solution.py:35
  82.2 18.9 %all_gather.12 = bf16[2048,128]{1,0:T(8,128)(2,1)S(1)} all-gather(bf16[128,128]{1,0:T(8,128)(2,1)S(1)} %collective-permute-done), channel_id=1, replica_groups=mesh['inner'=16,'outer'=2] {'inner'}, dimensions={0}, use_global_device_ids=true | all-gather | bytes 557056 | tf_op jit(solution)/shard_map/all_gather | solution.py:34
  101.1 3.1 %fusion.43 = (bf16[2560,128]{1,0:T(8,128)(2,1)S(1)}, bf16[2560,128]{1,0:T(8,128)(2,1)S(1)}) fusion(s32[]{:T(128)S(6)} %select_n.20, bf16[2048,128]{1,0:T(8,128)(2,1)S(1)} %all_gather.14, bf16[2048,128]{1,0:T(8,128)(2,1)} %all_gather.15, bf16[2560]{0:T(1024)(128)(2,1)S(1)} %pad_dynamic-slice_fusion.4, bf16[2048,128]{1,0:T(8,128)(2,1)S(1)} %all_gather.13, ...), kind=kLoop, calls=%fused_computation.65 | loop fusion | flops 3604480 | bytes 3412996 | tf_op jit(solution)/shard_map/concatenate | solution.py:39
  104.1 14.9 %while.30 = (s32[]{:T(128)}, f32[1024,1]{0,1:T(1,128)S(1)}, f32[1024,1]{0,1:T(1,128)S(1)}, f32[1024,128]{1,0:T(8,128)S(1)}, s32[5,512]{1,0:T(8,128)S(1)}, /*inde...) while((s32[]{:T(128)}, f32[1024,1]{0,1:T(1,128)S(1)}, ...), condition=%wide.region_3.4_spmd.clone, body=%wide.region_0.3_spmd.clone.sunk | while | flops 410524160 | bytes 11240605 | solution.py:98
  119.4 24.6 %while.31 = (s32[]{:T(128)}, f32[1024,128]{1,0:T(8,128)S(1)}, bf16[5,512,128]{2,1,0:T(8,128)(2,1)}, bf16[5,512,128]{2,1,0:T(8,128)(2,1)}, s32[5,512]{1,0:T(8,128...) while((s32[]{:T(128)}, f32[1024,128]{1,0:T(8,128)S(1)}, ...), condition=%wide.region_6.7_spmd.clone, body=%wide.region_5.6_spmd.clone.sunk | while | flops 677119488 | bytes 12494019 | solution.py:122
  121.1 1.1 fusion.103
  123.2 1.1 fusion.102
  125.1 0.8 fusion.100
  126.0 1.1 fusion.103
  128.2 1.1 fusion.102
  130.0 0.8 fusion.100
  130.9 1.1 fusion.103
  133.1 1.1 fusion.102
  134.9 0.8 fusion.100
  135.8 1.1 fusion.103
  138.0 1.1 fusion.102
  140.7 1.1 fusion.103
  142.9 1.1 fusion.102
  144.1 0.9 copy-done
  145.7 1.5 pad_maximum_fusion
  147.2 59.4 %reduce-scatter.2.cloned.1.call-done = bf16[128,512]{1,0:T(8,128)(2,1)} async-done(((bf16[2048,512]{1,0:T(8,128)(2,1)}), bf16[128,512]{1,0:T(8,128)(2,1)}) %reduce-scatter.2.cloned.1.call-update) | async-done | bytes 131088 | tf_op jit(solution)/shard_map/reduce_scatter | solution.py:139
  206.6 0.8 slice.36
  207.4 1.3 collective-permute-start.2
  209.6 4.0 %collective-permute-done.2 = bf16[128,256]{1,0:T(8,128)(2,1)S(1)} collective-permute-done((bf16[128,256]{1,0:T(8,128)(2,1)S(1)}, bf16[128,256]{1,0:T(8,128)(2,1)S(1)}, u32[]{:S(2)}, u32[]{:S(2)}) %collective-permute-start.2) | collective-permute-done | bytes 65568 | tf_op jit(solution)/shard_map/ppermute | solution.py:10
  213.6 0.9 add_convert_fusion
  (117 shorter events, 29.1 us)
Async XLA Ops:
  7.2 199.4 %reduce-scatter.2.cloned.1.call-start = ((), (), s32[]{:S(2)}) async-start(), calls=%async_computation.1 | async-start | bytes 2228224 | tf_op jit(solution)/shard_map/reduce_scatter | solution.py:139
  7.2 75.0 %collective-permute-start = (bf16[128,128]{1,0:T(8,128)(2,1)}, bf16[128,128]{1,0:T(8,128)(2,1)S(1)}, u32[]{:S(2)}, u32[]{:S(2)}) collective-permute-start(bf16[128,128]{1,0:T(8,128)(2,1)} %param.10), channel_id=1, source_target_pairs={{0,1},{2,3},{4,5},{6,7},{8,9},{10,11},{12,13},{14,15},{16,17},{18,... | collective-permute-start | bytes 98312 | tf_op jit(solution)/shard_map/ppermute | solution.py:10
  12.1 49.6 %collective-permute-start.1 = (bf16[128,128]{1,0:T(8,128)(2,1)}, bf16[128,128]{1,0:T(8,128)(2,1)S(1)}, u32[]{:S(2)}, u32[]{:S(2)}) collective-permute-start(bf16[128,128]{1,0:T(8,128)(2,1)} %param.11), channel_id=1, source_target_pairs={{0,1},{2,3},{4,5},{6,7},{8,9},{10,11},{12,13},{14,15},{16,17},{18,... | collective-permute-start | bytes 98312 | tf_op jit(solution)/shard_map/ppermute | solution.py:10
  144.0 1.1 copy-start
  144.0 1.3 copy-start.1
  207.4 6.1 %collective-permute-start.2 = (bf16[128,256]{1,0:T(8,128)(2,1)S(1)}, bf16[128,256]{1,0:T(8,128)(2,1)S(1)}, u32[]{:S(2)}, u32[]{:S(2)}) collective-permute-start(bf16[128,256]{1,0:T(8,128)(2,1)S(1)} %slice.36), channel_id=1, source_target_pairs={{1,0},{3,2},{5,4},{7,6},{9,8},{11,10},{13,12},{15,14},{17,16},{19,... | collective-permute-start | bytes 196616 | tf_op jit(solution)/shard_map/ppermute | solution.py:10
Sparse Core Ops, SparseCore 0:
  147.3 59.1 reduce-scatter.1
where the time goes:
time: 222 us
  blocking collectives  83.2 us (37%)
  waiting for transfers between devices  63.4 us (29%)
  matrix products  29.4 us (13%)
  other arithmetic  15.3 us (7%)
  between operations  14.1 us (6%)
  local copies, waits for them, and re-layouts  8.41 us (4%)
  starting transfers between devices  7.46 us (3%)
    reduce_scatter x1, waiting for transfers between devices, shards(): lax.psum_scatter(combined.astype(jnp.bfloat16), 'inner', scatter_dimensio...  59.4 us
    all_gather x1, blocking collectives, shards(): lax.all_gather(key_rows, 'inner', axis=0, tiled=True)  23.4 us
    all_gather x1, blocking collectives, shards(): lax.all_gather(value_rows, 'inner', axis=0, tiled=True)  20.5 us
    all_gather x1, blocking collectives, shards(): lax.all_gather(earlier_v, 'inner', axis=0, tiled=True)  20.5 us
    all_gather x1, blocking collectives, shards(): lax.all_gather(earlier_k, 'inner', axis=0, tiled=True)  18.9 us
    ppermute x3, starting transfers between devices, shifted(): return lax.ppermute(block, axis, route)  7.42 us
    eq x10, other arithmetic, allowed_of(): row_tags[:, None] == tag_tile[None, :]  6.52 us
    dot_general x5, matrix products, backward_tile(): jnp.einsum('rk,rd->kd', probs_low, grad_flat, preferred_element_type=jnp....  5.51 us
  transfers between devices with their start and end apart: 4, of which 2 were waited for; matrix products, arithmetic and copies ran while one was open for 2% of the time, Pallas kernels for 0%

commit v1 on v0

v1 whole, which is shorter than its diff:
```python
import functools
import math

import jax
import jax.numpy as jnp
from jax import lax
from jax.experimental import pallas as pl
from jax.experimental.pallas import tpu as pltpu
from jax.sharding import PartitionSpec as P

BLOCKED = -1e30


def window_ids(at, span):
    half = span // 2

    def earlier(t, bit):
        upper = (t // bit) % 2
        return [t - span * upper] + received(t, bit)

    def received(t, bit):
        pieces = [t - half]
        step = half // 2
        while step > bit:
            partner = t + step - 2 * step * ((t // step) % 2)
            pieces = pieces + earlier(partner, step)
            step //= 2
        return pieces

    return [at] + received(at, 0) if span > 1 else [at]


def attention_kernel(span, width, block_len, doc_ref, at_ref, q_ref, g_ref, kv_ref, dq_ref, dkv_ref, kt_ref, s_ref, dp_ref, dk_ref, dv_ref):
    at = at_ref[0]
    keys = span * block_len
    scale = width ** -0.5
    scale2 = scale * math.log2(math.e)
    ids = window_ids(at, span)
    own_doc = doc_ref[at]
    bias = [
        jnp.where((one >= 0) & (doc_ref[jnp.maximum(one, 0)] == own_doc), 0.0, BLOCKED).astype(jnp.float32)
        for one in ids
    ]
    heads = q_ref.shape[1] // width
    pair = 2 * block_len
    per_chunk = 4
    chunks = [(c, min(per_chunk, span - c)) for c in range(0, span, per_chunk)]
    kt_ref[...] = kv_ref[:, :width].T
    key_pos = lax.broadcasted_iota(jnp.int32, (block_len, pair), 0)
    row_pos = lax.broadcasted_iota(jnp.int32, (block_len, pair), 1) % block_len
    causal = key_pos <= row_pos
    nt = (((1,), (1,)), ((), ()))

    def fold(tile, op):
        return op(tile.reshape(-1, 8, pair), axis=0)

    for hp in range(heads // 2):
        left = 2 * hp * width
        q_rows = jnp.concatenate([q_ref[:, left : left + width], q_ref[:, left + width : left + 2 * width]], axis=0)
        g_rows = jnp.concatenate([g_ref[:, left : left + width], g_ref[:, left + width : left + 2 * width]], axis=0)
        top = None
        for first, count in chunks:
            rows = slice(first * block_len, (first + count) * block_len)
            s = lax.dot_general(kv_ref[rows, :width], q_rows, nt, preferred_element_type=jnp.float32)
            for i in range(count):
                part = s[i * block_len : (i + 1) * block_len]
                if first + i == 0:
                    part = jnp.where(causal, part, BLOCKED)
                s_ref[(first + i) * block_len : (first + i + 1) * block_len, :] = part
                best = fold(part, jnp.max) + bias[first + i]
                top = best if top is None else jnp.maximum(top, best)
        top = jnp.max(top, axis=0, keepdims=True) * scale2
        total = jnp.zeros((8, pair), jnp.float32)
        inner = jnp.zeros((8, pair), jnp.float32)
        for first, count in chunks:
            rows = slice(first * block_len, (first + count) * block_len)
            dp = lax.dot_general(kv_ref[rows, width:], g_rows, nt, preferred_element_type=jnp.float32)
            for i in range(count):
                at_rows = slice((first + i) * block_len, (first + i + 1) * block_len)
                dp_part = dp[i * block_len : (i + 1) * block_len]
                p = jnp.exp2(s_ref[at_rows, :] * scale2 + (bias[first + i] - top))
                s_ref[at_rows, :] = p
                dp_ref[at_rows, :] = dp_part
                total = total + fold(p, jnp.sum)
                inner = inner + fold(p * dp_part, jnp.sum)
        total = jnp.sum(total, axis=0, keepdims=True)
        inverse = 1.0 / total
        delta = jnp.sum(inner, axis=0, keepdims=True) * inverse
        scaled = inverse * scale
        dq = None
        for first, count in chunks:
            rows = slice(first * block_len, (first + count) * block_len)
            p = s_ref[rows, :]
            low = (p * inverse).astype(jnp.bfloat16)
            ds = ((p * scaled) * (dp_ref[rows, :] - delta)).astype(jnp.bfloat16)
            dv = jnp.dot(low, g_rows, preferred_element_type=jnp.float32)
            dk = jnp.dot(ds, q_rows, preferred_element_type=jnp.float32)
            part = jnp.dot(kt_ref[:, rows], ds, preferred_element_type=jnp.float32)
            dq = part if dq is None else dq + part
            if hp > 0:
                dk = dk_ref[rows, :] + dk
                dv = dv_ref[rows, :] + dv
            if hp < heads // 2 - 1:
                dk_ref[rows, :] = dk
                dv_ref[rows, :] = dv
            else:
                dkv_ref[rows, :width] = dk.astype(jnp.bfloat16)
                dkv_ref[rows, width:] = dv.astype(jnp.bfloat16)
        for h in range(2):
            dq_ref[:, left + h * width : left + (h + 1) * width] = dq[:, h * block_len : (h + 1) * block_len].T.astype(jnp.bfloat16)


def attention(span, doc_blocks, at, queries, grad_output, kv):
    block_len, columns = queries.shape
    width = kv.shape[1] // 2
    keys = span * block_len
    vmem = pl.BlockSpec(memory_space=pltpu.VMEM)
    smem = pl.BlockSpec(memory_space=pltpu.SMEM)
    rows = columns // width * block_len
    return pl.pallas_call(
        functools.partial(attention_kernel, span, width, block_len),
        out_shape=(
            jax.ShapeDtypeStruct(queries.shape, jnp.bfloat16),
            jax.ShapeDtypeStruct((keys, 2 * width), jnp.bfloat16),
        ),
        in_specs=[smem, smem, vmem, vmem, vmem],
        out_specs=(vmem, vmem),
        scratch_shapes=[
            pltpu.VMEM((width, keys), jnp.bfloat16),
            pltpu.VMEM((keys, 2 * block_len), jnp.float32),
            pltpu.VMEM((keys, 2 * block_len), jnp.float32),
            pltpu.VMEM((keys, width), jnp.float32),
            pltpu.VMEM((keys, width), jnp.float32),
        ],
        compiler_params=pltpu.CompilerParams(vmem_limit_bytes=40 * 1024 * 1024),
        cost_estimate=pl.CostEstimate(
            flops=10 * keys * rows * width,
            bytes_accessed=6 * rows * width + 6 * keys * width * 2,
            transcendentals=keys * rows,
        ),
        name="attention",
    )(doc_blocks, at, queries, grad_output, kv)


def shards(inner_count, outer_count, queries, key_rows, value_rows, grad_output, doc_blocks):
    width = key_rows.shape[1]
    block_len = key_rows.shape[0]
    span = inner_count
    half = span // 2
    devices = inner_count * outer_count
    inner_at = lax.axis_index("inner")
    outer_at = lax.axis_index("outer")
    at = outer_at * inner_count + inner_at

    def place(t):
        return (t % inner_count) * outer_count + t // inner_count

    def moved(x, distance):
        route = [(place(t), place((t + distance) % devices)) for t in range(devices)]
        return lax.ppermute(x, ("inner", "outer"), route)

    def grouped(x, distance):
        return lax.ppermute(x, "outer", [(i, (i + distance) % outer_count) for i in range(outer_count)])

    def swapped(x, bit):
        return lax.ppermute(x, "inner", [(i, i ^ bit) for i in range(inner_count)])

    def upper(bit):
        return (inner_at // bit) % 2 == 1

    own = jnp.concatenate([key_rows, value_rows], axis=1)
    held = moved(own, half)
    prior = grouped(own, 1)
    bits = []
    bit = half // 2
    while bit >= 1:
        bits.append(bit)
        bit //= 2
    for bit in bits:
        first = jnp.where(upper(bit), prior, own)
        held = jnp.concatenate([held, swapped(jnp.concatenate([first, held], axis=0), bit)], axis=0)
    window = jnp.concatenate([own, held], axis=0)

    grad_queries, parts = attention(span, doc_blocks, at.reshape(1), queries, grad_output, window)

    mine = parts[:block_len].astype(jnp.float32)
    before = jnp.zeros_like(mine)
    held = parts[block_len:]
    for bit in reversed(bits):
        kept = held.shape[0] // 2 if False else (half // bit - 1) * block_len
        got = swapped(held[kept:], bit)
        first = got[:block_len].astype(jnp.float32)
        mine = mine + jnp.where(upper(bit), 0.0, first)
        before = before + jnp.where(upper(bit), first, 0.0)
        held = (held[:kept].astype(jnp.float32) + got[block_len:].astype(jnp.float32)).astype(jnp.bfloat16)
    mine = mine + moved(held, -half).astype(jnp.float32) + grouped(before.astype(jnp.bfloat16), -1).astype(jnp.float32)
    grads = mine.astype(jnp.bfloat16)
    return grad_queries, grads[:, :width], grads[:, width:]


def solution(mesh):
    rows = P(("outer", "inner"), None)
    body = functools.partial(shards, mesh.shape["inner"], mesh.shape["outer"])
    return jax.shard_map(
        body, mesh=mesh, in_specs=(rows, rows, rows, rows, P()), out_specs=(rows, rows, rows), check_vma=False
    )
```

time: 222 us -> 56.9 us (0.26)
  blocking collectives: 83.2 us -> 0 us
  waiting for transfers between devices: 63.4 us -> 29.2 us
  matrix products: 29.4 us -> 0 us
  other arithmetic: 15.3 us -> 0.39 us
  between operations: 14.1 us -> 0.79 us
  Pallas kernels: 0 us -> 9.37 us
  starting transfers between devices: 7.46 us -> 14.8 us
  local copies, waits for them, and re-layouts: 8.41 us -> 2.21 us
    all_gather x4 -> x0, blocking collectives: 83.2 us -> none  [the longest x1 23.4 us: shards(): lax.all_gather(key_rows, 'inner', axis=0, tiled=True)]
    reduce_scatter x1 -> x0, waiting for transfers between devices: 59.4 us -> none  [shards(): lax.psum_scatter(combined.astype(jnp.bfloat16), 'inner', scatter_dimensio...]
    dot_general x40 -> x0, matrix products: 29.4 us -> none  [the longest x5 5.51 us: backward_tile(): jnp.einsum('rk,rd->kd', probs_low, grad_flat, preferred_element_type=jnp....]
    ppermute x3 -> x10, waiting for transfers between devices: 4.01 us -> 29.2 us  [the longest x6 22.6 us: swapped(): return lax.ppermute(x, 'inner', [(i, i ^ bit) for i in range(inner_count)])]
    pallas_call x0 -> x1, Pallas kernels: none -> 9.37 us  [attention(): pl.pallas_call(functools.partial(attention_kernel, span, width, block_len...]
    ppermute x3 -> x10, starting transfers between devices: 7.42 us -> 14.8 us  [the longest x6 6.12 us: swapped(): return lax.ppermute(x, 'inner', [(i, i ^ bit) for i in range(inner_count)])]
    eq x10 -> x0, other arithmetic: 6.52 us -> none  [allowed_of(): row_tags[:, None] == tag_tile[None, :]]
    concatenate x3, other arithmetic: 5.31 us -> 0.06 us  [shards(): jnp.concatenate([first, held], axis=0)]
  transfers between devices with their start and end apart: 4 -> 10, of which waited for: 2 -> 9; matrix products, arithmetic and copies ran while one was open for 2% -> 0% of each run, Pallas kernels for 0% -> 0%
where the time goes in v1:
time: 56.9 us; the launch traced here: 56.7 us
  waiting for transfers between devices  29.2 us (51%)
  starting transfers between devices  14.8 us (26%)
  Pallas kernels  9.37 us (16%)
  local copies, waits for them, and re-layouts  2.21 us (4%)
  between operations  0.79 us (1%)
    ppermute x6, waiting for transfers between devices, swapped(): return lax.ppermute(x, 'inner', [(i, i ^ bit) for i in range(inner_count)])  22.6 us
    pallas_call x1, Pallas kernels, attention(): pl.pallas_call(functools.partial(attention_kernel, span, width, block_len...  9.37 us
    ppermute x6, starting transfers between devices, swapped(): return lax.ppermute(x, 'inner', [(i, i ^ bit) for i in range(inner_count)])  6.12 us
    ppermute x2, waiting for transfers between devices, moved(): return lax.ppermute(x, ('inner', 'outer'), route)  5.89 us
    ppermute x2, starting transfers between devices, grouped(): lax.ppermute(x, 'outer', [(i, (i + distance) % outer_count) for i in rang...  4.5 us
    ppermute x2, starting transfers between devices, moved(): return lax.ppermute(x, ('inner', 'outer'), route)  4.16 us
    unnamed x12, local copies, waits for them, and re-layouts  1.46 us
  transfers between devices with their start and end apart: 10, of which 9 were waited for; matrix products, arithmetic and copies ran while one was open for 0% of the time, Pallas kernels for 0%

profile of v1, /device:TPU:0, one launch (start us, length us, event | category | flops | bytes accessed | tf_op | source)
XLA Modules:
  0.0 56.7 jit_solution(10967865874319855617)
XLA Ops:
  0.6 0.0 copy-start.3
  0.6 0.8 %constant_dynamic-update-slice_fusion.1 = (bf16[128,256]{1,0:T(8,128)(2,1)S(1)}, bf16[2048,256]{1,0:T(8,128)(2,1)S(1)}) fusion(bf16[128,128]{1,0:T(8,128)(2,1)} %param.6), kind=kLoop, calls=%fused_computation.25 | loop fusion | bytes 98304
  1.5 3.0 %collective-permute-start.1 = (bf16[128,256]{1,0:T(8,128)(2,1)S(1)}, bf16[128,256]{1,0:T(8,128)(2,1)S(1)}, u32[]{:S(2)}, u32[]{:S(2)}) collective-permute-start(bf16[128,256]{1,0:T(8,128)(2,1)S(1)} %get-tuple-element.14), channel_id=1, source_target_pairs={{0,1},{1,0},{2,3},{3,2},{4,5},{5,4},{6,7},{7,6},{8,9},{9,8},{10,11... | collective-permute-start | bytes 196616 | tf_op jit(solution)/shard_map/ppermute | solution.py:163
  4.5 2.6 %collective-permute-start = (bf16[128,256]{1,0:T(8,128)(2,1)S(1)}, bf16[128,256]{1,0:T(8,128)(2,1)S(1)}, u32[]{:S(2)}, u32[]{:S(2)}) collective-permute-start(bf16[128,256]{1,0:T(8,128)(2,1)S(1)} %get-tuple-element.14), channel_id=1, source_target_pairs={{0,16},{2,18},{4,20},{6,22},{8,24},{10,26},{12,28},{14,30},{16,1},... | collective-permute-start | bytes 196616 | tf_op jit(solution)/shard_map/ppermute | solution.py:160
  7.0 0.0 collective-permute-done.1
  7.1 3.7 %collective-permute-done = bf16[128,256]{1,0:T(8,128)(2,1)S(1)} collective-permute-done((bf16[128,256]{1,0:T(8,128)(2,1)S(1)}, bf16[128,256]{1,0:T(8,128)(2,1)S(1)}, u32[]{:S(2)}, u32[]{:S(2)}) %collective-permute-start) | collective-permute-done | bytes 65568 | tf_op jit(solution)/shard_map/ppermute | solution.py:160
  10.8 1.3 %collective-permute-start.2 = (bf16[256,256]{1,0:T(8,128)(2,1)S(1)}, bf16[256,256]{1,0:T(8,128)(2,1)S(1)}, u32[]{:S(2)}, u32[]{:S(2)}) collective-permute-start(bf16[256,256]{1,0:T(8,128)(2,1)S(1)} %pad_maximum_fusion.2), channel_id=1, source_target_pairs={{0,8},{2,10},{4,12},{6,14},{8,0},{10,2},{12,4},{14,6},{16,24},{18,... | collective-permute-start | bytes 393224 | tf_op jit(solution)/shard_map/ppermute | solution.py:166
  12.2 3.7 %collective-permute-done.2 = bf16[256,256]{1,0:T(8,128)(2,1)S(1)} collective-permute-done((bf16[256,256]{1,0:T(8,128)(2,1)S(1)}, bf16[256,256]{1,0:T(8,128)(2,1)S(1)}, u32[]{:S(2)}, u32[]{:S(2)}) %collective-permute-start.2) | collective-permute-done | bytes 131104 | tf_op jit(solution)/shard_map/ppermute | solution.py:166
  15.9 1.6 %collective-permute-start.3 = (bf16[512,256]{1,0:T(8,128)(2,1)S(1)}, bf16[512,256]{1,0:T(8,128)(2,1)S(1)}, u32[]{:S(2)}, u32[]{:S(2)}) collective-permute-start(bf16[512,256]{1,0:T(8,128)(2,1)S(1)} %pad_maximum_fusion.1), channel_id=1, source_target_pairs={{0,4},{2,6},{4,0},{6,2},{8,12},{10,14},{12,8},{14,10},{16,20},{18,... | collective-permute-start | bytes 786440 | tf_op jit(solution)/shard_map/ppermute | solution.py:166
  17.5 4.9 %collective-permute-done.3 = bf16[512,256]{1,0:T(8,128)(2,1)S(1)} collective-permute-done((bf16[512,256]{1,0:T(8,128)(2,1)S(1)}, bf16[512,256]{1,0:T(8,128)(2,1)S(1)}, u32[]{:S(2)}, u32[]{:S(2)}) %collective-permute-start.3) | collective-permute-done | bytes 262176 | tf_op jit(solution)/shard_map/ppermute | solution.py:166
  22.4 0.1 collective-permute-start.4
  22.5 0.0 copy-start
  22.5 0.0 copy-start.1
  22.5 1.8 %collective-permute-done.4 = bf16[1024,256]{1,0:T(8,128)(2,1)S(1)} collective-permute-done((bf16[1024,256]{1,0:T(8,128)(2,1)S(1)}, bf16[1024,256]{1,0:T(8,128)(2,1)S(1)}, u32[]{:S(2)}, u32[]{:S(2)}) %collective-permute-start.4) | collective-permute-done | bytes 524320 | tf_op jit(solution)/shard_map/ppermute | solution.py:166
  24.4 0.0 copy-start.2
  24.4 0.6 %copy-done.2 = s32[32]{0:T(128)S(1)} copy-done((s32[32]{0:T(128)S(1)}, s32[32]{0:T(128)}, u32[]{:S(2)}) %copy-start.2) | copy-done | bytes 152
  25.0 9.4 %attention.1 = (bf16[128,1024]{1,0:T(8,128)(2,1)}, bf16[2048,256]{1,0:T(8,128)(2,1)S(1)}) custom-call(s32[32]{0:T(128)S(1)} %copy-done.2, s32[1]{0:T(128)} %bitcast.at_ref, bf16[128,1024]{1,0:T(8,128)(2,1)S(1)} %copy-done, bf16[128,1024]{1,0:T(8,128)(2,1)S(1)} %copy-done.1, bf16[2048,256]{1,0:T(8,128)(2,1)S(1)} %constant_dynamic-update-slice_fusion.2.kv_ref), custom_call_target="tpu_custom_call" | custom-call | flops 2684354560 | bytes 3932160 | tf_op jit(solution)/shard_map/attention/pallas_call | solution.py:120
  34.5 0.2 collective-permute-start.5
  34.6 1.8 %collective-permute-done.5 = bf16[1024,256]{1,0:T(8,128)(2,1)S(1)} collective-permute-done((bf16[1024,256]{1,0:T(8,128)(2,1)S(1)}, bf16[1024,256]{1,0:T(8,128)(2,1)S(1)}, u32[]{:S(2)}, u32[]{:S(2)}) %collective-permute-start.5) | collective-permute-done | bytes 524320 | tf_op jit(solution)/shard_map/ppermute | solution.py:166
  36.4 0.1 add_convert_fusion
  36.6 1.6 %collective-permute-start.6 = (bf16[512,256]{1,0:T(8,128)(2,1)S(1)}, bf16[512,256]{1,0:T(8,128)(2,1)S(1)}, u32[]{:S(2)}, u32[]{:S(2)}) collective-permute-start(bf16[512,256]{1,0:T(8,128)(2,1)S(1)} %slice.65), channel_id=1, source_target_pairs={{0,4},{2,6},{4,0},{6,2},{8,12},{10,14},{12,8},{14,10},{16,20},{18,... | collective-permute-start | bytes 786440 | tf_op jit(solution)/shard_map/ppermute | solution.py:166
  38.2 6.8 %collective-permute-done.6 = bf16[512,256]{1,0:T(8,128)(2,1)S(1)} collective-permute-done((bf16[512,256]{1,0:T(8,128)(2,1)S(1)}, bf16[512,256]{1,0:T(8,128)(2,1)S(1)}, u32[]{:S(2)}, u32[]{:S(2)}) %collective-permute-start.6) | collective-permute-done | bytes 262176 | tf_op jit(solution)/shard_map/ppermute | solution.py:166
  45.0 0.1 add_convert_fusion.1
  45.1 1.3 %collective-permute-start.7 = (bf16[256,256]{1,0:T(8,128)(2,1)S(1)}, bf16[256,256]{1,0:T(8,128)(2,1)S(1)}, u32[]{:S(2)}, u32[]{:S(2)}) collective-permute-start(bf16[256,256]{1,0:T(8,128)(2,1)S(1)} %slice.69), channel_id=1, source_target_pairs={{0,8},{2,10},{4,12},{6,14},{8,0},{10,2},{12,4},{14,6},{16,24},{18,... | collective-permute-start | bytes 393224 | tf_op jit(solution)/shard_map/ppermute | solution.py:166
  46.4 3.7 %collective-permute-done.7 = bf16[256,256]{1,0:T(8,128)(2,1)S(1)} collective-permute-done((bf16[256,256]{1,0:T(8,128)(2,1)S(1)}, bf16[256,256]{1,0:T(8,128)(2,1)S(1)}, u32[]{:S(2)}, u32[]{:S(2)}) %collective-permute-start.7) | collective-permute-done | bytes 131104 | tf_op jit(solution)/shard_map/ppermute | solution.py:166
  50.1 0.1 add_convert_fusion.2
  50.2 1.6 %collective-permute-start.8 = (bf16[128,256]{1,0:T(8,128)(2,1)S(1)}, bf16[128,256]{1,0:T(8,128)(2,1)S(1)}, u32[]{:S(2)}, u32[]{:S(2)}) collective-permute-start(bf16[128,256]{1,0:T(8,128)(2,1)S(1)} %get-tuple-element.7), channel_id=1, source_target_pairs={{0,17},{2,19},{4,21},{6,23},{8,25},{10,27},{12,29},{14,31},{16,0},... | collective-permute-start | bytes 196616 | tf_op jit(solution)/shard_map/ppermute | solution.py:160
  51.7 1.5 %collective-permute-start.9 = (bf16[128,256]{1,0:T(8,128)(2,1)S(1)}, bf16[128,256]{1,0:T(8,128)(2,1)S(1)}, u32[]{:S(2)}, u32[]{:S(2)}) collective-permute-start(bf16[128,256]{1,0:T(8,128)(2,1)S(1)} %get-tuple-element.8), channel_id=1, source_target_pairs={{0,1},{1,0},{2,3},{3,2},{4,5},{5,4},{6,7},{7,6},{8,9},{9,8},{10,11... | collective-permute-start | bytes 196616 | tf_op jit(solution)/shard_map/ppermute | solution.py:163
  53.2 2.1 %collective-permute-done.8 = bf16[128,256]{1,0:T(8,128)(2,1)S(1)} collective-permute-done((bf16[128,256]{1,0:T(8,128)(2,1)S(1)}, bf16[128,256]{1,0:T(8,128)(2,1)S(1)}, u32[]{:S(2)}, u32[]{:S(2)}) %collective-permute-start.8) | collective-permute-done | bytes 65568 | tf_op jit(solution)/shard_map/ppermute | solution.py:160
  55.4 0.6 %collective-permute-done.9 = bf16[128,256]{1,0:T(8,128)(2,1)S(1)} collective-permute-done((bf16[128,256]{1,0:T(8,128)(2,1)S(1)}, bf16[128,256]{1,0:T(8,128)(2,1)S(1)}, u32[]{:S(2)}, u32[]{:S(2)}) %collective-permute-start.9) | collective-permute-done | bytes 65568 | tf_op jit(solution)/shard_map/ppermute | solution.py:163
  56.0 0.1 fusion.5
  56.1 0.6 %fusion.9 = (bf16[128,128]{1,0:T(8,128)(2,1)}, bf16[128,128]{1,0:T(8,128)(2,1)}) fusion(bf16[128,256]{1,0:T(8,128)(2,1)S(1)} %fusion.5), kind=kLoop, calls=%fused_computation.32 | loop fusion | bytes 131072 | tf_op jit(solution)/shard_map/slice | solution.py:198
  (15 shorter events, 0.2 us)
Async XLA Ops:
  0.6 0.8 %copy-start.3 = (bf16[128,128]{1,0:T(8,128)(2,1)S(1)}, bf16[128,128]{1,0:T(8,128)(2,1)}, u32[]{:S(2)}) copy-start(bf16[128,128]{1,0:T(8,128)(2,1)} %param.7) | copy-start | bytes 98308
  1.5 5.6 %collective-permute-start.1 = (bf16[128,256]{1,0:T(8,128)(2,1)S(1)}, bf16[128,256]{1,0:T(8,128)(2,1)S(1)}, u32[]{:S(2)}, u32[]{:S(2)}) collective-permute-start(bf16[128,256]{1,0:T(8,128)(2,1)S(1)} %get-tuple-element.14), channel_id=1, source_target_pairs={{0,1},{1,0},{2,3},{3,2},{4,5},{5,4},{6,7},{7,6},{8,9},{9,8},{10,11... | collective-permute-start | bytes 196616 | tf_op jit(solution)/shard_map/ppermute | solution.py:163
  4.5 6.4 %collective-permute-start = (bf16[128,256]{1,0:T(8,128)(2,1)S(1)}, bf16[128,256]{1,0:T(8,128)(2,1)S(1)}, u32[]{:S(2)}, u32[]{:S(2)}) collective-permute-start(bf16[128,256]{1,0:T(8,128)(2,1)S(1)} %get-tuple-element.14), channel_id=1, source_target_pairs={{0,16},{2,18},{4,20},{6,22},{8,24},{10,26},{12,28},{14,30},{16,1},... | collective-permute-start | bytes 196616 | tf_op jit(solution)/shard_map/ppermute | solution.py:160
  10.8 5.0 %collective-permute-start.2 = (bf16[256,256]{1,0:T(8,128)(2,1)S(1)}, bf16[256,256]{1,0:T(8,128)(2,1)S(1)}, u32[]{:S(2)}, u32[]{:S(2)}) collective-permute-start(bf16[256,256]{1,0:T(8,128)(2,1)S(1)} %pad_maximum_fusion.2), channel_id=1, source_target_pairs={{0,8},{2,10},{4,12},{6,14},{8,0},{10,2},{12,4},{14,6},{16,24},{18,... | collective-permute-start | bytes 393224 | tf_op jit(solution)/shard_map/ppermute | solution.py:166
  15.9 6.4 %collective-permute-start.3 = (bf16[512,256]{1,0:T(8,128)(2,1)S(1)}, bf16[512,256]{1,0:T(8,128)(2,1)S(1)}, u32[]{:S(2)}, u32[]{:S(2)}) collective-permute-start(bf16[512,256]{1,0:T(8,128)(2,1)S(1)} %pad_maximum_fusion.1), channel_id=1, source_target_pairs={{0,4},{2,6},{4,0},{6,2},{8,12},{10,14},{12,8},{14,10},{16,20},{18,... | collective-permute-start | bytes 786440 | tf_op jit(solution)/shard_map/ppermute | solution.py:166
  22.4 2.0 %collective-permute-start.4 = (bf16[1024,256]{1,0:T(8,128)(2,1)S(1)}, bf16[1024,256]{1,0:T(8,128)(2,1)S(1)}, u32[]{:S(2)}, u32[]{:S(2)}) collective-permute-start(bf16[1024,256]{1,0:T(8,128)(2,1)S(1)} %pad_maximum_fusion), channel_id=1, source_target_pairs={{0,2},{2,0},{4,6},{6,4},{8,10},{10,8},{12,14},{14,12},{16,18},{18,... | collective-permute-start | bytes 1572872 | tf_op jit(solution)/shard_map/ppermute | solution.py:166
  22.5 1.9 %copy-start = (bf16[128,1024]{1,0:T(8,128)(2,1)S(1)}, bf16[128,1024]{1,0:T(8,128)(2,1)}, u32[]{:S(2)}) copy-start(bf16[128,1024]{1,0:T(8,128)(2,1)} %q_ref.1) | copy-start | bytes 786436
  22.5 1.9 %copy-start.1 = (bf16[128,1024]{1,0:T(8,128)(2,1)S(1)}, bf16[128,1024]{1,0:T(8,128)(2,1)}, u32[]{:S(2)}) copy-start(bf16[128,1024]{1,0:T(8,128)(2,1)} %g_ref.1) | copy-start | bytes 786436
  24.4 0.7 %copy-start.2 = (s32[32]{0:T(128)S(1)}, s32[32]{0:T(128)}, u32[]{:S(2)}) copy-start(s32[32]{0:T(128)} %doc_ref.1) | copy-start | bytes 388
  34.5 2.0 %collective-permute-start.5 = (bf16[1024,256]{1,0:T(8,128)(2,1)S(1)}, bf16[1024,256]{1,0:T(8,128)(2,1)S(1)}, u32[]{:S(2)}, u32[]{:S(2)}) collective-permute-start(bf16[1024,256]{1,0:T(8,128)(2,1)S(1)} %slice.49), channel_id=1, source_target_pairs={{0,2},{2,0},{4,6},{6,4},{8,10},{10,8},{12,14},{14,12},{16,18},{18,... | collective-permute-start | bytes 1572872 | tf_op jit(solution)/shard_map/ppermute | solution.py:166
  36.6 8.4 %collective-permute-start.6 = (bf16[512,256]{1,0:T(8,128)(2,1)S(1)}, bf16[512,256]{1,0:T(8,128)(2,1)S(1)}, u32[]{:S(2)}, u32[]{:S(2)}) collective-permute-start(bf16[512,256]{1,0:T(8,128)(2,1)S(1)} %slice.65), channel_id=1, source_target_pairs={{0,4},{2,6},{4,0},{6,2},{8,12},{10,14},{12,8},{14,10},{16,20},{18,... | collective-permute-start | bytes 786440 | tf_op jit(solution)/shard_map/ppermute | solution.py:166
  45.1 5.0 %collective-permute-start.7 = (bf16[256,256]{1,0:T(8,128)(2,1)S(1)}, bf16[256,256]{1,0:T(8,128)(2,1)S(1)}, u32[]{:S(2)}, u32[]{:S(2)}) collective-permute-start(bf16[256,256]{1,0:T(8,128)(2,1)S(1)} %slice.69), channel_id=1, source_target_pairs={{0,8},{2,10},{4,12},{6,14},{8,0},{10,2},{12,4},{14,6},{16,24},{18,... | collective-permute-start | bytes 393224 | tf_op jit(solution)/shard_map/ppermute | solution.py:166
  50.2 5.2 %collective-permute-start.8 = (bf16[128,256]{1,0:T(8,128)(2,1)S(1)}, bf16[128,256]{1,0:T(8,128)(2,1)S(1)}, u32[]{:S(2)}, u32[]{:S(2)}) collective-permute-start(bf16[128,256]{1,0:T(8,128)(2,1)S(1)} %get-tuple-element.7), channel_id=1, source_target_pairs={{0,17},{2,19},{4,21},{6,23},{8,25},{10,27},{12,29},{14,31},{16,0},... | collective-permute-start | bytes 196616 | tf_op jit(solution)/shard_map/ppermute | solution.py:160
  51.7 4.3 %collective-permute-start.9 = (bf16[128,256]{1,0:T(8,128)(2,1)S(1)}, bf16[128,256]{1,0:T(8,128)(2,1)S(1)}, u32[]{:S(2)}, u32[]{:S(2)}) collective-permute-start(bf16[128,256]{1,0:T(8,128)(2,1)S(1)} %get-tuple-element.8), channel_id=1, source_target_pairs={{0,1},{1,0},{2,3},{3,2},{4,5},{5,4},{6,7},{7,6},{8,9},{9,8},{10,11... | collective-permute-start | bytes 196616 | tf_op jit(solution)/shard_map/ppermute | solution.py:163

commit v2 on v1

v2 whole, which is shorter than its diff:
```python
import functools
import math

import jax
import jax.numpy as jnp
from jax import lax
from jax.experimental import pallas as pl
from jax.experimental.pallas import tpu as pltpu
from jax.sharding import PartitionSpec as P

BLOCKED = -1e30
F32 = jnp.float32
LOW = jnp.bfloat16


def strides(span):
    return list(range(2, span // 2, 2))


def window_ids(at, span):
    def nearest(t, u):
        return jnp.where(u < t, u, u - span)

    def same_core(t):
        others = [t ^ d for d in strides(span)]
        return [nearest(t, u) for u in others], [u - span // 2 for u in others]

    near, far = same_core(at)
    twin = at ^ 1
    twin_near, twin_far = same_core(twin)
    return [at, at - span // 2] + near + far + [nearest(at, twin), twin - span // 2] + twin_near + twin_far


def attention_kernel(span, width, block_len, doc_ref, at_ref, q_ref, g_ref, kv_ref, dq_ref, own_ref, far_ref, nears_ref, fars_ref, twin_near_ref, twin_far_ref, kt_ref, vt_ref, s_ref, p_ref, dk_ref, dv_ref):
    at = at_ref[0]
    keys = span * block_len
    scale = width**-0.5
    scale2 = scale * math.log2(math.e)
    own_doc = doc_ref[at]
    bias = [
        jnp.where((one >= 0) & (doc_ref[jnp.maximum(one, 0)] == own_doc), 0.0, BLOCKED).astype(F32)
        for one in window_ids(at, span)
    ]
    pairs = q_ref.shape[1] // width // 2
    pair = 2 * block_len
    steps = len(strides(span))
    twin = 2 + 2 * steps
    homes = [(own_ref, 0), (far_ref, 0)]
    homes += [(nears_ref, i) for i in range(steps)] + [(fars_ref, i) for i in range(steps)]
    homes += [(twin_near_ref, steps), (twin_far_ref, steps)]
    homes += [(twin_near_ref, i) for i in range(steps)] + [(twin_far_ref, i) for i in range(steps)]
    chunks = [(0, twin), (twin, span - twin)]
    kt_ref[...] = kv_ref[:, :width].T
    vt_ref[:width, :] = kv_ref[:, width:].T
    vt_ref[width:, :] = jnp.ones((vt_ref.shape[0] - width, keys), LOW)
    key_pos = lax.broadcasted_iota(jnp.int32, (block_len, pair), 0)
    row_pos = lax.broadcasted_iota(jnp.int32, (block_len, pair), 1) % block_len
    causal = key_pos <= row_pos
    nt = (((1,), (1,)), ((), ()))
    qt, gt, top, sums, state = ({} for _ in range(5))

    def slot(i):
        return slice(i * block_len, (i + 1) * block_len)

    def turned(ref, hp):
        left = 2 * hp * width
        return jnp.concatenate([ref[:, left : left + width].T, ref[:, left + width : left + 2 * width].T], axis=1)

    def score(hp, chunk):
        first, count = chunk
        rows = slice(first * block_len, (first + count) * block_len)
        s = jnp.dot(kv_ref[rows, :width], qt[hp], preferred_element_type=F32)
        for i in range(count):
            part = s[slot(i)]
            if first + i == 0:
                part = jnp.where(causal, part, BLOCKED)
            s_ref[hp % 2, slot(first + i), :] = part
            best = jnp.max(part.reshape(-1, 8, pair), axis=0) + bias[first + i]
            top[hp] = jnp.maximum(top[hp], best) if hp in top else best

    def weigh(hp, chunk):
        first, count = chunk
        for i in range(first, first + count):
            weights = jnp.exp2(s_ref[hp % 2, slot(i), :] * scale2 + (bias[i] - top[hp]))
            p_ref[hp % 2, slot(i), :] = weights.astype(LOW)
        rows = slice(first * block_len, (first + count) * block_len)
        part = jnp.dot(vt_ref[:, rows], p_ref[hp % 2, rows, :], preferred_element_type=F32)
        sums[hp] = sums[hp] + part if hp in sums else part

    def settle(hp):
        inverse = 1.0 / sums[hp][width : width + 1]
        wide_g = gt[hp].astype(F32)
        delta = jnp.sum(sums[hp][:width] * wide_g, axis=0, keepdims=True) * inverse
        scaled_q = (qt[hp].astype(F32) * (inverse * scale)).astype(LOW)
        scaled_g = (wide_g * inverse).astype(LOW)
        state[hp] = [inverse * scale, delta, scaled_q, scaled_g, None]

    def spread(hp, chunk):
        unused_factor, delta, scaled_q, scaled_g, dq = state[hp]
        first, count = chunk
        rows = slice(first * block_len, (first + count) * block_len)
        dp = jnp.dot(kv_ref[rows, width:], gt[hp], preferred_element_type=F32)
        low = p_ref[hp % 2, rows, :]
        ds = (low.astype(F32) * (dp - delta)).astype(LOW)
        dv = lax.dot_general(low, scaled_g, nt, preferred_element_type=F32)
        dk = lax.dot_general(ds, scaled_q, nt, preferred_element_type=F32)
        part = jnp.dot(kt_ref[:, rows], ds, preferred_element_type=F32)
        state[hp][4] = part if dq is None else dq + part
        if hp > 0:
            dk = dk_ref[rows, :] + dk
            dv = dv_ref[rows, :] + dv
        if hp < pairs - 1:
            dk_ref[rows, :] = dk
            dv_ref[rows, :] = dv
            return
        dk, dv = dk.astype(LOW), dv.astype(LOW)
        for i in range(count):
            home, place = homes[first + i]
            home[slot(place), :width] = dk[slot(i)]
            home[slot(place), width:] = dv[slot(i)]

    def finish(hp):
        left = 2 * hp * width
        dq = state[hp][4] * state[hp][0]
        for h in range(2):
            dq_ref[:, left + h * width : left + (h + 1) * width] = dq[:, slot(h)].T.astype(LOW)

    def load(hp):
        qt[hp], gt[hp] = turned(q_ref, hp), turned(g_ref, hp)

    def peak(hp):
        top[hp] = jnp.max(top[hp], axis=0, keepdims=True) * scale2

    for hp in range(-2, pairs):
        if hp >= 0:
            settle(hp)
        if 0 <= hp + 1 < pairs:
            peak(hp + 1)
        if hp + 2 < pairs:
            load(hp + 2)
        for chunk in chunks:
            if 0 <= hp + 1 < pairs:
                weigh(hp + 1, chunk)
            if hp + 2 < pairs:
                score(hp + 2, chunk)
            if hp >= 0:
                spread(hp, chunk)
        if hp >= 0:
            finish(hp)


def attention(span, doc_blocks, at, queries, grad_output, kv):
    block_len, columns = queries.shape
    width = kv.shape[1] // 2
    keys = span * block_len
    rows = columns // width * block_len
    steps = len(strides(span))
    vmem = pl.BlockSpec(memory_space=pltpu.VMEM)
    smem = pl.BlockSpec(memory_space=pltpu.SMEM)
    slots = [1, 1, steps, steps, steps + 1, steps + 1]
    return pl.pallas_call(
        functools.partial(attention_kernel, span, width, block_len),
        out_shape=(
            jax.ShapeDtypeStruct(queries.shape, LOW),
            *(jax.ShapeDtypeStruct((n * block_len, 2 * width), LOW) for n in slots),
        ),
        in_specs=[smem, smem, vmem, vmem, vmem],
        out_specs=(vmem,) * 7,
        scratch_shapes=[
            pltpu.VMEM((width, keys), LOW),
            pltpu.VMEM((width + 16, keys), LOW),
            pltpu.VMEM((2, keys, 2 * block_len), F32),
            pltpu.VMEM((2, keys, 2 * block_len), LOW),
            pltpu.VMEM((keys, width), F32),
            pltpu.VMEM((keys, width), F32),
        ],
        compiler_params=pltpu.CompilerParams(vmem_limit_bytes=40 * 1024 * 1024),
        cost_estimate=pl.CostEstimate(
            flops=12 * keys * rows * width,
            bytes_accessed=6 * rows * width + 6 * keys * width * 2,
            transcendentals=keys * rows,
        ),
        name="attention",
    )(doc_blocks, at, queries, grad_output, kv)


def shards(inner_count, outer_count, queries, key_rows, value_rows, grad_output, doc_blocks):
    width = key_rows.shape[1]
    block_len = key_rows.shape[0]
    span = inner_count
    half = span // 2
    devices = inner_count * outer_count
    inner_at = lax.axis_index("inner")
    outer_at = lax.axis_index("outer")
    at = outer_at * inner_count + inner_at
    ways = strides(span)

    def place(t):
        return (t % inner_count) * outer_count + t // inner_count

    def moved(x, distance):
        route = [(place(t), place((t + distance) % devices)) for t in range(devices)]
        return lax.ppermute(x, ("inner", "outer"), route)

    def grouped(x, distance):
        return lax.ppermute(x, "outer", [(i, (i + distance) % outer_count) for i in range(outer_count)])

    def swapped(x, d):
        return lax.ppermute(x, "inner", [(i, i ^ d) for i in range(inner_count)])

    def above(d):
        return inner_at > (inner_at ^ d)

    def block(x, i):
        return x[i * block_len : (i + 1) * block_len]

    own = jnp.concatenate([key_rows, value_rows], axis=1)
    prior = grouped(own, 1)
    far = moved(own, half)
    nears = [swapped(jnp.where(above(d), prior, own), d) for d in ways]
    fars = [swapped(far, d) for d in ways]
    nears, fars = jnp.concatenate(nears, axis=0), jnp.concatenate(fars, axis=0)
    twin_first = swapped(jnp.concatenate([jnp.where(above(1), prior, own), far], axis=0), 1)
    twin_nears, twin_fars = swapped(nears, 1), swapped(fars, 1)
    window = jnp.concatenate([own, far, nears, fars, twin_first, twin_nears, twin_fars], axis=0)

    grad_queries, own_part, far_part, near_parts, far_parts, twin_near, twin_far = attention(
        span, doc_blocks, at.reshape(1), queries, grad_output, window
    )

    def added(x, y):
        return (x.astype(F32) + y.astype(F32)).astype(LOW)

    steps = len(ways)
    from_twin_far = swapped(twin_far, 1)
    from_twin_near = swapped(twin_near, 1)
    far_back = [swapped(added(block(far_parts, i), block(from_twin_far, i)), d) for i, d in enumerate(ways)]
    near_back = [swapped(added(block(near_parts, i), block(from_twin_near, i)), d) for i, d in enumerate(ways)]
    far_sum = far_part.astype(F32) + block(from_twin_far, steps).astype(F32)
    for one in far_back:
        far_sum = far_sum + one.astype(F32)
    far_home = moved(far_sum.astype(LOW), -half)
    mine = own_part.astype(F32)
    before = jnp.zeros_like(mine)
    for d, one in zip([1] + ways, [block(from_twin_near, steps)] + near_back):
        one = one.astype(F32)
        mine = mine + jnp.where(above(d), 0.0, one)
        before = before + jnp.where(above(d), one, 0.0)
    prior_home = grouped(before.astype(LOW), -1)
    grads = (mine + far_home.astype(F32) + prior_home.astype(F32)).astype(LOW)
    return grad_queries, grads[:, :width], grads[:, width:]


def solution(mesh):
    rows = P(("outer", "inner"), None)
    body = functools.partial(shards, mesh.shape["inner"], mesh.shape["outer"])
    return jax.shard_map(
        body, mesh=mesh, in_specs=(rows, rows, rows, rows, P()), out_specs=(rows, rows, rows), check_vma=False
    )
```

time: 56.9 us -> 48.2 us (0.85)
  waiting for transfers between devices: 29.2 us -> 11 us
  starting transfers between devices: 14.8 us -> 26.1 us
  Pallas kernels: 9.37 us -> 7.51 us
    ppermute x6 -> x17, waiting for transfers between devices: 22.6 us -> 8.04 us  [swapped(): return lax.ppermute(x, 'inner', [(i, i ^ d) for i in range(inner_count)])]
    ppermute x6 -> x17, starting transfers between devices: 6.12 us -> 15.7 us  [swapped(): return lax.ppermute(x, 'inner', [(i, i ^ d) for i in range(inner_count)])]
    ppermute x2, waiting for transfers between devices: 5.89 us -> 2.93 us  [moved(): return lax.ppermute(x, ('inner', 'outer'), route)]
    pallas_call x1, Pallas kernels: 9.37 us -> 7.51 us  [attention(): pl.pallas_call(functools.partial(attention_kernel, span, width, block_len...]
    ppermute x2, starting transfers between devices: 4.16 us -> 5.76 us  [moved(): return lax.ppermute(x, ('inner', 'outer'), route)]
    ppermute x2, waiting for transfers between devices: 0.63 us -> 0.01 us  [grouped(): lax.ppermute(x, 'outer', [(i, (i + distance) % outer_count) for i in rang...]
    unnamed x12 -> x18, local copies, waits for them, and re-layouts: 1.46 us -> 1.49 us
  transfers between devices with their start and end apart: 10 -> 21, of which waited for: 9 -> 10; matrix products, arithmetic and copies ran while one was open for 0% -> 1% of each run, Pallas kernels for 0% -> 0%
where the time goes in v2:
time: 48.2 us; the launch traced here: 48 us
  starting transfers between devices  26.1 us (54%)
  waiting for transfers between devices  11 us (23%)
  Pallas kernels  7.51 us (16%)
  local copies, waits for them, and re-layouts  2.16 us (4%)
  between operations  0.86 us (2%)
    ppermute x17, starting transfers between devices, swapped(): return lax.ppermute(x, 'inner', [(i, i ^ d) for i in range(inner_count)])  15.7 us
    ppermute x17, waiting for transfers between devices, swapped(): return lax.ppermute(x, 'inner', [(i, i ^ d) for i in range(inner_count)])  8.04 us
    pallas_call x1, Pallas kernels, attention(): pl.pallas_call(functools.partial(attention_kernel, span, width, block_len...  7.51 us
    ppermute x2, starting transfers between devices, moved(): return lax.ppermute(x, ('inner', 'outer'), route)  5.76 us
    ppermute x2, starting transfers between devices, grouped(): lax.ppermute(x, 'outer', [(i, (i + distance) % outer_count) for i in rang...  4.61 us
    ppermute x2, waiting for transfers between devices, moved(): return lax.ppermute(x, ('inner', 'outer'), route)  2.93 us
    unnamed x18, local copies, waits for them, and re-layouts  1.49 us
  transfers between devices with their start and end apart: 21, of which 10 were waited for; matrix products, arithmetic and copies ran while one was open for 1% of the time, Pallas kernels for 0%

profile of v2, /device:TPU:0, one launch (start us, length us, event | category | flops | bytes accessed | tf_op | source)
XLA Modules:
  0.0 48.0 jit_solution(8786342927758224774)
XLA Ops:
  0.6 0.8 %constant_dynamic-update-slice_fusion.1 = (bf16[128,256]{1,0:T(8,128)(2,1)S(1)}, bf16[2048,256]{1,0:T(8,128)(2,1)S(1)}) fusion(bf16[128,128]{1,0:T(8,128)(2,1)} %param.6), kind=kLoop, calls=%fused_computation.34 | loop fusion | bytes 98304
  1.5 3.0 %collective-permute-start.1 = (bf16[128,256]{1,0:T(8,128)(2,1)S(1)}, bf16[128,256]{1,0:T(8,128)(2,1)S(1)}, u32[]{:S(2)}, u32[]{:S(2)}) collective-permute-start(bf16[128,256]{1,0:T(8,128)(2,1)S(1)} %get-tuple-element.29), channel_id=1, source_target_pairs={{0,1},{1,0},{2,3},{3,2},{4,5},{5,4},{6,7},{7,6},{8,9},{9,8},{10,11... | collective-permute-start | bytes 196616 | tf_op jit(solution)/shard_map/ppermute | solution.py:206
  4.5 2.6 %collective-permute-start = (bf16[128,256]{1,0:T(8,128)(2,1)S(1)}, bf16[128,256]{1,0:T(8,128)(2,1)S(1)}, u32[]{:S(2)}, u32[]{:S(2)}) collective-permute-start(bf16[128,256]{1,0:T(8,128)(2,1)S(1)} %get-tuple-element.29), channel_id=1, source_target_pairs={{0,16},{2,18},{4,20},{6,22},{8,24},{10,26},{12,28},{14,30},{16,1},... | collective-permute-start | bytes 196616 | tf_op jit(solution)/shard_map/ppermute | solution.py:203
  7.1 1.8 %collective-permute-start.2 = (bf16[128,256]{1,0:T(8,128)(2,1)S(1)}, bf16[128,256]{1,0:T(8,128)(2,1)S(1)}, u32[]{:S(2)}, u32[]{:S(2)}) collective-permute-start(bf16[128,256]{1,0:T(8,128)(2,1)S(1)} %get-tuple-element.26), channel_id=1, source_target_pairs={{0,4},{2,6},{4,0},{6,2},{8,12},{10,14},{12,8},{14,10},{16,20},{18,... | collective-permute-start | bytes 196616 | tf_op jit(solution)/shard_map/ppermute | solution.py:209
  8.8 1.6 %collective-permute-start.3 = (bf16[128,256]{1,0:T(8,128)(2,1)S(1)}, bf16[128,256]{1,0:T(8,128)(2,1)S(1)}, u32[]{:S(2)}, u32[]{:S(2)}) collective-permute-start(bf16[128,256]{1,0:T(8,128)(2,1)S(1)} %get-tuple-element.25), channel_id=1, source_target_pairs={{0,8},{2,10},{4,12},{6,14},{8,0},{10,2},{12,4},{14,6},{16,24},{18,... | collective-permute-start | bytes 196616 | tf_op jit(solution)/shard_map/ppermute | solution.py:209
  10.4 0.2 collective-permute-start.4
  10.6 0.2 collective-permute-done
  10.9 1.7 %collective-permute-start.5 = (bf16[128,256]{1,0:T(8,128)(2,1)S(1)}, bf16[128,256]{1,0:T(8,128)(2,1)S(1)}, u32[]{:S(2)}, u32[]{:S(2)}) collective-permute-start(bf16[128,256]{1,0:T(8,128)(2,1)S(1)} %collective-permute-done), channel_id=1, source_target_pairs={{0,4},{2,6},{4,0},{6,2},{8,12},{10,14},{12,8},{14,10},{16,20},{18,... | collective-permute-start | bytes 196616 | tf_op jit(solution)/shard_map/ppermute | solution.py:209
  12.6 1.5 %collective-permute-start.6 = (bf16[128,256]{1,0:T(8,128)(2,1)S(1)}, bf16[128,256]{1,0:T(8,128)(2,1)S(1)}, u32[]{:S(2)}, u32[]{:S(2)}) collective-permute-start(bf16[128,256]{1,0:T(8,128)(2,1)S(1)} %collective-permute-done), channel_id=1, source_target_pairs={{0,8},{2,10},{4,12},{6,14},{8,0},{10,2},{12,4},{14,6},{16,24},{18,... | collective-permute-start | bytes 196616 | tf_op jit(solution)/shard_map/ppermute | solution.py:209
  14.2 1.1 %collective-permute-start.7 = (bf16[128,256]{1,0:T(8,128)(2,1)S(1)}, bf16[128,256]{1,0:T(8,128)(2,1)S(1)}, u32[]{:S(2)}, u32[]{:S(2)}) collective-permute-start(bf16[128,256]{1,0:T(8,128)(2,1)S(1)} %collective-permute-done), channel_id=1, source_target_pairs={{0,12},{2,14},{4,8},{6,10},{8,4},{10,6},{12,0},{14,2},{16,28},{18,... | collective-permute-start | bytes 196616 | tf_op jit(solution)/shard_map/ppermute | solution.py:209
  15.3 0.7 %collective-permute-done.4 = bf16[128,256]{1,0:T(8,128)(2,1)S(1)} collective-permute-done((bf16[128,256]{1,0:T(8,128)(2,1)S(1)}, bf16[128,256]{1,0:T(8,128)(2,1)S(1)}, u32[]{:S(2)}, u32[]{:S(2)}) %collective-permute-start.4) | collective-permute-done | bytes 65568 | tf_op jit(solution)/shard_map/ppermute | solution.py:209
  16.1 1.2 %collective-permute-done.6 = bf16[128,256]{1,0:T(8,128)(2,1)S(1)} collective-permute-done((bf16[128,256]{1,0:T(8,128)(2,1)S(1)}, bf16[128,256]{1,0:T(8,128)(2,1)S(1)}, u32[]{:S(2)}, u32[]{:S(2)}) %collective-permute-start.6) | collective-permute-done | bytes 65568 | tf_op jit(solution)/shard_map/ppermute | solution.py:209
  17.3 2.0 %collective-permute-done.7 = bf16[128,256]{1,0:T(8,128)(2,1)S(1)} collective-permute-done((bf16[128,256]{1,0:T(8,128)(2,1)S(1)}, bf16[128,256]{1,0:T(8,128)(2,1)S(1)}, u32[]{:S(2)}, u32[]{:S(2)}) %collective-permute-start.7) | collective-permute-done | bytes 65568 | tf_op jit(solution)/shard_map/ppermute | solution.py:209
  19.6 1.3 %collective-permute-done.10 = bf16[384,256]{1,0:T(8,128)(2,1)S(1)} collective-permute-done((bf16[384,256]{1,0:T(8,128)(2,1)S(1)}, bf16[384,256]{1,0:T(8,128)(2,1)S(1)}, u32[]{:S(2)}, u32[]{:S(2)}) %collective-permute-start.10) | collective-permute-done | bytes 196640 | tf_op jit(solution)/shard_map/ppermute | solution.py:209
  20.9 0.6 %copy-done.2 = s32[32]{0:T(128)S(1)} copy-done((s32[32]{0:T(128)S(1)}, s32[32]{0:T(128)}, u32[]{:S(2)}) %copy-start.2) | copy-done | bytes 152
  21.5 7.5 %attention.1 = (bf16[128,1024]{1,0:T(8,128)(2,1)}, bf16[128,256]{1,0:T(8,128)(2,1)S(1)}, bf16[128,256]{1,0:T(8,128)(2,1)S(1)}, bf16[384,256]{1,0:T(8,128)(2,1)S(...) custom-call(s32[32]{0:T(128)S(1)} %copy-done.2, s32[1]{0:T(128)} %bitcast.at_ref, ...), custom_call_target="tpu_custom_call" | custom-call | flops 3221225472 | bytes 3932160 | tf_op jit(solution)/shard_map/attention/pallas_call | solution.py:161
  29.0 0.2 collective-permute-start.11
  29.2 0.4 collective-permute-start.15
  29.5 1.0 %collective-permute-done.11 = bf16[512,256]{1,0:T(8,128)(2,1)S(1)} collective-permute-done((bf16[512,256]{1,0:T(8,128)(2,1)S(1)}, bf16[512,256]{1,0:T(8,128)(2,1)S(1)}, u32[]{:S(2)}, u32[]{:S(2)}) %collective-permute-start.11) | collective-permute-done | bytes 262176 | tf_op jit(solution)/shard_map/ppermute | solution.py:209
  30.6 1.3 %collective-permute-start.12 = (bf16[128,256]{1,0:T(8,128)(2,1)S(1)}, bf16[128,256]{1,0:T(8,128)(2,1)S(1)}, u32[]{:S(2)}, u32[]{:S(2)}) collective-permute-start(bf16[128,256]{1,0:T(8,128)(2,1)S(1)} %get-tuple-element.22), channel_id=1, source_target_pairs={{0,4},{2,6},{4,0},{6,2},{8,12},{10,14},{12,8},{14,10},{16,20},{18,... | collective-permute-start | bytes 196616 | tf_op jit(solution)/shard_map/ppermute | solution.py:209
  31.9 0.6 %collective-permute-start.13 = (bf16[128,256]{1,0:T(8,128)(2,1)S(1)}, bf16[128,256]{1,0:T(8,128)(2,1)S(1)}, u32[]{:S(2)}, u32[]{:S(2)}) collective-permute-start(bf16[128,256]{1,0:T(8,128)(2,1)S(1)} %get-tuple-element.21), channel_id=1, source_target_pairs={{0,8},{2,10},{4,12},{6,14},{8,0},{10,2},{12,4},{14,6},{16,24},{18,... | collective-permute-start | bytes 196616 | tf_op jit(solution)/shard_map/ppermute | solution.py:209
  32.5 1.6 %collective-permute-start.14 = (bf16[128,256]{1,0:T(8,128)(2,1)S(1)}, bf16[128,256]{1,0:T(8,128)(2,1)S(1)}, u32[]{:S(2)}, u32[]{:S(2)}) collective-permute-start(bf16[128,256]{1,0:T(8,128)(2,1)S(1)} %get-tuple-element.20), channel_id=1, source_target_pairs={{0,12},{2,14},{4,8},{6,10},{8,4},{10,6},{12,0},{14,2},{16,28},{18,... | collective-permute-start | bytes 196616 | tf_op jit(solution)/shard_map/ppermute | solution.py:209
  34.2 1.4 %collective-permute-start.18 = (bf16[128,256]{1,0:T(8,128)(2,1)S(1)}, bf16[128,256]{1,0:T(8,128)(2,1)S(1)}, u32[]{:S(2)}, u32[]{:S(2)}) collective-permute-start(bf16[128,256]{1,0:T(8,128)(2,1)S(1)} %get-tuple-element.18), channel_id=1, source_target_pairs={{0,12},{2,14},{4,8},{6,10},{8,4},{10,6},{12,0},{14,2},{16,28},{18,... | collective-permute-start | bytes 196616 | tf_op jit(solution)/shard_map/ppermute | solution.py:209
  35.6 1.4 %collective-permute-start.17 = (bf16[128,256]{1,0:T(8,128)(2,1)S(1)}, bf16[128,256]{1,0:T(8,128)(2,1)S(1)}, u32[]{:S(2)}, u32[]{:S(2)}) collective-permute-start(bf16[128,256]{1,0:T(8,128)(2,1)S(1)} %get-tuple-element.19), channel_id=1, source_target_pairs={{0,8},{2,10},{4,12},{6,14},{8,0},{10,2},{12,4},{14,6},{16,24},{18,... | collective-permute-start | bytes 196616 | tf_op jit(solution)/shard_map/ppermute | solution.py:209
  37.0 0.8 %collective-permute-start.16 = (bf16[128,256]{1,0:T(8,128)(2,1)S(1)}, bf16[128,256]{1,0:T(8,128)(2,1)S(1)}, u32[]{:S(2)}, u32[]{:S(2)}) collective-permute-start(bf16[128,256]{1,0:T(8,128)(2,1)S(1)} %get-tuple-element.17), channel_id=1, source_target_pairs={{0,4},{2,6},{4,0},{6,2},{8,12},{10,14},{12,8},{14,10},{16,20},{18,... | collective-permute-start | bytes 196616 | tf_op jit(solution)/shard_map/ppermute | solution.py:209
  37.8 0.5 %collective-permute-done.14 = bf16[128,256]{1,0:T(8,128)(2,1)S(1)} collective-permute-done((bf16[128,256]{1,0:T(8,128)(2,1)S(1)}, bf16[128,256]{1,0:T(8,128)(2,1)S(1)}, u32[]{:S(2)}, u32[]{:S(2)}) %collective-permute-start.14) | collective-permute-done | bytes 65568 | tf_op jit(solution)/shard_map/ppermute | solution.py:209
  38.4 1.6 %collective-permute-start.20 = (bf16[128,256]{1,0:T(8,128)(2,1)S(1)}, bf16[128,256]{1,0:T(8,128)(2,1)S(1)}, u32[]{:S(2)}, u32[]{:S(2)}) collective-permute-start(bf16[128,256]{1,0:T(8,128)(2,1)S(1)} %fusion.10), channel_id=1, source_target_pairs={{0,1},{1,0},{2,3},{3,2},{4,5},{5,4},{6,7},{7,6},{8,9},{9,8},{10,11... | collective-permute-start | bytes 196616 | tf_op jit(solution)/shard_map/ppermute | solution.py:206
  40.0 0.2 collective-permute-done.17
  40.1 1.1 %collective-permute-done.16 = bf16[128,256]{1,0:T(8,128)(2,1)S(1)} collective-permute-done((bf16[128,256]{1,0:T(8,128)(2,1)S(1)}, bf16[128,256]{1,0:T(8,128)(2,1)S(1)}, u32[]{:S(2)}, u32[]{:S(2)}) %collective-permute-start.16) | collective-permute-done | bytes 65568 | tf_op jit(solution)/shard_map/ppermute | solution.py:209
  41.3 3.2 %collective-permute-start.19 = (bf16[128,256]{1,0:T(8,128)(2,1)S(1)}, bf16[128,256]{1,0:T(8,128)(2,1)S(1)}, u32[]{:S(2)}, u32[]{:S(2)}) collective-permute-start(bf16[128,256]{1,0:T(8,128)(2,1)S(1)} %add_convert_fusion), channel_id=1, source_target_pairs={{0,17},{2,19},{4,21},{6,23},{8,25},{10,27},{12,29},{14,31},{16,0},... | collective-permute-start | bytes 196616 | tf_op jit(solution)/shard_map/ppermute | solution.py:203
  44.5 2.7 %collective-permute-done.19 = bf16[128,256]{1,0:T(8,128)(2,1)S(1)} collective-permute-done((bf16[128,256]{1,0:T(8,128)(2,1)S(1)}, bf16[128,256]{1,0:T(8,128)(2,1)S(1)}, u32[]{:S(2)}, u32[]{:S(2)}) %collective-permute-start.19) | collective-permute-done | bytes 65568 | tf_op jit(solution)/shard_map/ppermute | solution.py:203
  47.3 0.6 %fusion.11 = (bf16[128,128]{1,0:T(8,128)(2,1)}, bf16[128,128]{1,0:T(8,128)(2,1)}) fusion(bf16[128,256]{1,0:T(8,128)(2,1)S(1)} %fusion.6), kind=kLoop, calls=%fused_computation.47 | loop fusion | bytes 131072 | tf_op jit(solution)/shard_map/slice | solution.py:251
  (41 shorter events, 0.8 us)
Async XLA Ops:
  0.6 0.8 %copy-start.3 = (bf16[128,128]{1,0:T(8,128)(2,1)S(1)}, bf16[128,128]{1,0:T(8,128)(2,1)}, u32[]{:S(2)}) copy-start(bf16[128,128]{1,0:T(8,128)(2,1)} %param.7) | copy-start | bytes 98308
  1.5 5.6 %collective-permute-start.1 = (bf16[128,256]{1,0:T(8,128)(2,1)S(1)}, bf16[128,256]{1,0:T(8,128)(2,1)S(1)}, u32[]{:S(2)}, u32[]{:S(2)}) collective-permute-start(bf16[128,256]{1,0:T(8,128)(2,1)S(1)} %get-tuple-element.29), channel_id=1, source_target_pairs={{0,1},{1,0},{2,3},{3,2},{4,5},{5,4},{6,7},{7,6},{8,9},{9,8},{10,11... | collective-permute-start | bytes 196616 | tf_op jit(solution)/shard_map/ppermute | solution.py:206
  4.5 6.4 %collective-permute-start = (bf16[128,256]{1,0:T(8,128)(2,1)S(1)}, bf16[128,256]{1,0:T(8,128)(2,1)S(1)}, u32[]{:S(2)}, u32[]{:S(2)}) collective-permute-start(bf16[128,256]{1,0:T(8,128)(2,1)S(1)} %get-tuple-element.29), channel_id=1, source_target_pairs={{0,16},{2,18},{4,20},{6,22},{8,24},{10,26},{12,28},{14,30},{16,1},... | collective-permute-start | bytes 196616 | tf_op jit(solution)/shard_map/ppermute | solution.py:203
  7.1 5.5 %collective-permute-start.2 = (bf16[128,256]{1,0:T(8,128)(2,1)S(1)}, bf16[128,256]{1,0:T(8,128)(2,1)S(1)}, u32[]{:S(2)}, u32[]{:S(2)}) collective-permute-start(bf16[128,256]{1,0:T(8,128)(2,1)S(1)} %get-tuple-element.26), channel_id=1, source_target_pairs={{0,4},{2,6},{4,0},{6,2},{8,12},{10,14},{12,8},{14,10},{16,20},{18,... | collective-permute-start | bytes 196616 | tf_op jit(solution)/shard_map/ppermute | solution.py:209
  8.8 5.3 %collective-permute-start.3 = (bf16[128,256]{1,0:T(8,128)(2,1)S(1)}, bf16[128,256]{1,0:T(8,128)(2,1)S(1)}, u32[]{:S(2)}, u32[]{:S(2)}) collective-permute-start(bf16[128,256]{1,0:T(8,128)(2,1)S(1)} %get-tuple-element.25), channel_id=1, source_target_pairs={{0,8},{2,10},{4,12},{6,14},{8,0},{10,2},{12,4},{14,6},{16,24},{18,... | collective-permute-start | bytes 196616 | tf_op jit(solution)/shard_map/ppermute | solution.py:209
  10.4 5.6 %collective-permute-start.4 = (bf16[128,256]{1,0:T(8,128)(2,1)S(1)}, bf16[128,256]{1,0:T(8,128)(2,1)S(1)}, u32[]{:S(2)}, u32[]{:S(2)}) collective-permute-start(bf16[128,256]{1,0:T(8,128)(2,1)S(1)} %get-tuple-element.24), channel_id=1, source_target_pairs={{0,12},{2,14},{4,8},{6,10},{8,4},{10,6},{12,0},{14,2},{16,28},{18,... | collective-permute-start | bytes 196616 | tf_op jit(solution)/shard_map/ppermute | solution.py:209
  10.8 8.7 %collective-permute-start.8 = (bf16[256,256]{1,0:T(8,128)(2,1)S(1)}, bf16[256,256]{1,0:T(8,128)(2,1)S(1)}, u32[]{:S(2)}, u32[]{:S(2)}) collective-permute-start(bf16[256,256]{1,0:T(8,128)(2,1)S(1)} %pad_maximum_fusion.2), channel_id=1, source_target_pairs={{0,2},{2,0},{4,6},{6,4},{8,10},{10,8},{12,14},{14,12},{16,18},{18,... | collective-permute-start | bytes 393224 | tf_op jit(solution)/shard_map/ppermute | solution.py:209
  10.9 5.2 %collective-permute-start.5 = (bf16[128,256]{1,0:T(8,128)(2,1)S(1)}, bf16[128,256]{1,0:T(8,128)(2,1)S(1)}, u32[]{:S(2)}, u32[]{:S(2)}) collective-permute-start(bf16[128,256]{1,0:T(8,128)(2,1)S(1)} %collective-permute-done), channel_id=1, source_target_pairs={{0,4},{2,6},{4,0},{6,2},{8,12},{10,14},{12,8},{14,10},{16,20},{18,... | collective-permute-start | bytes 196616 | tf_op jit(solution)/shard_map/ppermute | solution.py:209
  12.6 4.7 %collective-permute-start.6 = (bf16[128,256]{1,0:T(8,128)(2,1)S(1)}, bf16[128,256]{1,0:T(8,128)(2,1)S(1)}, u32[]{:S(2)}, u32[]{:S(2)}) collective-permute-start(bf16[128,256]{1,0:T(8,128)(2,1)S(1)} %collective-permute-done), channel_id=1, source_target_pairs={{0,8},{2,10},{4,12},{6,14},{8,0},{10,2},{12,4},{14,6},{16,24},{18,... | collective-permute-start | bytes 196616 | tf_op jit(solution)/shard_map/ppermute | solution.py:209
  14.2 5.2 %collective-permute-start.7 = (bf16[128,256]{1,0:T(8,128)(2,1)S(1)}, bf16[128,256]{1,0:T(8,128)(2,1)S(1)}, u32[]{:S(2)}, u32[]{:S(2)}) collective-permute-start(bf16[128,256]{1,0:T(8,128)(2,1)S(1)} %collective-permute-done), channel_id=1, source_target_pairs={{0,12},{2,14},{4,8},{6,10},{8,4},{10,6},{12,0},{14,2},{16,28},{18,... | collective-permute-start | bytes 196616 | tf_op jit(solution)/shard_map/ppermute | solution.py:209
  16.0 3.5 %collective-permute-start.9 = (bf16[384,256]{1,0:T(8,128)(2,1)S(1)}, bf16[384,256]{1,0:T(8,128)(2,1)S(1)}, u32[]{:S(2)}, u32[]{:S(2)}) collective-permute-start(bf16[384,256]{1,0:T(8,128)(2,1)S(1)} %pad_maximum_fusion), channel_id=1, source_target_pairs={{0,2},{2,0},{4,6},{6,4},{8,10},{10,8},{12,14},{14,12},{16,18},{18,... | collective-permute-start | bytes 589832 | tf_op jit(solution)/shard_map/ppermute | solution.py:209
  19.3 1.5 %collective-permute-start.10 = (bf16[384,256]{1,0:T(8,128)(2,1)S(1)}, bf16[384,256]{1,0:T(8,128)(2,1)S(1)}, u32[]{:S(2)}, u32[]{:S(2)}) collective-permute-start(bf16[384,256]{1,0:T(8,128)(2,1)S(1)} %pad_maximum_fusion.1), channel_id=1, source_target_pairs={{0,2},{2,0},{4,6},{6,4},{8,10},{10,8},{12,14},{14,12},{16,18},{18,... | collective-permute-start | bytes 589832 | tf_op jit(solution)/shard_map/ppermute | solution.py:209
  19.5 1.3 %copy-start.1 = (bf16[128,1024]{1,0:T(8,128)(2,1)S(1)}, bf16[128,1024]{1,0:T(8,128)(2,1)}, u32[]{:S(2)}) copy-start(bf16[128,1024]{1,0:T(8,128)(2,1)} %g_ref.1) | copy-start | bytes 786436
  19.6 1.3 %copy-start = (bf16[128,1024]{1,0:T(8,128)(2,1)S(1)}, bf16[128,1024]{1,0:T(8,128)(2,1)}, u32[]{:S(2)}) copy-start(bf16[128,1024]{1,0:T(8,128)(2,1)} %q_ref.1) | copy-start | bytes 786436
  20.9 0.7 %copy-start.2 = (s32[32]{0:T(128)S(1)}, s32[32]{0:T(128)}, u32[]{:S(2)}) copy-start(s32[32]{0:T(128)} %doc_ref.1) | copy-start | bytes 388
  29.0 1.5 %collective-permute-start.11 = (bf16[512,256]{1,0:T(8,128)(2,1)S(1)}, bf16[512,256]{1,0:T(8,128)(2,1)S(1)}, u32[]{:S(2)}, u32[]{:S(2)}) collective-permute-start(bf16[512,256]{1,0:T(8,128)(2,1)S(1)} %get-tuple-element.12), channel_id=1, source_target_pairs={{0,2},{2,0},{4,6},{6,4},{8,10},{10,8},{12,14},{14,12},{16,18},{18,... | collective-permute-start | bytes 786440 | tf_op jit(solution)/shard_map/ppermute | solution.py:209
  29.2 5.0 %collective-permute-start.15 = (bf16[512,256]{1,0:T(8,128)(2,1)S(1)}, bf16[512,256]{1,0:T(8,128)(2,1)S(1)}, u32[]{:S(2)}, u32[]{:S(2)}) collective-permute-start(bf16[512,256]{1,0:T(8,128)(2,1)S(1)} %get-tuple-element.15), channel_id=1, source_target_pairs={{0,2},{2,0},{4,6},{6,4},{8,10},{10,8},{12,14},{14,12},{16,18},{18,... | collective-permute-start | bytes 786440 | tf_op jit(solution)/shard_map/ppermute | solution.py:209
  30.6 6.4 %collective-permute-start.12 = (bf16[128,256]{1,0:T(8,128)(2,1)S(1)}, bf16[128,256]{1,0:T(8,128)(2,1)S(1)}, u32[]{:S(2)}, u32[]{:S(2)}) collective-permute-start(bf16[128,256]{1,0:T(8,128)(2,1)S(1)} %get-tuple-element.22), channel_id=1, source_target_pairs={{0,4},{2,6},{4,0},{6,2},{8,12},{10,14},{12,8},{14,10},{16,20},{18,... | collective-permute-start | bytes 196616 | tf_op jit(solution)/shard_map/ppermute | solution.py:209
  31.9 5.9 %collective-permute-start.13 = (bf16[128,256]{1,0:T(8,128)(2,1)S(1)}, bf16[128,256]{1,0:T(8,128)(2,1)S(1)}, u32[]{:S(2)}, u32[]{:S(2)}) collective-permute-start(bf16[128,256]{1,0:T(8,128)(2,1)S(1)} %get-tuple-element.21), channel_id=1, source_target_pairs={{0,8},{2,10},{4,12},{6,14},{8,0},{10,2},{12,4},{14,6},{16,24},{18,... | collective-permute-start | bytes 196616 | tf_op jit(solution)/shard_map/ppermute | solution.py:209
  32.5 5.8 %collective-permute-start.14 = (bf16[128,256]{1,0:T(8,128)(2,1)S(1)}, bf16[128,256]{1,0:T(8,128)(2,1)S(1)}, u32[]{:S(2)}, u32[]{:S(2)}) collective-permute-start(bf16[128,256]{1,0:T(8,128)(2,1)S(1)} %get-tuple-element.20), channel_id=1, source_target_pairs={{0,12},{2,14},{4,8},{6,10},{8,4},{10,6},{12,0},{14,2},{16,28},{18,... | collective-permute-start | bytes 196616 | tf_op jit(solution)/shard_map/ppermute | solution.py:209
  34.2 5.8 %collective-permute-start.18 = (bf16[128,256]{1,0:T(8,128)(2,1)S(1)}, bf16[128,256]{1,0:T(8,128)(2,1)S(1)}, u32[]{:S(2)}, u32[]{:S(2)}) collective-permute-start(bf16[128,256]{1,0:T(8,128)(2,1)S(1)} %get-tuple-element.18), channel_id=1, source_target_pairs={{0,12},{2,14},{4,8},{6,10},{8,4},{10,6},{12,0},{14,2},{16,28},{18,... | collective-permute-start | bytes 196616 | tf_op jit(solution)/shard_map/ppermute | solution.py:209
  35.6 4.5 %collective-permute-start.17 = (bf16[128,256]{1,0:T(8,128)(2,1)S(1)}, bf16[128,256]{1,0:T(8,128)(2,1)S(1)}, u32[]{:S(2)}, u32[]{:S(2)}) collective-permute-start(bf16[128,256]{1,0:T(8,128)(2,1)S(1)} %get-tuple-element.19), channel_id=1, source_target_pairs={{0,8},{2,10},{4,12},{6,14},{8,0},{10,2},{12,4},{14,6},{16,24},{18,... | collective-permute-start | bytes 196616 | tf_op jit(solution)/shard_map/ppermute | solution.py:209
  37.0 4.3 %collective-permute-start.16 = (bf16[128,256]{1,0:T(8,128)(2,1)S(1)}, bf16[128,256]{1,0:T(8,128)(2,1)S(1)}, u32[]{:S(2)}, u32[]{:S(2)}) collective-permute-start(bf16[128,256]{1,0:T(8,128)(2,1)S(1)} %get-tuple-element.17), channel_id=1, source_target_pairs={{0,4},{2,6},{4,0},{6,2},{8,12},{10,14},{12,8},{14,10},{16,20},{18,... | collective-permute-start | bytes 196616 | tf_op jit(solution)/shard_map/ppermute | solution.py:209
  38.4 6.1 %collective-permute-start.20 = (bf16[128,256]{1,0:T(8,128)(2,1)S(1)}, bf16[128,256]{1,0:T(8,128)(2,1)S(1)}, u32[]{:S(2)}, u32[]{:S(2)}) collective-permute-start(bf16[128,256]{1,0:T(8,128)(2,1)S(1)} %fusion.10), channel_id=1, source_target_pairs={{0,1},{1,0},{2,3},{3,2},{4,5},{5,4},{6,7},{7,6},{8,9},{9,8},{10,11... | collective-permute-start | bytes 196616 | tf_op jit(solution)/shard_map/ppermute | solution.py:206
  41.3 5.9 %collective-permute-start.19 = (bf16[128,256]{1,0:T(8,128)(2,1)S(1)}, bf16[128,256]{1,0:T(8,128)(2,1)S(1)}, u32[]{:S(2)}, u32[]{:S(2)}) collective-permute-start(bf16[128,256]{1,0:T(8,128)(2,1)S(1)} %add_convert_fusion), channel_id=1, source_target_pairs={{0,17},{2,19},{4,21},{6,23},{8,25},{10,27},{12,29},{14,31},{16,0},... | collective-permute-start | bytes 196616 | tf_op jit(solution)/shard_map/ppermute | solution.py:203

commit v3 on v2

v3 whole, which is shorter than its diff:
```python
import functools
import math

import jax
import jax.numpy as jnp
from jax import lax
from jax.experimental import pallas as pl
from jax.experimental.pallas import tpu as pltpu
from jax.sharding import PartitionSpec as P

BLOCKED = -1e30
F32 = jnp.float32
LOW = jnp.bfloat16


def strides(span):
    return list(range(span // 2 - 2, 0, -2))


def window_ids(at, span):
    def nearest(t, u):
        return jnp.where(u < t, u, u - span)

    def same_core(t):
        others = [t ^ d for d in strides(span)]
        return [nearest(t, u) for u in others], [u - span // 2 for u in others]

    near, far = same_core(at)
    twin = at ^ 1
    twin_near, twin_far = same_core(twin)
    early = [at, at - span // 2] + near + [nearest(at, twin), twin - span // 2]
    return early, far + twin_near + twin_far


def biases(doc_ref, at, ids):
    own_doc = doc_ref[at]
    return [
        jnp.where((one >= 0) & (doc_ref[jnp.maximum(one, 0)] == own_doc), 0.0, BLOCKED).astype(F32) for one in ids
    ]


def peaks(tile, bias):
    return jnp.max(tile.reshape(-1, 8, tile.shape[1]), axis=0) + bias


def pack_kernel(k_hbm, v_hbm, kv_ref, arrived):
    width = k_hbm.shape[1]
    copies = [
        pltpu.make_async_copy(one, kv_ref.at[:, pl.ds(i * width, width)], arrived.at[i])
        for i, one in enumerate((k_hbm, v_hbm))
    ]
    for copy in copies:
        copy.start()
    for copy in copies:
        copy.wait()


def early_kernel(span, width, block_len, doc_hbm, at_ref, q_hbm, g_hbm, kv_ref, qt_ref, gt_ref, vt_ref, s_ref, dp_ref, top_ref, bias_ref, q_ref, g_ref, doc_ref, arrived):
    places = enumerate(((q_hbm, q_ref), (g_hbm, g_ref), (doc_hbm, doc_ref)))
    copies = [pltpu.make_async_copy(there, here, arrived.at[i]) for i, (there, here) in places]
    for copy in copies:
        copy.start()
    pair = 2 * block_len
    vt_ref[:width, :] = kv_ref[:, width:].T
    vt_ref[width:, :] = jnp.ones((vt_ref.shape[0] - width, vt_ref.shape[1]), LOW)
    key_pos = lax.broadcasted_iota(jnp.int32, (block_len, pair), 0)
    row_pos = lax.broadcasted_iota(jnp.int32, (block_len, pair), 1) % block_len
    causal = key_pos <= row_pos
    for copy in copies:
        copy.wait()
    at = at_ref[0]
    early_ids, late_ids = window_ids(at, span)
    bias = biases(doc_ref, at, early_ids + late_ids)
    for i, one in enumerate(bias):
        bias_ref[8 * i : 8 * i + 8, :] = jnp.full((8, pair), one)
    for hp in range(q_ref.shape[1] // width // 2):
        left = 2 * hp * width
        lanes = slice(hp * pair, (hp + 1) * pair)
        for h in range(2):
            head = slice(left + h * width, left + (h + 1) * width)
            place = slice(hp * pair + h * block_len, hp * pair + (h + 1) * block_len)
            qt_ref[:, place] = q_ref[:, head].T
            gt_ref[:, place] = g_ref[:, head].T
        s = jnp.dot(kv_ref[:, :width], qt_ref[:, lanes], preferred_element_type=F32)
        dp_ref[:, lanes] = jnp.dot(kv_ref[:, width:], gt_ref[:, lanes], preferred_element_type=F32)
        top = None
        for i, one in enumerate(bias[: len(early_ids)]):
            slot = slice(i * block_len, (i + 1) * block_len)
            part = s[slot]
            if i == 0:
                part = jnp.where(causal, part, BLOCKED)
            s_ref[slot, lanes] = part
            best = peaks(part, one)
            top = best if top is None else jnp.maximum(top, best)
        top_ref[:, lanes] = top


def main_kernel(span, width, block_len, bias_ref, qt_ref, gt_ref, vte_ref, se_ref, dpe_ref, tope_ref, kv_ref, first_ref, twin_near_ref, twin_far_ref, p_ref, ds_ref, sq_ref, sg_ref, factor_ref, vt_ref, s_ref, dk_ref, dv_ref):
    scale = width**-0.5
    scale2 = scale * math.log2(math.e)
    pairs = qt_ref.shape[1] // block_len // 2
    pair = 2 * block_len
    steps = len(strides(span))
    early = steps + 4
    vt_ref[:width, :] = kv_ref[:, width:].T
    vt_ref[width:, :] = jnp.ones((vt_ref.shape[0] - width, vt_ref.shape[1]), LOW)
    nt = (((1,), (1,)), ((), ()))
    homes = [(first_ref, 0), (twin_far_ref, steps)]
    homes += [(twin_near_ref, i) for i in range(steps)] + [(twin_far_ref, i) for i in range(steps)]
    twin_slots = {0: (early - 2, 2, 0), 1: (early + steps, 2 * steps, 2)}
    spans = {0: (0, early), 1: (early, span)}
    top, sums, state = {}, {}, {}

    def rows_of(first, end):
        return slice(first * block_len, end * block_len)

    def lanes_of(hp):
        return slice(hp * pair, (hp + 1) * pair)

    def score(hp):
        s = jnp.dot(kv_ref[:, :width], qt_ref[:, lanes_of(hp)], preferred_element_type=F32)
        s_ref[hp % 2, :, :] = s
        top[hp] = tope_ref[:, lanes_of(hp)]
        for i in range(early, span):
            top[hp] = jnp.maximum(top[hp], peaks(s[rows_of(i - early, i - early + 1)], bias_ref[8 * i : 8 * i + 8, :]))

    def peak(hp):
        top[hp] = jnp.max(top[hp], axis=0, keepdims=True) * scale2

    def weigh(hp, part):
        first, end = spans[part]
        for i in range(first, end):
            s = s_ref[hp % 2, rows_of(i - early, i - early + 1), :] if part else se_ref[rows_of(i, i + 1), lanes_of(hp)]
            p_ref[rows_of(i, i + 1), lanes_of(hp)] = jnp.exp2(s * scale2 + (bias_ref[8 * i : 8 * i + 1, :] - top[hp])).astype(LOW)
        turned = vt_ref if part else vte_ref
        more = jnp.dot(turned[...], p_ref[rows_of(first, end), lanes_of(hp)], preferred_element_type=F32)
        sums[hp] = sums[hp] + more if hp in sums else more

    def settle(hp):
        inverse = 1.0 / sums[hp][width : width + 1]
        wide_g = gt_ref[:, lanes_of(hp)].astype(F32)
        delta = jnp.sum(sums[hp][:width] * wide_g, axis=0, keepdims=True) * inverse
        scaled_q = (qt_ref[:, lanes_of(hp)].astype(F32) * (inverse * scale)).astype(LOW)
        scaled_g = (wide_g * inverse).astype(LOW)
        sq_ref[:, lanes_of(hp)] = scaled_q
        sg_ref[:, lanes_of(hp)] = scaled_g
        factor_ref[:, lanes_of(hp)] = jnp.broadcast_to(inverse * scale, (8, pair))
        state[hp] = (delta, scaled_q, scaled_g)

    def spread(hp, part):
        delta, scaled_q, scaled_g = state[hp]
        first, end = spans[part]
        rows = rows_of(first, end)
        if part:
            dp = jnp.dot(kv_ref[:, width:], gt_ref[:, lanes_of(hp)], preferred_element_type=F32)
        else:
            dp = dpe_ref[:, lanes_of(hp)]
        ds_ref[rows, lanes_of(hp)] = (p_ref[rows, lanes_of(hp)].astype(F32) * (dp - delta)).astype(LOW)
        at_slot, count, place = twin_slots[part]
        rows, kept = rows_of(at_slot, at_slot + count), rows_of(place, place + count)
        dv = lax.dot_general(p_ref[rows, lanes_of(hp)], scaled_g, nt, preferred_element_type=F32)
        dk = lax.dot_general(ds_ref[rows, lanes_of(hp)], scaled_q, nt, preferred_element_type=F32)
        if hp > 0:
            dk = dk_ref[kept, :] + dk
            dv = dv_ref[kept, :] + dv
        if hp < pairs - 1:
            dk_ref[kept, :] = dk
            dv_ref[kept, :] = dv
            return
        dk, dv = dk.astype(LOW), dv.astype(LOW)
        for i in range(count):
            home, where = homes[place + i]
            home[rows_of(where, where + 1), :width] = dk[rows_of(i, i + 1)]
            home[rows_of(where, where + 1), width:] = dv[rows_of(i, i + 1)]

    for hp in range(-2, pairs):
        if hp >= 0:
            settle(hp)
        if 0 <= hp + 1 < pairs:
            peak(hp + 1)
        for part in (0, 1):
            if 0 <= hp + 1 < pairs:
                weigh(hp + 1, part)
            if hp + 2 < pairs and part == 0:
                score(hp + 2)
            if hp >= 0:
                spread(hp, part)


def kept_kernel(span, width, block_len, p_ref, ds_ref, sq_ref, sg_ref, own_ref, far_ref, nears_ref, fars_ref):
    steps = len(strides(span))
    nt = (((1,), (1,)), ((), ()))
    for slot, refs in ((0, (own_ref, far_ref, nears_ref)), (4 + steps, (fars_ref,))):
        count = sum(ref.shape[0] for ref in refs)
        rows = slice(slot * block_len, slot * block_len + count)
        dk = lax.dot_general(ds_ref[rows, :], sq_ref[...], nt, preferred_element_type=F32).astype(LOW)
        dv = lax.dot_general(p_ref[rows, :], sg_ref[...], nt, preferred_element_type=F32).astype(LOW)
        first = 0
        for ref in refs:
            ref[:, :width] = dk[first : first + ref.shape[0]]
            ref[:, width:] = dv[first : first + ref.shape[0]]
            first += ref.shape[0]


def query_kernel(width, block_len, unused_ref, ds_ref, factor_ref, early_ref, late_ref, dq_ref):
    early = early_ref.shape[0]
    early_t, late_t = early_ref[:, :width].T, late_ref[:, :width].T
    pair = 2 * block_len
    for hp in range(dq_ref.shape[1] // width // 2):
        lanes = slice(hp * pair, (hp + 1) * pair)
        dq = jnp.dot(early_t, ds_ref[:early, lanes], preferred_element_type=F32)
        dq = dq + jnp.dot(late_t, ds_ref[early:, lanes], preferred_element_type=F32)
        dq = dq * factor_ref[0:1, lanes]
        for h in range(2):
            head = slice((2 * hp + h) * width, (2 * hp + h + 1) * width)
            dq_ref[:, head] = dq[:, h * block_len : (h + 1) * block_len].T.astype(LOW)


HBM = pl.BlockSpec(memory_space=pltpu.HBM)
VMEM = pl.BlockSpec(memory_space=pltpu.VMEM)
SMEM = pl.BlockSpec(memory_space=pltpu.SMEM)


def in_hbm(x):
    return pltpu.with_memory_space_constraint(x, pltpu.HBM)


def call(body, name, ins, outs, scratch, flops, *operands):
    return pl.pallas_call(
        body,
        out_shape=tuple(jax.ShapeDtypeStruct(shape, kind) for shape, kind in outs),
        in_specs=ins,
        out_specs=(VMEM,) * len(outs),
        scratch_shapes=scratch,
        compiler_params=pltpu.CompilerParams(vmem_limit_bytes=24 * 1024 * 1024),
        cost_estimate=pl.CostEstimate(flops=flops, bytes_accessed=1 << 16, transcendentals=0),
        name=name,
    )(*operands)


def shards(inner_count, outer_count, queries, key_rows, value_rows, grad_output, doc_blocks):
    width = key_rows.shape[1]
    block_len = key_rows.shape[0]
    span = inner_count
    half = span // 2
    devices = inner_count * outer_count
    inner_at = lax.axis_index("inner")
    outer_at = lax.axis_index("outer")
    at = outer_at * inner_count + inner_at
    ways = strides(span)

    def place(t):
        return (t % inner_count) * outer_count + t // inner_count

    def moved(x, distance):
        route = [(place(t), place((t + distance) % devices)) for t in range(devices)]
        return lax.ppermute(x, ("inner", "outer"), route)

    def grouped(x, distance):
        return lax.ppermute(x, "outer", [(i, (i + distance) % outer_count) for i in range(outer_count)])

    def returned(x, d):
        route = []
        for t in range(devices):
            u = t ^ d
            route.append((place(t), place(u if u < t else (u - inner_count) % devices)))
        return lax.ppermute(x, ("inner", "outer"), route)

    def swapped(x, d):
        return lax.ppermute(x, "inner", [(i, i ^ d) for i in range(inner_count)])

    def above(d):
        return inner_at > (inner_at ^ d)

    def block(x, i):
        return x[i * block_len : (i + 1) * block_len]

    (own,) = call(
        pack_kernel,
        "pack",
        [HBM, HBM],
        [((block_len, 2 * width), LOW)],
        [pltpu.SemaphoreType.DMA((2,))],
        0,
        *(in_hbm(key_rows), in_hbm(value_rows)),
    )
    prior = grouped(own, 1)
    far = moved(own, half)
    nears = [swapped(jnp.where(above(d), prior, own), d) for d in ways]
    fars = [swapped(far, d) for d in ways[:-1]]
    nears, later_far = lax.optimization_barrier((jnp.concatenate(nears, axis=0), far))
    fars = jnp.concatenate(fars + [swapped(later_far, ways[-1])], axis=0)
    twin_first = swapped(jnp.concatenate([jnp.where(above(1), prior, own), far], axis=0), 1)
    twin_nears = swapped(nears, 1)
    early = jnp.concatenate([own, far, nears, twin_first], axis=0)

    steps = len(ways)
    heads = queries.shape[1] // width
    rows, keys = heads * block_len, span * block_len
    pair = 2 * block_len
    work = 2 * rows * width * block_len
    place_here = at.reshape(1)
    here = early.shape[0]
    turned = ((width, rows), LOW)

    def parts(n):
        return ((n * block_len, 2 * width), LOW)

    qt, gt, early_vt, early_s, early_dp, early_top, bias = call(
        functools.partial(early_kernel, span, width, block_len),
        "early",
        [HBM, SMEM, HBM, HBM, VMEM],
        [
            *(turned, turned, ((width + 16, here), LOW), ((here, rows), F32), ((here, rows), F32), ((8, rows), F32)),
            ((8 * span, pair), F32),
        ],
        [
            pltpu.VMEM(queries.shape, LOW),
            pltpu.VMEM(queries.shape, LOW),
            pltpu.SMEM(doc_blocks.shape, jnp.int32),
            pltpu.SemaphoreType.DMA((3,)),
        ],
        40 * work * (here // block_len),
        *(in_hbm(doc_blocks), place_here, in_hbm(queries), in_hbm(grad_output), early),
    )
    late = jnp.concatenate([fars, twin_nears, swapped(fars, 1)], axis=0)
    first_part, twin_near, twin_far, p, ds, scaled_q, scaled_g, factor = call(
        functools.partial(main_kernel, span, width, block_len),
        "main",
        [VMEM] * 8,
        [parts(1), parts(steps), parts(steps + 1), ((keys, rows), LOW), ((keys, rows), LOW), turned, turned, ((8, rows), F32)],
        [
            pltpu.VMEM((width + 16, keys - here), LOW),
            pltpu.VMEM((2, keys - here, pair), F32),
            pltpu.VMEM((keys // 2, width), F32),
            pltpu.VMEM((keys // 2, width), F32),
        ],
        6 * work * span,
        *(bias, qt, gt, early_vt, early_s, early_dp, early_top, late),
    )
    own_part, far_part, near_parts, far_parts = call(
        functools.partial(kept_kernel, span, width, block_len),
        "kept",
        [VMEM] * 4,
        [parts(1), parts(1), parts(steps), parts(steps)],
        [],
        work * span,
        *(p, ds, scaled_q, scaled_g),
    )

    def added(x, y):
        return (x.astype(F32) + y.astype(F32)).astype(LOW)

    from_twin_far = swapped(twin_far, 1)
    from_twin_near = swapped(twin_near, 1)
    far_back = [swapped(added(block(far_parts, i), block(from_twin_far, i)), d) for i, d in enumerate(ways)]
    near_sums = [added(block(near_parts, i), block(from_twin_near, i)) for i in range(steps)]
    far_sum = far_part.astype(F32) + block(from_twin_far, steps).astype(F32)
    for one in far_back:
        far_sum = far_sum + one.astype(F32)
    far_sum = far_sum.astype(LOW)
    near_home = [returned(first_part, 1)] + [returned(one, d) for one, d in zip(near_sums, ways)]
    far_home = moved(far_sum, -half)
    (grad_queries,) = call(
        functools.partial(query_kernel, width, block_len),
        "query",
        [pl.BlockSpec(memory_space=pl.ANY)] + [VMEM] * 4,
        [(queries.shape, LOW)],
        [],
        work * span,
        *(far_sum, ds, factor, early, late),
    )
    mine = own_part.astype(F32)
    for one in near_home + [far_home]:
        mine = mine + one.astype(F32)
    grads = mine.astype(LOW)
    return grad_queries, grads[:, :width], grads[:, width:]


def solution(mesh):
    rows = P(("outer", "inner"), None)
    body = functools.partial(shards, mesh.shape["inner"], mesh.shape["outer"])
    return jax.shard_map(
        body, mesh=mesh, in_specs=(rows, rows, rows, rows, P()), out_specs=(rows, rows, rows), check_vma=False
    )
```

time: 48.2 us -> 44.8 us (0.929)
  waiting for transfers between devices: 11 us -> 3.99 us
  Pallas kernels: 7.51 us -> 11 us
  starting transfers between devices: 26.1 us -> 27.8 us
  local copies, waits for them, and re-layouts: 2.16 us -> 0.68 us
    ppermute x0 -> x4, starting transfers between devices: none -> 5.79 us  [returned(): return lax.ppermute(x, ('inner', 'outer'), route)]
    ppermute x17 -> x14, waiting for transfers between devices: 8.04 us -> 3.16 us  [swapped(): return lax.ppermute(x, 'inner', [(i, i ^ d) for i in range(inner_count)])]
    pallas_call x1 -> x5, Pallas kernels: 7.51 us -> 11 us  [call(): pl.pallas_call(body, out_shape=tuple((jax.ShapeDtypeStruct(shape, kind) f...]
    ppermute x17 -> x14, starting transfers between devices: 15.7 us -> 13.5 us  [swapped(): return lax.ppermute(x, 'inner', [(i, i ^ d) for i in range(inner_count)])]
    ppermute x2, waiting for transfers between devices: 2.93 us -> 0.82 us  [moved(): return lax.ppermute(x, ('inner', 'outer'), route)]
    ppermute x2 -> x1, starting transfers between devices: 4.61 us -> 3 us  [grouped(): lax.ppermute(x, 'outer', [(i, (i + distance) % outer_count) for i in rang...]
    unnamed x18 -> x4, local copies, waits for them, and re-layouts: 1.49 us -> 0.03 us
  transfers between devices with their start and end apart: 21 -> 21, of which waited for: 10 -> 6; matrix products, arithmetic and copies ran while one was open for 1% -> 1% of each run, Pallas kernels for 0% -> 12%
where the time goes in v3:
time: 44.8 us; the launch traced here: 44.5 us
  starting transfers between devices  27.8 us (62%)
  Pallas kernels  11 us (25%)
  waiting for transfers between devices  3.99 us (9%)
  between operations  0.81 us (2%)
  local copies, waits for them, and re-layouts  0.68 us (2%)
    ppermute x14, starting transfers between devices, swapped(): return lax.ppermute(x, 'inner', [(i, i ^ d) for i in range(inner_count)])  13.5 us
    pallas_call x5, Pallas kernels, call(): pl.pallas_call(body, out_shape=tuple((jax.ShapeDtypeStruct(shape, kind) f...  11 us
    ppermute x4, starting transfers between devices, returned(): return lax.ppermute(x, ('inner', 'outer'), route)  5.79 us
    ppermute x2, starting transfers between devices, moved(): return lax.ppermute(x, ('inner', 'outer'), route)  5.57 us
    ppermute x14, waiting for transfers between devices, swapped(): return lax.ppermute(x, 'inner', [(i, i ^ d) for i in range(inner_count)])  3.16 us
    ppermute x1, starting transfers between devices, grouped(): lax.ppermute(x, 'outer', [(i, (i + distance) % outer_count) for i in rang...  3 us
  transfers between devices with their start and end apart: 21, of which 6 were waited for; matrix products, arithmetic and copies ran while one was open for 1% of the time, Pallas kernels for 12%

profile of v3, /device:TPU:0, one launch (start us, length us, event | category | flops | bytes accessed | tf_op | source)
XLA Modules:
  0.0 44.5 jit_solution(4174774453681011537)
XLA Ops:
  0.6 0.8 %pack.1 = bf16[128,256]{1,0:T(8,128)(2,1)S(1)} custom-call(bf16[128,128]{1,0:T(8,128)(2,1)} %k_hbm.1, bf16[128,128]{1,0:T(8,128)(2,1)} %v_hbm.1), custom_call_target="tpu_custom_call" | custom-call | bytes 65536 | tf_op jit(solution)/shard_map/pack/pallas_call | solution.py:229
  1.4 3.0 %collective-permute-start.1 = (bf16[128,256]{1,0:T(8,128)(2,1)S(1)}, bf16[128,256]{1,0:T(8,128)(2,1)S(1)}, u32[]{:S(2)}, u32[]{:S(2)}) collective-permute-start(bf16[128,256]{1,0:T(8,128)(2,1)S(1)} %pack.1), channel_id=1, source_target_pairs={{0,1},{1,0},{2,3},{3,2},{4,5},{5,4},{6,7},{7,6},{8,9},{9,8},{10,11... | collective-permute-start | bytes 196616 | tf_op jit(solution)/shard_map/ppermute | solution.py:260
  4.4 2.6 %collective-permute-start = (bf16[128,256]{1,0:T(8,128)(2,1)S(1)}, bf16[128,256]{1,0:T(8,128)(2,1)S(1)}, u32[]{:S(2)}, u32[]{:S(2)}) collective-permute-start(bf16[128,256]{1,0:T(8,128)(2,1)S(1)} %pack.1), channel_id=1, source_target_pairs={{0,16},{2,18},{4,20},{6,22},{8,24},{10,26},{12,28},{14,30},{16,1},... | collective-permute-start | bytes 196616 | tf_op jit(solution)/shard_map/ppermute | solution.py:257
  7.1 2.8 %collective-permute-start.2 = (bf16[128,256]{1,0:T(8,128)(2,1)S(1)}, bf16[128,256]{1,0:T(8,128)(2,1)S(1)}, u32[]{:S(2)}, u32[]{:S(2)}) collective-permute-start(bf16[128,256]{1,0:T(8,128)(2,1)S(1)} %get-tuple-element.51), channel_id=1, source_target_pairs={{0,12},{2,14},{4,8},{6,10},{8,4},{10,6},{12,0},{14,2},{16,28},{18,... | collective-permute-start | bytes 196616 | tf_op jit(solution)/shard_map/ppermute | solution.py:270
  9.8 0.5 %collective-permute-start.4 = (bf16[128,256]{1,0:T(8,128)(2,1)S(1)}, bf16[128,256]{1,0:T(8,128)(2,1)S(1)}, u32[]{:S(2)}, u32[]{:S(2)}) collective-permute-start(bf16[128,256]{1,0:T(8,128)(2,1)S(1)} %get-tuple-element.53), channel_id=1, source_target_pairs={{0,4},{2,6},{4,0},{6,2},{8,12},{10,14},{12,8},{14,10},{16,20},{18,... | collective-permute-start | bytes 196616 | tf_op jit(solution)/shard_map/ppermute | solution.py:270
  10.3 0.3 collective-permute-start.3
  10.6 0.2 collective-permute-done
  10.8 0.1 collective-permute-start.5
  10.9 1.6 %collective-permute-start.7 = (bf16[128,256]{1,0:T(8,128)(2,1)S(1)}, bf16[128,256]{1,0:T(8,128)(2,1)S(1)}, u32[]{:S(2)}, u32[]{:S(2)}) collective-permute-start(bf16[128,256]{1,0:T(8,128)(2,1)S(1)} %collective-permute-done), channel_id=1, source_target_pairs={{0,8},{2,10},{4,12},{6,14},{8,0},{10,2},{12,4},{14,6},{16,24},{18,... | collective-permute-start | bytes 196616 | tf_op jit(solution)/shard_map/ppermute | solution.py:270
  12.5 2.5 %collective-permute-start.6 = (bf16[128,256]{1,0:T(8,128)(2,1)S(1)}, bf16[128,256]{1,0:T(8,128)(2,1)S(1)}, u32[]{:S(2)}, u32[]{:S(2)}) collective-permute-start(bf16[128,256]{1,0:T(8,128)(2,1)S(1)} %collective-permute-done), channel_id=1, source_target_pairs={{0,12},{2,14},{4,8},{6,10},{8,4},{10,6},{12,0},{14,2},{16,28},{18,... | collective-permute-start | bytes 196616 | tf_op jit(solution)/shard_map/ppermute | solution.py:270
  15.0 0.2 collective-permute-done.3
  15.2 1.6 %collective-permute-start.8 = (bf16[128,256]{1,0:T(8,128)(2,1)S(1)}, bf16[128,256]{1,0:T(8,128)(2,1)S(1)}, u32[]{:S(2)}, u32[]{:S(2)}) collective-permute-start(bf16[128,256]{1,0:T(8,128)(2,1)S(1)} %collective-permute-done), channel_id=1, source_target_pairs={{0,4},{2,6},{4,0},{6,2},{8,12},{10,14},{12,8},{14,10},{16,20},{18,... | collective-permute-start | bytes 196616 | tf_op jit(solution)/shard_map/ppermute | solution.py:270
  16.8 1.7 %collective-permute-done.6 = bf16[128,256]{1,0:T(8,128)(2,1)S(1)} collective-permute-done((bf16[128,256]{1,0:T(8,128)(2,1)S(1)}, bf16[128,256]{1,0:T(8,128)(2,1)S(1)}, u32[]{:S(2)}, u32[]{:S(2)}) %collective-permute-start.6) | collective-permute-done | bytes 65568 | tf_op jit(solution)/shard_map/ppermute | solution.py:270
  18.5 1.0 %collective-permute-done.8 = bf16[128,256]{1,0:T(8,128)(2,1)S(1)} collective-permute-done((bf16[128,256]{1,0:T(8,128)(2,1)S(1)}, bf16[128,256]{1,0:T(8,128)(2,1)S(1)}, u32[]{:S(2)}, u32[]{:S(2)}) %collective-permute-start.8) | collective-permute-done | bytes 65568 | tf_op jit(solution)/shard_map/ppermute | solution.py:270
  19.5 0.1 collective-permute-start.10
  19.7 2.3 %early.1 = (bf16[128,1024]{1,0:T(8,128)(2,1)S(1)}, bf16[128,1024]{1,0:T(8,128)(2,1)S(1)}, bf16[144,896]{1,0:T(8,128)(2,1)S(1)}, f32[896,1024]{1,0:T(8,128)S(1)},...) custom-call(s32[32]{0:T(128)} %doc_hbm.1, s32[1]{0:T(128)} %bitcast.at_ref, ...), custom_call_target="tpu_custom_call" | custom-call | flops 9395240960 | bytes 65536 | tf_op jit(solution)/shard_map/early/pallas_call | solution.py:229
  22.1 5.0 %main.1 = (bf16[128,256]{1,0:T(8,128)(2,1)S(1)}, bf16[384,256]{1,0:T(8,128)(2,1)S(1)}, bf16[512,256]{1,0:T(8,128)(2,1)S(1)}, bf16[2048,1024]{1,0:T(8,128)(2,1)S(...) custom-call(f32[128,256]{1,0:T(8,128)S(1)} %get-tuple-element.25.bia, ...), custom_call_target="tpu_custom_call" | custom-call | flops 3221225472 | bytes 65536 | tf_op jit(solution)/shard_map/main/pallas_call | solution.py:229
  27.1 0.6 %collective-permute-start.11 = (bf16[512,256]{1,0:T(8,128)(2,1)S(1)}, bf16[512,256]{1,0:T(8,128)(2,1)S(1)}, u32[]{:S(2)}, u32[]{:S(2)}) collective-permute-start(bf16[512,256]{1,0:T(8,128)(2,1)S(1)} %get-tuple-element.38), channel_id=1, source_target_pairs={{0,2},{2,0},{4,6},{6,4},{8,10},{10,8},{12,14},{14,12},{16,18},{18,... | collective-permute-start | bytes 786440 | tf_op jit(solution)/shard_map/ppermute | solution.py:270
  27.6 1.2 %collective-permute-start.15 = (bf16[128,256]{1,0:T(8,128)(2,1)S(1)}, bf16[128,256]{1,0:T(8,128)(2,1)S(1)}, u32[]{:S(2)}, u32[]{:S(2)}) collective-permute-start(bf16[128,256]{1,0:T(8,128)(2,1)S(1)} %get-tuple-element.42), channel_id=1, source_target_pairs={{0,3},{2,0},{4,7},{6,4},{8,11},{10,8},{12,15},{14,12},{16,19},{18,... | collective-permute-start | bytes 196616 | tf_op jit(solution)/shard_map/ppermute | solution.py:267
  28.8 1.2 %kept.1 = (bf16[128,256]{1,0:T(8,128)(2,1)S(1)}, bf16[128,256]{1,0:T(8,128)(2,1)S(1)}, bf16[384,256]{1,0:T(8,128)(2,1)S(1)}, bf16[384,256]{1,0:T(8,128)(2,1)S(1)}) custom-call(bf16[2048,1024]{1,0:T(8,128)(2,1)S(1)} %get-tuple-element.33.p_ref, bf16[2048,1024]{1,0:T(8,128)(2,1)S(1)} %get-tuple-element.34.ds_ref, ...), custom_call_target="tpu_custom_call" | custom-call | flops 536870912 | bytes 65536 | tf_op jit(solution)/shard_map/kept/pallas_call | solution.py:229
  30.1 1.5 %collective-permute-start.12 = (bf16[128,256]{1,0:T(8,128)(2,1)S(1)}, bf16[128,256]{1,0:T(8,128)(2,1)S(1)}, u32[]{:S(2)}, u32[]{:S(2)}) collective-permute-start(bf16[128,256]{1,0:T(8,128)(2,1)S(1)} %get-tuple-element.45), channel_id=1, source_target_pairs={{0,12},{2,14},{4,8},{6,10},{8,4},{10,6},{12,0},{14,2},{16,28},{18,... | collective-permute-start | bytes 196616 | tf_op jit(solution)/shard_map/ppermute | solution.py:270
  31.6 1.1 %collective-permute-start.14 = (bf16[128,256]{1,0:T(8,128)(2,1)S(1)}, bf16[128,256]{1,0:T(8,128)(2,1)S(1)}, u32[]{:S(2)}, u32[]{:S(2)}) collective-permute-start(bf16[128,256]{1,0:T(8,128)(2,1)S(1)} %get-tuple-element.46), channel_id=1, source_target_pairs={{0,4},{2,6},{4,0},{6,2},{8,12},{10,14},{12,8},{14,10},{16,20},{18,... | collective-permute-start | bytes 196616 | tf_op jit(solution)/shard_map/ppermute | solution.py:270
  32.7 1.0 %collective-permute-start.13 = (bf16[128,256]{1,0:T(8,128)(2,1)S(1)}, bf16[128,256]{1,0:T(8,128)(2,1)S(1)}, u32[]{:S(2)}, u32[]{:S(2)}) collective-permute-start(bf16[128,256]{1,0:T(8,128)(2,1)S(1)} %get-tuple-element.47), channel_id=1, source_target_pairs={{0,8},{2,10},{4,12},{6,14},{8,0},{10,2},{12,4},{14,6},{16,24},{18,... | collective-permute-start | bytes 196616 | tf_op jit(solution)/shard_map/ppermute | solution.py:270
  33.8 1.7 %collective-permute-start.17 = (bf16[128,256]{1,0:T(8,128)(2,1)S(1)}, bf16[128,256]{1,0:T(8,128)(2,1)S(1)}, u32[]{:S(2)}, u32[]{:S(2)}) collective-permute-start(bf16[128,256]{1,0:T(8,128)(2,1)S(1)} %get-tuple-element.48), channel_id=1, source_target_pairs={{0,13},{2,15},{4,9},{6,11},{8,4},{10,6},{12,0},{14,2},{16,29},{18,... | collective-permute-start | bytes 196616 | tf_op jit(solution)/shard_map/ppermute | solution.py:267
  35.5 0.2 collective-permute-done.12
  35.7 2.0 %collective-permute-start.19 = (bf16[128,256]{1,0:T(8,128)(2,1)S(1)}, bf16[128,256]{1,0:T(8,128)(2,1)S(1)}, u32[]{:S(2)}, u32[]{:S(2)}) collective-permute-start(bf16[128,256]{1,0:T(8,128)(2,1)S(1)} %get-tuple-element.49), channel_id=1, source_target_pairs={{0,5},{2,7},{4,0},{6,2},{8,13},{10,15},{12,8},{14,10},{16,21},{18,... | collective-permute-start | bytes 196616 | tf_op jit(solution)/shard_map/ppermute | solution.py:267
  37.7 0.9 %collective-permute-start.18 = (bf16[128,256]{1,0:T(8,128)(2,1)S(1)}, bf16[128,256]{1,0:T(8,128)(2,1)S(1)}, u32[]{:S(2)}, u32[]{:S(2)}) collective-permute-start(bf16[128,256]{1,0:T(8,128)(2,1)S(1)} %get-tuple-element.50), channel_id=1, source_target_pairs={{0,9},{2,11},{4,13},{6,15},{8,0},{10,2},{12,4},{14,6},{16,25},{18,... | collective-permute-start | bytes 196616 | tf_op jit(solution)/shard_map/ppermute | solution.py:267
  38.6 3.0 %collective-permute-start.20 = (bf16[128,256]{1,0:T(8,128)(2,1)S(1)}, bf16[128,256]{1,0:T(8,128)(2,1)S(1)}, u32[]{:S(2)}, u32[]{:S(2)}) collective-permute-start(bf16[128,256]{1,0:T(8,128)(2,1)S(1)} %add_convert_fusion.4.unused_ref), channel_id=1, source_target_pairs={{0,17},{2,19},{4,21},{6,23},{8,25},{10,27},{12,29},{14,31},{16,0},... | collective-permute-start | bytes 196616 | tf_op jit(solution)/shard_map/ppermute | solution.py:257
  41.6 1.6 %query.1 = bf16[128,1024]{1,0:T(8,128)(2,1)} custom-call(bf16[128,256]{1,0:T(8,128)(2,1)S(1)} %add_convert_fusion.4.unused_ref, bf16[2048,1024]{1,0:T(8,128)(2,1)S(1)} %get-tuple-element.34.ds_ref, f32[8,1024]{1,0:T(8,128)S(1)} %get-tuple-element.40.factor_ref, bf16[896,256]{1,0:T(8,128)(2,1)S(1)} %pad_maximum_fusion.kv_ref.early_ref, ...), custom_call_target="tpu_custom_call" | custom-call | flops 536870912 | bytes 65536 | tf_op jit(solution)/shard_map/query/pallas_call | solution.py:229
  43.3 0.6 %collective-permute-done.20 = bf16[128,256]{1,0:T(8,128)(2,1)S(1)} collective-permute-done((bf16[128,256]{1,0:T(8,128)(2,1)S(1)}, bf16[128,256]{1,0:T(8,128)(2,1)S(1)}, u32[]{:S(2)}, u32[]{:S(2)}) %collective-permute-start.20) | collective-permute-done | bytes 65568 | tf_op jit(solution)/shard_map/ppermute | solution.py:257
  43.9 0.1 add_convert_fusion
  43.9 0.6 %fusion = (bf16[128,128]{1,0:T(8,128)(2,1)}, bf16[128,128]{1,0:T(8,128)(2,1)}) fusion(bf16[128,256]{1,0:T(8,128)(2,1)S(1)} %add_convert_fusion), kind=kLoop, calls=%fused_computation.21 | loop fusion | bytes 131072 | tf_op jit(solution)/shard_map/slice | solution.py:377
  (30 shorter events, 0.3 us)
Async XLA Ops:
  1.4 5.6 %collective-permute-start.1 = (bf16[128,256]{1,0:T(8,128)(2,1)S(1)}, bf16[128,256]{1,0:T(8,128)(2,1)S(1)}, u32[]{:S(2)}, u32[]{:S(2)}) collective-permute-start(bf16[128,256]{1,0:T(8,128)(2,1)S(1)} %pack.1), channel_id=1, source_target_pairs={{0,1},{1,0},{2,3},{3,2},{4,5},{5,4},{6,7},{7,6},{8,9},{9,8},{10,11... | collective-permute-start | bytes 196616 | tf_op jit(solution)/shard_map/ppermute | solution.py:260
  4.4 6.4 %collective-permute-start = (bf16[128,256]{1,0:T(8,128)(2,1)S(1)}, bf16[128,256]{1,0:T(8,128)(2,1)S(1)}, u32[]{:S(2)}, u32[]{:S(2)}) collective-permute-start(bf16[128,256]{1,0:T(8,128)(2,1)S(1)} %pack.1), channel_id=1, source_target_pairs={{0,16},{2,18},{4,20},{6,22},{8,24},{10,26},{12,28},{14,30},{16,1},... | collective-permute-start | bytes 196616 | tf_op jit(solution)/shard_map/ppermute | solution.py:257
  7.1 5.5 %collective-permute-start.2 = (bf16[128,256]{1,0:T(8,128)(2,1)S(1)}, bf16[128,256]{1,0:T(8,128)(2,1)S(1)}, u32[]{:S(2)}, u32[]{:S(2)}) collective-permute-start(bf16[128,256]{1,0:T(8,128)(2,1)S(1)} %get-tuple-element.51), channel_id=1, source_target_pairs={{0,12},{2,14},{4,8},{6,10},{8,4},{10,6},{12,0},{14,2},{16,28},{18,... | collective-permute-start | bytes 196616 | tf_op jit(solution)/shard_map/ppermute | solution.py:270
  9.8 5.2 %collective-permute-start.4 = (bf16[128,256]{1,0:T(8,128)(2,1)S(1)}, bf16[128,256]{1,0:T(8,128)(2,1)S(1)}, u32[]{:S(2)}, u32[]{:S(2)}) collective-permute-start(bf16[128,256]{1,0:T(8,128)(2,1)S(1)} %get-tuple-element.53), channel_id=1, source_target_pairs={{0,4},{2,6},{4,0},{6,2},{8,12},{10,14},{12,8},{14,10},{16,20},{18,... | collective-permute-start | bytes 196616 | tf_op jit(solution)/shard_map/ppermute | solution.py:270
  10.3 4.8 %collective-permute-start.3 = (bf16[128,256]{1,0:T(8,128)(2,1)S(1)}, bf16[128,256]{1,0:T(8,128)(2,1)S(1)}, u32[]{:S(2)}, u32[]{:S(2)}) collective-permute-start(bf16[128,256]{1,0:T(8,128)(2,1)S(1)} %get-tuple-element.54), channel_id=1, source_target_pairs={{0,8},{2,10},{4,12},{6,14},{8,0},{10,2},{12,4},{14,6},{16,24},{18,... | collective-permute-start | bytes 196616 | tf_op jit(solution)/shard_map/ppermute | solution.py:270
  10.8 8.8 %collective-permute-start.5 = (bf16[256,256]{1,0:T(8,128)(2,1)S(1)}, bf16[256,256]{1,0:T(8,128)(2,1)S(1)}, u32[]{:S(2)}, u32[]{:S(2)}) collective-permute-start(bf16[256,256]{1,0:T(8,128)(2,1)S(1)} %pad_maximum_fusion.3), channel_id=1, source_target_pairs={{0,2},{2,0},{4,6},{6,4},{8,10},{10,8},{12,14},{14,12},{16,18},{18,... | collective-permute-start | bytes 393224 | tf_op jit(solution)/shard_map/ppermute | solution.py:270
  10.9 7.6 %collective-permute-start.7 = (bf16[128,256]{1,0:T(8,128)(2,1)S(1)}, bf16[128,256]{1,0:T(8,128)(2,1)S(1)}, u32[]{:S(2)}, u32[]{:S(2)}) collective-permute-start(bf16[128,256]{1,0:T(8,128)(2,1)S(1)} %collective-permute-done), channel_id=1, source_target_pairs={{0,8},{2,10},{4,12},{6,14},{8,0},{10,2},{12,4},{14,6},{16,24},{18,... | collective-permute-start | bytes 196616 | tf_op jit(solution)/shard_map/ppermute | solution.py:270
  12.5 5.9 %collective-permute-start.6 = (bf16[128,256]{1,0:T(8,128)(2,1)S(1)}, bf16[128,256]{1,0:T(8,128)(2,1)S(1)}, u32[]{:S(2)}, u32[]{:S(2)}) collective-permute-start(bf16[128,256]{1,0:T(8,128)(2,1)S(1)} %collective-permute-done), channel_id=1, source_target_pairs={{0,12},{2,14},{4,8},{6,10},{8,4},{10,6},{12,0},{14,2},{16,28},{18,... | collective-permute-start | bytes 196616 | tf_op jit(solution)/shard_map/ppermute | solution.py:270
  15.2 4.3 %collective-permute-start.8 = (bf16[128,256]{1,0:T(8,128)(2,1)S(1)}, bf16[128,256]{1,0:T(8,128)(2,1)S(1)}, u32[]{:S(2)}, u32[]{:S(2)}) collective-permute-start(bf16[128,256]{1,0:T(8,128)(2,1)S(1)} %collective-permute-done), channel_id=1, source_target_pairs={{0,4},{2,6},{4,0},{6,2},{8,12},{10,14},{12,8},{14,10},{16,20},{18,... | collective-permute-start | bytes 196616 | tf_op jit(solution)/shard_map/ppermute | solution.py:270
  16.8 5.2 %collective-permute-start.9 = (bf16[384,256]{1,0:T(8,128)(2,1)S(1)}, bf16[384,256]{1,0:T(8,128)(2,1)S(1)}, u32[]{:S(2)}, u32[]{:S(2)}) collective-permute-start(bf16[384,256]{1,0:T(8,128)(2,1)S(1)} %pad_maximum_fusion.1), channel_id=1, source_target_pairs={{0,2},{2,0},{4,6},{6,4},{8,10},{10,8},{12,14},{14,12},{16,18},{18,... | collective-permute-start | bytes 589832 | tf_op jit(solution)/shard_map/ppermute | solution.py:270
  19.5 2.5 %collective-permute-start.10 = (bf16[384,256]{1,0:T(8,128)(2,1)S(1)}, bf16[384,256]{1,0:T(8,128)(2,1)S(1)}, u32[]{:S(2)}, u32[]{:S(2)}) collective-permute-start(bf16[384,256]{1,0:T(8,128)(2,1)S(1)} %pad_maximum_fusion.2), channel_id=1, source_target_pairs={{0,2},{2,0},{4,6},{6,4},{8,10},{10,8},{12,14},{14,12},{16,18},{18,... | collective-permute-start | bytes 589832 | tf_op jit(solution)/shard_map/ppermute | solution.py:270
  27.1 3.0 %collective-permute-start.11 = (bf16[512,256]{1,0:T(8,128)(2,1)S(1)}, bf16[512,256]{1,0:T(8,128)(2,1)S(1)}, u32[]{:S(2)}, u32[]{:S(2)}) collective-permute-start(bf16[512,256]{1,0:T(8,128)(2,1)S(1)} %get-tuple-element.38), channel_id=1, source_target_pairs={{0,2},{2,0},{4,6},{6,4},{8,10},{10,8},{12,14},{14,12},{16,18},{18,... | collective-permute-start | bytes 786440 | tf_op jit(solution)/shard_map/ppermute | solution.py:270
  27.6 15.6 %collective-permute-start.15 = (bf16[128,256]{1,0:T(8,128)(2,1)S(1)}, bf16[128,256]{1,0:T(8,128)(2,1)S(1)}, u32[]{:S(2)}, u32[]{:S(2)}) collective-permute-start(bf16[128,256]{1,0:T(8,128)(2,1)S(1)} %get-tuple-element.42), channel_id=1, source_target_pairs={{0,3},{2,0},{4,7},{6,4},{8,11},{10,8},{12,15},{14,12},{16,19},{18,... | collective-permute-start | bytes 196616 | tf_op jit(solution)/shard_map/ppermute | solution.py:267
  28.8 4.9 %collective-permute-start.16 = (bf16[384,256]{1,0:T(8,128)(2,1)S(1)}, bf16[384,256]{1,0:T(8,128)(2,1)S(1)}, u32[]{:S(2)}, u32[]{:S(2)}) collective-permute-start(bf16[384,256]{1,0:T(8,128)(2,1)S(1)} %get-tuple-element.44), channel_id=1, source_target_pairs={{0,2},{2,0},{4,6},{6,4},{8,10},{10,8},{12,14},{14,12},{16,18},{18,... | collective-permute-start | bytes 589832 | tf_op jit(solution)/shard_map/ppermute | solution.py:270
  30.1 5.6 %collective-permute-start.12 = (bf16[128,256]{1,0:T(8,128)(2,1)S(1)}, bf16[128,256]{1,0:T(8,128)(2,1)S(1)}, u32[]{:S(2)}, u32[]{:S(2)}) collective-permute-start(bf16[128,256]{1,0:T(8,128)(2,1)S(1)} %get-tuple-element.45), channel_id=1, source_target_pairs={{0,12},{2,14},{4,8},{6,10},{8,4},{10,6},{12,0},{14,2},{16,28},{18,... | collective-permute-start | bytes 196616 | tf_op jit(solution)/shard_map/ppermute | solution.py:270
  31.6 6.1 %collective-permute-start.14 = (bf16[128,256]{1,0:T(8,128)(2,1)S(1)}, bf16[128,256]{1,0:T(8,128)(2,1)S(1)}, u32[]{:S(2)}, u32[]{:S(2)}) collective-permute-start(bf16[128,256]{1,0:T(8,128)(2,1)S(1)} %get-tuple-element.46), channel_id=1, source_target_pairs={{0,4},{2,6},{4,0},{6,2},{8,12},{10,14},{12,8},{14,10},{16,20},{18,... | collective-permute-start | bytes 196616 | tf_op jit(solution)/shard_map/ppermute | solution.py:270
  32.7 5.9 %collective-permute-start.13 = (bf16[128,256]{1,0:T(8,128)(2,1)S(1)}, bf16[128,256]{1,0:T(8,128)(2,1)S(1)}, u32[]{:S(2)}, u32[]{:S(2)}) collective-permute-start(bf16[128,256]{1,0:T(8,128)(2,1)S(1)} %get-tuple-element.47), channel_id=1, source_target_pairs={{0,8},{2,10},{4,12},{6,14},{8,0},{10,2},{12,4},{14,6},{16,24},{18,... | collective-permute-start | bytes 196616 | tf_op jit(solution)/shard_map/ppermute | solution.py:270
  33.8 9.5 %collective-permute-start.17 = (bf16[128,256]{1,0:T(8,128)(2,1)S(1)}, bf16[128,256]{1,0:T(8,128)(2,1)S(1)}, u32[]{:S(2)}, u32[]{:S(2)}) collective-permute-start(bf16[128,256]{1,0:T(8,128)(2,1)S(1)} %get-tuple-element.48), channel_id=1, source_target_pairs={{0,13},{2,15},{4,9},{6,11},{8,4},{10,6},{12,0},{14,2},{16,29},{18,... | collective-permute-start | bytes 196616 | tf_op jit(solution)/shard_map/ppermute | solution.py:267
  35.7 7.5 %collective-permute-start.19 = (bf16[128,256]{1,0:T(8,128)(2,1)S(1)}, bf16[128,256]{1,0:T(8,128)(2,1)S(1)}, u32[]{:S(2)}, u32[]{:S(2)}) collective-permute-start(bf16[128,256]{1,0:T(8,128)(2,1)S(1)} %get-tuple-element.49), channel_id=1, source_target_pairs={{0,5},{2,7},{4,0},{6,2},{8,13},{10,15},{12,8},{14,10},{16,21},{18,... | collective-permute-start | bytes 196616 | tf_op jit(solution)/shard_map/ppermute | solution.py:267
  37.7 5.6 %collective-permute-start.18 = (bf16[128,256]{1,0:T(8,128)(2,1)S(1)}, bf16[128,256]{1,0:T(8,128)(2,1)S(1)}, u32[]{:S(2)}, u32[]{:S(2)}) collective-permute-start(bf16[128,256]{1,0:T(8,128)(2,1)S(1)} %get-tuple-element.50), channel_id=1, source_target_pairs={{0,9},{2,11},{4,13},{6,15},{8,0},{10,2},{12,4},{14,6},{16,25},{18,... | collective-permute-start | bytes 196616 | tf_op jit(solution)/shard_map/ppermute | solution.py:267
  38.6 5.2 %collective-permute-start.20 = (bf16[128,256]{1,0:T(8,128)(2,1)S(1)}, bf16[128,256]{1,0:T(8,128)(2,1)S(1)}, u32[]{:S(2)}, u32[]{:S(2)}) collective-permute-start(bf16[128,256]{1,0:T(8,128)(2,1)S(1)} %add_convert_fusion.4.unused_ref), channel_id=1, source_target_pairs={{0,17},{2,19},{4,21},{6,23},{8,25},{10,27},{12,29},{14,31},{16,0},... | collective-permute-start | bytes 196616 | tf_op jit(solution)/shard_map/ppermute | solution.py:257

commit v4 on v3

v4 whole, which is shorter than its diff:
```python
import functools
import math

import jax
import jax.numpy as jnp
from jax import lax
from jax.experimental import pallas as pl
from jax.experimental.pallas import tpu as pltpu
from jax.sharding import PartitionSpec as P

BLOCKED = -1e30
F32 = jnp.float32
LOW = jnp.bfloat16


def strides(span):
    return list(range(span // 2 - 2, 0, -2))


def window_ids(at, span):
    def nearest(t, u):
        return jnp.where(u < t, u, u - span)

    def same_core(t):
        others = [t ^ d for d in strides(span)]
        return [nearest(t, u) for u in others], [u - span // 2 for u in others]

    near, far = same_core(at)
    twin = at ^ 1
    twin_near, twin_far = same_core(twin)
    early = [at, at - span // 2] + near + [nearest(at, twin), twin - span // 2]
    return early, far + twin_near, twin_far


def pack_kernel(k_hbm, v_hbm, kv_ref, arrived):
    width = k_hbm.shape[1]
    copies = [
        pltpu.make_async_copy(one, kv_ref.at[:, pl.ds(i * width, width)], arrived.at[i])
        for i, one in enumerate((k_hbm, v_hbm))
    ]
    for copy in copies:
        copy.start()
    for copy in copies:
        copy.wait()


def group_passes(width, block_len, qt_ref, gt_ref, kv_ref, bias_ref, first, p_ref, dp_ref, sums_ref, top_ref, vt_ref, s_ref):
    pair = 2 * block_len
    slots = kv_ref.shape[0] // block_len
    vt_ref[:width, :] = kv_ref[:, width:].T
    vt_ref[width:, :] = jnp.ones((vt_ref.shape[0] - width, vt_ref.shape[1]), LOW)
    key_pos = lax.broadcasted_iota(jnp.int32, (block_len, pair), 0)
    row_pos = lax.broadcasted_iota(jnp.int32, (block_len, pair), 1) % block_len
    causal = key_pos <= row_pos
    scale2 = width**-0.5 * math.log2(math.e)

    def score(hp):
        lanes = slice(hp * pair, (hp + 1) * pair)
        s = jnp.dot(kv_ref[:, :width], qt_ref[:, lanes], preferred_element_type=F32)
        dp_ref[:, lanes] = jnp.dot(kv_ref[:, width:], gt_ref[:, lanes], preferred_element_type=F32)
        top = None
        for i in range(slots):
            slot = slice(i * block_len, (i + 1) * block_len)
            part = jnp.where(causal, s[slot], BLOCKED) if first + i == 0 else s[slot]
            s_ref[hp % 2, slot, :] = part
            best = jnp.max(part.reshape(-1, 8, pair), axis=0) + bias_ref[8 * (first + i) : 8 * (first + i) + 8, :]
            top = best if top is None else jnp.maximum(top, best)
        top_ref[:, lanes] = jnp.broadcast_to(jnp.max(top, axis=0, keepdims=True) * scale2, (8, pair))

    def weigh(hp):
        lanes = slice(hp * pair, (hp + 1) * pair)
        top = top_ref[0:1, lanes]
        for i in range(slots):
            slot = slice(i * block_len, (i + 1) * block_len)
            shift = bias_ref[8 * (first + i) : 8 * (first + i) + 1, :] - top
            p_ref[slot, lanes] = jnp.exp2(s_ref[hp % 2, slot, :] * scale2 + shift).astype(LOW)
        sums_ref[:, lanes] = jnp.dot(vt_ref[...], p_ref[:, lanes], preferred_element_type=F32)

    return score, weigh


def early_kernel(span, width, block_len, doc_hbm, at_ref, q_hbm, g_hbm, kv_ref, qt_ref, gt_ref, bias_ref, p_ref, dp_ref, sums_ref, top_ref, q_ref, g_ref, doc_ref, arrived, vt_ref, s_ref):
    places = enumerate(((q_hbm, q_ref), (g_hbm, g_ref), (doc_hbm, doc_ref)))
    copies = [pltpu.make_async_copy(there, here, arrived.at[i]) for i, (there, here) in places]
    for copy in copies:
        copy.start()
    pair = 2 * block_len
    score, weigh = group_passes(
        width, block_len, qt_ref, gt_ref, kv_ref, bias_ref, 0, p_ref, dp_ref, sums_ref, top_ref, vt_ref, s_ref
    )
    for copy in copies:
        copy.wait()
    at = at_ref[0]
    own_doc = doc_ref[at]
    for i, one in enumerate(sum(window_ids(at, span), [])):
        allowed = (one >= 0) & (doc_ref[jnp.maximum(one, 0)] == own_doc)
        bias_ref[8 * i : 8 * i + 8, :] = jnp.full((8, pair), jnp.where(allowed, 0.0, BLOCKED).astype(F32))
    pairs = q_ref.shape[1] // width // 2
    for hp in range(-1, pairs):
        if hp + 1 < pairs:
            for h in (2 * hp + 2, 2 * hp + 3):
                qt_ref[:, h * block_len : (h + 1) * block_len] = q_ref[:, h * width : (h + 1) * width].T
                gt_ref[:, h * block_len : (h + 1) * block_len] = g_ref[:, h * width : (h + 1) * width].T
            score(hp + 1)
        if hp >= 0:
            weigh(hp)


def middle_kernel(first, width, block_len, bias_ref, qt_ref, gt_ref, kv_ref, p_ref, dp_ref, sums_ref, top_ref, vt_ref, s_ref):
    score, weigh = group_passes(
        width, block_len, qt_ref, gt_ref, kv_ref, bias_ref, first, p_ref, dp_ref, sums_ref, top_ref, vt_ref, s_ref
    )
    pairs = qt_ref.shape[1] // block_len // 2
    for hp in range(-1, pairs):
        if hp + 1 < pairs:
            score(hp + 1)
        if hp >= 0:
            weigh(hp)


def main_kernel(span, width, block_len, *refs):
    bias_ref, qt_ref, gt_ref, kv_ref = refs[:4]
    early, middle = refs[4:8], refs[8:12]
    first_ref, twin_near_ref, twin_far_ref = refs[12:15]
    ds_refs, sq_refs, sg_refs, factor_refs = refs[15:18], refs[18:20], refs[20:22], refs[22:25]
    late, (vt_ref, s_ref, dk_ref, dv_ref) = refs[25:29], refs[29:]
    scale = width**-0.5
    pairs = qt_ref.shape[1] // block_len // 2
    pair = 2 * block_len
    steps = len(strides(span))
    groups = (early, middle, late)
    score, weigh = group_passes(
        width, block_len, qt_ref, gt_ref, kv_ref, bias_ref, span - steps, *late, vt_ref, s_ref
    )
    nt = (((1,), (1,)), ((), ()))
    twins = ((steps + 2, 2), (steps, steps), (0, steps))
    homes = [(first_ref, 0), (twin_far_ref, steps)]
    homes += [(twin_near_ref, i) for i in range(steps)] + [(twin_far_ref, i) for i in range(steps)]
    state = {}

    def rows_of(first, count):
        return slice(first * block_len, (first + count) * block_len)

    def settle(hp):
        lanes = slice(hp * pair, (hp + 1) * pair)
        tops = [top_ref[0:1, lanes] for _, _, _, top_ref in groups]
        top = functools.reduce(jnp.maximum, tops)
        shares = [jnp.exp2(one - top) for one in tops]
        sums = None
        for share, (_, _, sums_ref, _) in zip(shares, groups):
            part = sums_ref[:, lanes] * share
            sums = part if sums is None else sums + part
        inverse = 1.0 / sums[width : width + 1]
        wide_q, wide_g = qt_ref[:, lanes].astype(F32), gt_ref[:, lanes].astype(F32)
        delta = jnp.sum(sums[:width] * wide_g, axis=0, keepdims=True) * inverse
        scaled = []
        for i, share in enumerate(shares):
            factor = inverse * share
            factor_refs[i][:, lanes] = jnp.broadcast_to(factor * scale, (8, pair))
            scaled.append(((wide_q * (factor * scale)).astype(LOW), (wide_g * factor).astype(LOW)))
            if i < 2:
                sq_refs[i][:, lanes], sg_refs[i][:, lanes] = scaled[i]
        state[hp] = (delta, scaled)

    def spread(hp):
        lanes = slice(hp * pair, (hp + 1) * pair)
        delta, scaled = state[hp]
        place = 0
        for (p_ref, dp_ref, _, _), ds_ref, (sq, sg), (first, count) in zip(groups, ds_refs, scaled, twins):
            ds_ref[:, lanes] = (p_ref[:, lanes].astype(F32) * (dp_ref[:, lanes] - delta)).astype(LOW)
            rows, kept = rows_of(first, count), rows_of(place, count)
            dv = lax.dot_general(p_ref[rows, lanes], sg, nt, preferred_element_type=F32)
            dk = lax.dot_general(ds_ref[rows, lanes], sq, nt, preferred_element_type=F32)
            if hp > 0:
                dk = dk_ref[kept, :] + dk
                dv = dv_ref[kept, :] + dv
            if hp < pairs - 1:
                dk_ref[kept, :] = dk
                dv_ref[kept, :] = dv
            else:
                dk, dv = dk.astype(LOW), dv.astype(LOW)
                for i in range(count):
                    home, where = homes[place + i]
                    home[rows_of(where, 1), :width] = dk[rows_of(i, 1)]
                    home[rows_of(where, 1), width:] = dv[rows_of(i, 1)]
            place += count

    for hp in range(-2, pairs):
        if hp >= 0:
            settle(hp)
        if hp + 2 < pairs:
            score(hp + 2)
        if 0 <= hp + 1 < pairs:
            weigh(hp + 1)
        if hp >= 0:
            spread(hp)


def kept_kernel(width, *refs):
    nt = (((1,), (1,)), ((), ()))
    for p_ref, ds_ref, sq_ref, sg_ref, outs in (refs[:4] + (refs[8:11],), refs[4:8] + (refs[11:],)):
        count = sum(ref.shape[0] for ref in outs)
        dk = lax.dot_general(ds_ref[:count, :], sq_ref[...], nt, preferred_element_type=F32).astype(LOW)
        dv = lax.dot_general(p_ref[:count, :], sg_ref[...], nt, preferred_element_type=F32).astype(LOW)
        first = 0
        for ref in outs:
            ref[:, :width] = dk[first : first + ref.shape[0]]
            ref[:, width:] = dv[first : first + ref.shape[0]]
            first += ref.shape[0]


def query_kernel(width, block_len, unused_ref, *refs):
    ds_refs, factor_refs, kv_refs, dq_ref = refs[:3], refs[3:6], refs[6:9], refs[9]
    turned = [kv_ref[:, :width].T for kv_ref in kv_refs]
    pair = 2 * block_len
    for hp in range(dq_ref.shape[1] // width // 2):
        lanes = slice(hp * pair, (hp + 1) * pair)
        dq = None
        for keys, ds_ref, factor_ref in zip(turned, ds_refs, factor_refs):
            part = jnp.dot(keys, ds_ref[:, lanes], preferred_element_type=F32) * factor_ref[0:1, lanes]
            dq = part if dq is None else dq + part
        for h in range(2):
            head = slice((2 * hp + h) * width, (2 * hp + h + 1) * width)
            dq_ref[:, head] = dq[:, h * block_len : (h + 1) * block_len].T.astype(LOW)


HBM = pl.BlockSpec(memory_space=pltpu.HBM)
VMEM = pl.BlockSpec(memory_space=pltpu.VMEM)
SMEM = pl.BlockSpec(memory_space=pltpu.SMEM)


def in_hbm(x):
    return pltpu.with_memory_space_constraint(x, pltpu.HBM)


def call(body, name, ins, outs, scratch, flops, *operands):
    return pl.pallas_call(
        body,
        out_shape=tuple(jax.ShapeDtypeStruct(shape, kind) for shape, kind in outs),
        in_specs=ins,
        out_specs=(VMEM,) * len(outs),
        scratch_shapes=scratch,
        compiler_params=pltpu.CompilerParams(vmem_limit_bytes=24 * 1024 * 1024),
        cost_estimate=pl.CostEstimate(flops=flops, bytes_accessed=1 << 16, transcendentals=0),
        name=name,
    )(*operands)


def shards(inner_count, outer_count, queries, key_rows, value_rows, grad_output, doc_blocks):
    width = key_rows.shape[1]
    block_len = key_rows.shape[0]
    span = inner_count
    half = span // 2
    devices = inner_count * outer_count
    inner_at = lax.axis_index("inner")
    outer_at = lax.axis_index("outer")
    at = outer_at * inner_count + inner_at
    ways = strides(span)

    def place(t):
        return (t % inner_count) * outer_count + t // inner_count

    def moved(x, distance):
        route = [(place(t), place((t + distance) % devices)) for t in range(devices)]
        return lax.ppermute(x, ("inner", "outer"), route)

    def grouped(x, distance):
        return lax.ppermute(x, "outer", [(i, (i + distance) % outer_count) for i in range(outer_count)])

    def returned(x, d):
        route = []
        for t in range(devices):
            u = t ^ d
            route.append((place(t), place(u if u < t else (u - inner_count) % devices)))
        return lax.ppermute(x, ("inner", "outer"), route)

    def swapped(x, d):
        return lax.ppermute(x, "inner", [(i, i ^ d) for i in range(inner_count)])

    def above(d):
        return inner_at > (inner_at ^ d)

    def block(x, i):
        return x[i * block_len : (i + 1) * block_len]

    (own,) = call(
        pack_kernel,
        "pack",
        [HBM, HBM],
        [((block_len, 2 * width), LOW)],
        [pltpu.SemaphoreType.DMA((2,))],
        0,
        *(in_hbm(key_rows), in_hbm(value_rows)),
    )
    prior = grouped(own, 1)
    far = moved(own, half)
    nears = [swapped(jnp.where(above(d), prior, own), d) for d in ways]
    fars = [swapped(far, d) for d in ways[:-1]]
    nears, later_far = lax.optimization_barrier((jnp.concatenate(nears, axis=0), far))
    fars.append(swapped(later_far, ways[-1]))
    twin_first = swapped(jnp.concatenate([jnp.where(above(1), prior, own), far], axis=0), 1)
    early = jnp.concatenate([own, far, nears, twin_first], axis=0)

    steps = len(ways)
    heads = queries.shape[1] // width
    rows = heads * block_len
    pair = 2 * block_len
    work = 2 * rows * width * block_len
    turned = ((width, rows), LOW)

    def parts(n):
        return ((n * block_len, 2 * width), LOW)

    def sums_of(kv):
        keys = kv.shape[0]
        return [((keys, rows), LOW), ((keys, rows), F32), ((width + 16, rows), F32), ((8, rows), F32)]

    def scratch_of(kv):
        return [pltpu.VMEM((width + 16, kv.shape[0]), LOW), pltpu.VMEM((2, kv.shape[0], pair), F32)]

    qt, gt, bias, *early_sums = call(
        functools.partial(early_kernel, span, width, block_len),
        "early",
        [HBM, SMEM, HBM, HBM, VMEM],
        [turned, turned, ((8 * span, pair), F32)] + sums_of(early),
        [
            pltpu.VMEM(queries.shape, LOW),
            pltpu.VMEM(queries.shape, LOW),
            pltpu.SMEM(doc_blocks.shape, jnp.int32),
            pltpu.SemaphoreType.DMA((3,)),
            *scratch_of(early),
        ],
        40 * work * (steps + 4),
        *(in_hbm(doc_blocks), at.reshape(1), in_hbm(queries), in_hbm(grad_output), early),
    )
    *fars, early_sums[-1] = lax.optimization_barrier((*fars, early_sums[-1]))
    fars = jnp.concatenate(fars, axis=0)
    twin_nears, late = swapped(nears, 1), swapped(fars, 1)
    middle = jnp.concatenate([fars, twin_nears], axis=0)
    middle_sums = call(
        functools.partial(middle_kernel, steps + 4, width, block_len),
        "middle",
        [VMEM] * 4,
        sums_of(middle),
        scratch_of(middle),
        40 * work * (2 * steps),
        *(bias, qt, gt, middle),
    )
    groups = (early, middle, late)
    first_part, twin_near, twin_far, *rest = call(
        functools.partial(main_kernel, span, width, block_len),
        "main",
        [VMEM] * 12,
        [
            *(parts(1), parts(steps), parts(steps + 1)),
            *(((kv.shape[0], rows), LOW) for kv in groups),
            *([turned] * 4),
            *([((8, rows), F32)] * 3),
        ],
        [
            *(pltpu.VMEM(shape, kind) for shape, kind in sums_of(late)),
            *scratch_of(late),
            pltpu.VMEM((span // 2 * block_len, width), F32),
            pltpu.VMEM((span // 2 * block_len, width), F32),
        ],
        6 * work * span,
        *(bias, qt, gt, late, *early_sums, *middle_sums),
    )
    ds, scaled_q, scaled_g, factors = rest[:3], rest[3:5], rest[5:7], rest[7:]
    own_part, far_part, near_parts, far_parts = call(
        functools.partial(kept_kernel, width),
        "kept",
        [VMEM] * 8,
        [parts(1), parts(1), parts(steps), parts(steps)],
        [],
        work * span,
        *(early_sums[0], ds[0], scaled_q[0], scaled_g[0], middle_sums[0], ds[1], scaled_q[1], scaled_g[1]),
    )

    def added(x, y):
        return (x.astype(F32) + y.astype(F32)).astype(LOW)

    from_twin_far = swapped(twin_far, 1)
    from_twin_near = swapped(twin_near, 1)
    far_back = [swapped(added(block(far_parts, i), block(from_twin_far, i)), d) for i, d in enumerate(ways)]
    near_sums = [added(block(near_parts, i), block(from_twin_near, i)) for i in range(steps)]
    far_sum = far_part.astype(F32) + block(from_twin_far, steps).astype(F32)
    for one in far_back:
        far_sum = far_sum + one.astype(F32)
    far_sum = far_sum.astype(LOW)
    near_home = [returned(one, d) for one, d in zip(near_sums, ways)]
    far_sum, first_part = lax.optimization_barrier((far_sum, first_part))
    far_home = moved(far_sum, -half)
    first_home = returned(first_part, 1)
    (grad_queries,) = call(
        functools.partial(query_kernel, width, block_len),
        "query",
        [pl.BlockSpec(memory_space=pl.ANY)] + [VMEM] * 9,
        [(queries.shape, LOW)],
        [],
        work * span,
        *(far_sum, *ds, *factors, *groups),
    )
    mine = own_part.astype(F32)
    for one in near_home + [first_home, far_home]:
        mine = mine + one.astype(F32)
    grads = mine.astype(LOW)
    return grad_queries, grads[:, :width], grads[:, width:]


def solution(mesh):
    rows = P(("outer", "inner"), None)
    body = functools.partial(shards, mesh.shape["inner"], mesh.shape["outer"])
    return jax.shard_map(
        body, mesh=mesh, in_specs=(rows, rows, rows, rows, P()), out_specs=(rows, rows, rows), check_vma=False
    )
```

time: 44.8 us -> 43.3 us (0.967)
  waiting for transfers between devices: 3.99 us -> 1.9 us
  Pallas kernels: 11 us -> 11.8 us
    ppermute x14, waiting for transfers between devices: 3.16 us -> 0.2 us  [swapped(): return lax.ppermute(x, 'inner', [(i, i ^ d) for i in range(inner_count)])]
    ppermute x4, starting transfers between devices: 5.79 us -> 4.5 us  [returned(): return lax.ppermute(x, ('inner', 'outer'), route)]
    ppermute x2, waiting for transfers between devices: 0.82 us -> 1.69 us  [moved(): return lax.ppermute(x, ('inner', 'outer'), route)]
    pallas_call x5 -> x6, Pallas kernels: 11 us -> 11.8 us  [call(): pl.pallas_call(body, out_shape=tuple((jax.ShapeDtypeStruct(shape, kind) f...]
    ppermute x2, starting transfers between devices: 5.57 us -> 6.22 us  [moved(): return lax.ppermute(x, ('inner', 'outer'), route)]
    ppermute x14, starting transfers between devices: 13.5 us -> 14 us  [swapped(): return lax.ppermute(x, 'inner', [(i, i ^ d) for i in range(inner_count)])]
  transfers between devices with their start and end apart: 21 -> 21, of which waited for: 6 -> 3; matrix products, arithmetic and copies ran while one was open for 1% -> 1% of each run, Pallas kernels for 12% -> 17%
where the time goes in v4:
time: 43.3 us; the launch traced here: 43.1 us
  starting transfers between devices  27.7 us (64%)
  Pallas kernels  11.8 us (27%)
  waiting for transfers between devices  1.9 us (4%)
  between operations  0.82 us (2%)
  local copies, waits for them, and re-layouts  0.66 us (2%)
    ppermute x14, starting transfers between devices, swapped(): return lax.ppermute(x, 'inner', [(i, i ^ d) for i in range(inner_count)])  14 us
    pallas_call x6, Pallas kernels, call(): pl.pallas_call(body, out_shape=tuple((jax.ShapeDtypeStruct(shape, kind) f...  11.8 us
    ppermute x2, starting transfers between devices, moved(): return lax.ppermute(x, ('inner', 'outer'), route)  6.22 us
    ppermute x4, starting transfers between devices, returned(): return lax.ppermute(x, ('inner', 'outer'), route)  4.5 us
    ppermute x1, starting transfers between devices, grouped(): lax.ppermute(x, 'outer', [(i, (i + distance) % outer_count) for i in rang...  3 us
    ppermute x2, waiting for transfers between devices, moved(): return lax.ppermute(x, ('inner', 'outer'), route)  1.69 us
  transfers between devices with their start and end apart: 21, of which 3 were waited for; matrix products, arithmetic and copies ran while one was open for 1% of the time, Pallas kernels for 17%

profile of v4, /device:TPU:0, one launch (start us, length us, event | category | flops | bytes accessed | tf_op | source)
XLA Modules:
  0.0 43.1 jit_solution(1213972164019767770)
XLA Ops:
  0.6 0.8 %pack.1 = bf16[128,256]{1,0:T(8,128)(2,1)S(1)} custom-call(bf16[128,128]{1,0:T(8,128)(2,1)} %k_hbm.1, bf16[128,128]{1,0:T(8,128)(2,1)} %v_hbm.1), custom_call_target="tpu_custom_call" | custom-call | bytes 65536 | tf_op jit(solution)/shard_map/pack/pallas_call | solution.py:237
  1.4 3.0 %collective-permute-start.1 = (bf16[128,256]{1,0:T(8,128)(2,1)S(1)}, bf16[128,256]{1,0:T(8,128)(2,1)S(1)}, u32[]{:S(2)}, u32[]{:S(2)}) collective-permute-start(bf16[128,256]{1,0:T(8,128)(2,1)S(1)} %pack.1), channel_id=1, source_target_pairs={{0,1},{1,0},{2,3},{3,2},{4,5},{5,4},{6,7},{7,6},{8,9},{9,8},{10,11... | collective-permute-start | bytes 196616 | tf_op jit(solution)/shard_map/ppermute | solution.py:268
  4.4 2.6 %collective-permute-start = (bf16[128,256]{1,0:T(8,128)(2,1)S(1)}, bf16[128,256]{1,0:T(8,128)(2,1)S(1)}, u32[]{:S(2)}, u32[]{:S(2)}) collective-permute-start(bf16[128,256]{1,0:T(8,128)(2,1)S(1)} %pack.1), channel_id=1, source_target_pairs={{0,16},{2,18},{4,20},{6,22},{8,24},{10,26},{12,28},{14,30},{16,1},... | collective-permute-start | bytes 196616 | tf_op jit(solution)/shard_map/ppermute | solution.py:265
  7.1 2.8 %collective-permute-start.2 = (bf16[128,256]{1,0:T(8,128)(2,1)S(1)}, bf16[128,256]{1,0:T(8,128)(2,1)S(1)}, u32[]{:S(2)}, u32[]{:S(2)}) collective-permute-start(bf16[128,256]{1,0:T(8,128)(2,1)S(1)} %get-tuple-element.81), channel_id=1, source_target_pairs={{0,12},{2,14},{4,8},{6,10},{8,4},{10,6},{12,0},{14,2},{16,28},{18,... | collective-permute-start | bytes 196616 | tf_op jit(solution)/shard_map/ppermute | solution.py:278
  9.8 0.5 %collective-permute-start.4 = (bf16[128,256]{1,0:T(8,128)(2,1)S(1)}, bf16[128,256]{1,0:T(8,128)(2,1)S(1)}, u32[]{:S(2)}, u32[]{:S(2)}) collective-permute-start(bf16[128,256]{1,0:T(8,128)(2,1)S(1)} %get-tuple-element.83), channel_id=1, source_target_pairs={{0,4},{2,6},{4,0},{6,2},{8,12},{10,14},{12,8},{14,10},{16,20},{18,... | collective-permute-start | bytes 196616 | tf_op jit(solution)/shard_map/ppermute | solution.py:278
  10.3 0.3 collective-permute-start.3
  10.6 0.2 collective-permute-done
  10.8 0.1 collective-permute-start.5
  10.9 1.6 %collective-permute-start.7 = (bf16[128,256]{1,0:T(8,128)(2,1)S(1)}, bf16[128,256]{1,0:T(8,128)(2,1)S(1)}, u32[]{:S(2)}, u32[]{:S(2)}) collective-permute-start(bf16[128,256]{1,0:T(8,128)(2,1)S(1)} %collective-permute-done), channel_id=1, source_target_pairs={{0,8},{2,10},{4,12},{6,14},{8,0},{10,2},{12,4},{14,6},{16,24},{18,... | collective-permute-start | bytes 196616 | tf_op jit(solution)/shard_map/ppermute | solution.py:278
  12.5 0.0 collective-permute-done.2
  12.5 2.5 %collective-permute-start.6 = (bf16[128,256]{1,0:T(8,128)(2,1)S(1)}, bf16[128,256]{1,0:T(8,128)(2,1)S(1)}, u32[]{:S(2)}, u32[]{:S(2)}) collective-permute-start(bf16[128,256]{1,0:T(8,128)(2,1)S(1)} %collective-permute-done), channel_id=1, source_target_pairs={{0,12},{2,14},{4,8},{6,10},{8,4},{10,6},{12,0},{14,2},{16,28},{18,... | collective-permute-start | bytes 196616 | tf_op jit(solution)/shard_map/ppermute | solution.py:278
  15.0 0.2 collective-permute-done.3
  15.2 1.6 %collective-permute-start.8 = (bf16[128,256]{1,0:T(8,128)(2,1)S(1)}, bf16[128,256]{1,0:T(8,128)(2,1)S(1)}, u32[]{:S(2)}, u32[]{:S(2)}) collective-permute-start(bf16[128,256]{1,0:T(8,128)(2,1)S(1)} %collective-permute-done), channel_id=1, source_target_pairs={{0,4},{2,6},{4,0},{6,2},{8,12},{10,14},{12,8},{14,10},{16,20},{18,... | collective-permute-start | bytes 196616 | tf_op jit(solution)/shard_map/ppermute | solution.py:278
  16.8 2.9 %early.1 = (bf16[128,1024]{1,0:T(8,128)(2,1)S(1)}, bf16[128,1024]{1,0:T(8,128)(2,1)S(1)}, f32[128,256]{1,0:T(8,128)S(1)}, bf16[896,1024]{1,0:T(8,128)(2,1)S(1)},...) custom-call(s32[32]{0:T(128)} %doc_hbm.1, s32[1]{0:T(128)} %bitcast.at_ref, ...), custom_call_target="tpu_custom_call" | custom-call | flops 9395240960 | bytes 65536 | tf_op jit(solution)/shard_map/early/pallas_call | solution.py:237
  19.8 0.6 %collective-permute-start.9 = (bf16[384,256]{1,0:T(8,128)(2,1)S(1)}, bf16[384,256]{1,0:T(8,128)(2,1)S(1)}, u32[]{:S(2)}, u32[]{:S(2)}) collective-permute-start(bf16[384,256]{1,0:T(8,128)(2,1)S(1)} %pad_maximum_fusion.2), channel_id=1, source_target_pairs={{0,2},{2,0},{4,6},{6,4},{8,10},{10,8},{12,14},{14,12},{16,18},{18,... | collective-permute-start | bytes 589832 | tf_op jit(solution)/shard_map/ppermute | solution.py:278
  20.4 1.5 %middle.1 = (bf16[768,1024]{1,0:T(8,128)(2,1)S(1)}, f32[768,1024]{1,0:T(8,128)S(1)}, f32[144,1024]{1,0:T(8,128)S(1)}, f32[8,1024]{1,0:T(8,128)S(1)}) custom-call(f32[128,256]{1,0:T(8,128)S(1)} %get-tuple-element.41.bias_ref.refs_0_, bf16[128,1024]{1,0:T(8,128)(2,1)S(1)} %get-tuple-element.42.qt_ref.refs_1_, ...), custom_call_target="tpu_custom_call" | custom-call | flops 8053063680 | bytes 65536 | tf_op jit(solution)/shard_map/middle/pallas_call | solution.py:237
  21.9 3.7 %main.1 = (bf16[128,256]{1,0:T(8,128)(2,1)S(1)}, bf16[384,256]{1,0:T(8,128)(2,1)S(1)}, bf16[512,256]{1,0:T(8,128)(2,1)S(1)}, bf16[896,1024]{1,0:T(8,128)(2,1)S(1...) custom-call(f32[128,256]{1,0:T(8,128)S(1)} %get-tuple-element.41.bia, ...), custom_call_target="tpu_custom_call" | custom-call | flops 3221225472 | bytes 65536 | tf_op jit(solution)/shard_map/main/pallas_call | solution.py:237
  25.6 0.1 collective-permute-start.11
  25.7 0.5 %collective-permute-start.15 = (bf16[384,256]{1,0:T(8,128)(2,1)S(1)}, bf16[384,256]{1,0:T(8,128)(2,1)S(1)}, u32[]{:S(2)}, u32[]{:S(2)}) collective-permute-start(bf16[384,256]{1,0:T(8,128)(2,1)S(1)} %get-tuple-element.73), channel_id=1, source_target_pairs={{0,2},{2,0},{4,6},{6,4},{8,10},{10,8},{12,14},{14,12},{16,18},{18,... | collective-permute-start | bytes 589832 | tf_op jit(solution)/shard_map/ppermute | solution.py:278
  26.2 1.2 %kept.1 = (bf16[128,256]{1,0:T(8,128)(2,1)S(1)}, bf16[128,256]{1,0:T(8,128)(2,1)S(1)}, bf16[384,256]{1,0:T(8,128)(2,1)S(1)}, bf16[384,256]{1,0:T(8,128)(2,1)S(1)}) custom-call(bf16[896,1024]{1,0:T(8,128)(2,1)S(1)} %get-tuple-element.40.refs_4_.refs_0_, bf16[896,1024]{1,0:T(8,128)(2,1)S(1)} %get-tuple-element.56.refs_1_.refs_0_, ...), custom_call_target="tpu_custom_call" | custom-call | flops 536870912 | bytes 65536 | tf_op jit(solution)/shard_map/kept/pallas_call | solution.py:237
  27.6 0.8 %collective-permute-start.12 = (bf16[128,256]{1,0:T(8,128)(2,1)S(1)}, bf16[128,256]{1,0:T(8,128)(2,1)S(1)}, u32[]{:S(2)}, u32[]{:S(2)}) collective-permute-start(bf16[128,256]{1,0:T(8,128)(2,1)S(1)} %get-tuple-element.75), channel_id=1, source_target_pairs={{0,12},{2,14},{4,8},{6,10},{8,4},{10,6},{12,0},{14,2},{16,28},{18,... | collective-permute-start | bytes 196616 | tf_op jit(solution)/shard_map/ppermute | solution.py:278
  28.3 1.2 %collective-permute-start.14 = (bf16[128,256]{1,0:T(8,128)(2,1)S(1)}, bf16[128,256]{1,0:T(8,128)(2,1)S(1)}, u32[]{:S(2)}, u32[]{:S(2)}) collective-permute-start(bf16[128,256]{1,0:T(8,128)(2,1)S(1)} %get-tuple-element.76), channel_id=1, source_target_pairs={{0,4},{2,6},{4,0},{6,2},{8,12},{10,14},{12,8},{14,10},{16,20},{18,... | collective-permute-start | bytes 196616 | tf_op jit(solution)/shard_map/ppermute | solution.py:278
  29.5 1.6 %collective-permute-start.13 = (bf16[128,256]{1,0:T(8,128)(2,1)S(1)}, bf16[128,256]{1,0:T(8,128)(2,1)S(1)}, u32[]{:S(2)}, u32[]{:S(2)}) collective-permute-start(bf16[128,256]{1,0:T(8,128)(2,1)S(1)} %get-tuple-element.77), channel_id=1, source_target_pairs={{0,8},{2,10},{4,12},{6,14},{8,0},{10,2},{12,4},{14,6},{16,24},{18,... | collective-permute-start | bytes 196616 | tf_op jit(solution)/shard_map/ppermute | solution.py:278
  31.2 1.8 %collective-permute-start.16 = (bf16[128,256]{1,0:T(8,128)(2,1)S(1)}, bf16[128,256]{1,0:T(8,128)(2,1)S(1)}, u32[]{:S(2)}, u32[]{:S(2)}) collective-permute-start(bf16[128,256]{1,0:T(8,128)(2,1)S(1)} %get-tuple-element.78), channel_id=1, source_target_pairs={{0,13},{2,15},{4,9},{6,11},{8,4},{10,6},{12,0},{14,2},{16,29},{18,... | collective-permute-start | bytes 196616 | tf_op jit(solution)/shard_map/ppermute | solution.py:275
  32.9 1.1 %collective-permute-start.18 = (bf16[128,256]{1,0:T(8,128)(2,1)S(1)}, bf16[128,256]{1,0:T(8,128)(2,1)S(1)}, u32[]{:S(2)}, u32[]{:S(2)}) collective-permute-start(bf16[128,256]{1,0:T(8,128)(2,1)S(1)} %get-tuple-element.79), channel_id=1, source_target_pairs={{0,5},{2,7},{4,0},{6,2},{8,13},{10,15},{12,8},{14,10},{16,21},{18,... | collective-permute-start | bytes 196616 | tf_op jit(solution)/shard_map/ppermute | solution.py:275
  34.0 1.6 %collective-permute-start.17 = (bf16[128,256]{1,0:T(8,128)(2,1)S(1)}, bf16[128,256]{1,0:T(8,128)(2,1)S(1)}, u32[]{:S(2)}, u32[]{:S(2)}) collective-permute-start(bf16[128,256]{1,0:T(8,128)(2,1)S(1)} %get-tuple-element.80), channel_id=1, source_target_pairs={{0,9},{2,11},{4,13},{6,15},{8,0},{10,2},{12,4},{14,6},{16,25},{18,... | collective-permute-start | bytes 196616 | tf_op jit(solution)/shard_map/ppermute | solution.py:275
  35.7 0.1 collective-permute-start.19
  35.7 3.6 %collective-permute-start.20 = (bf16[128,256]{1,0:T(8,128)(2,1)S(1)}, bf16[128,256]{1,0:T(8,128)(2,1)S(1)}, u32[]{:S(2)}, u32[]{:S(2)}) collective-permute-start(bf16[128,256]{1,0:T(8,128)(2,1)S(1)} %add_convert_fusion.4.unused_ref), channel_id=1, source_target_pairs={{0,17},{2,19},{4,21},{6,23},{8,25},{10,27},{12,29},{14,31},{16,0},... | collective-permute-start | bytes 196616 | tf_op jit(solution)/shard_map/ppermute | solution.py:265
  39.4 1.6 %query.1 = bf16[128,1024]{1,0:T(8,128)(2,1)} custom-call(bf16[128,256]{1,0:T(8,128)(2,1)S(1)} %add_convert_fusion.4.unused_ref, bf16[896,1024]{1,0:T(8,128)(2,1)S(1)} %get-tuple-element.56.refs_1_.refs_0_, bf16[768,1024]{1,0:T(8,128)(2,1)S(1)} %get-tuple-element.59.refs_5_.refs_1_, bf16[384,1024]{1,0:T(8,128)(2,1)S(1)} %get-tuple-element.67.refs_2_, ...), custom_call_target="tpu_custom_call" | custom-call | flops 536870912 | bytes 65536 | tf_op jit(solution)/shard_map/query/pallas_call | solution.py:237
  41.0 1.5 %collective-permute-done.20 = bf16[128,256]{1,0:T(8,128)(2,1)S(1)} collective-permute-done((bf16[128,256]{1,0:T(8,128)(2,1)S(1)}, bf16[128,256]{1,0:T(8,128)(2,1)S(1)}, u32[]{:S(2)}, u32[]{:S(2)}) %collective-permute-start.20) | collective-permute-done | bytes 65568 | tf_op jit(solution)/shard_map/ppermute | solution.py:265
  42.4 0.1 add_convert_fusion
  42.5 0.6 %fusion = (bf16[128,128]{1,0:T(8,128)(2,1)}, bf16[128,128]{1,0:T(8,128)(2,1)}) fusion(bf16[128,256]{1,0:T(8,128)(2,1)S(1)} %add_convert_fusion), kind=kLoop, calls=%fused_computation.20 | loop fusion | bytes 131072 | tf_op jit(solution)/shard_map/slice | solution.py:408
  (30 shorter events, 0.3 us)
Async XLA Ops:
  1.4 5.6 %collective-permute-start.1 = (bf16[128,256]{1,0:T(8,128)(2,1)S(1)}, bf16[128,256]{1,0:T(8,128)(2,1)S(1)}, u32[]{:S(2)}, u32[]{:S(2)}) collective-permute-start(bf16[128,256]{1,0:T(8,128)(2,1)S(1)} %pack.1), channel_id=1, source_target_pairs={{0,1},{1,0},{2,3},{3,2},{4,5},{5,4},{6,7},{7,6},{8,9},{9,8},{10,11... | collective-permute-start | bytes 196616 | tf_op jit(solution)/shard_map/ppermute | solution.py:268
  4.4 6.4 %collective-permute-start = (bf16[128,256]{1,0:T(8,128)(2,1)S(1)}, bf16[128,256]{1,0:T(8,128)(2,1)S(1)}, u32[]{:S(2)}, u32[]{:S(2)}) collective-permute-start(bf16[128,256]{1,0:T(8,128)(2,1)S(1)} %pack.1), channel_id=1, source_target_pairs={{0,16},{2,18},{4,20},{6,22},{8,24},{10,26},{12,28},{14,30},{16,1},... | collective-permute-start | bytes 196616 | tf_op jit(solution)/shard_map/ppermute | solution.py:265
  7.1 5.5 %collective-permute-start.2 = (bf16[128,256]{1,0:T(8,128)(2,1)S(1)}, bf16[128,256]{1,0:T(8,128)(2,1)S(1)}, u32[]{:S(2)}, u32[]{:S(2)}) collective-permute-start(bf16[128,256]{1,0:T(8,128)(2,1)S(1)} %get-tuple-element.81), channel_id=1, source_target_pairs={{0,12},{2,14},{4,8},{6,10},{8,4},{10,6},{12,0},{14,2},{16,28},{18,... | collective-permute-start | bytes 196616 | tf_op jit(solution)/shard_map/ppermute | solution.py:278
  9.8 5.2 %collective-permute-start.4 = (bf16[128,256]{1,0:T(8,128)(2,1)S(1)}, bf16[128,256]{1,0:T(8,128)(2,1)S(1)}, u32[]{:S(2)}, u32[]{:S(2)}) collective-permute-start(bf16[128,256]{1,0:T(8,128)(2,1)S(1)} %get-tuple-element.83), channel_id=1, source_target_pairs={{0,4},{2,6},{4,0},{6,2},{8,12},{10,14},{12,8},{14,10},{16,20},{18,... | collective-permute-start | bytes 196616 | tf_op jit(solution)/shard_map/ppermute | solution.py:278
  10.3 4.8 %collective-permute-start.3 = (bf16[128,256]{1,0:T(8,128)(2,1)S(1)}, bf16[128,256]{1,0:T(8,128)(2,1)S(1)}, u32[]{:S(2)}, u32[]{:S(2)}) collective-permute-start(bf16[128,256]{1,0:T(8,128)(2,1)S(1)} %get-tuple-element.84), channel_id=1, source_target_pairs={{0,8},{2,10},{4,12},{6,14},{8,0},{10,2},{12,4},{14,6},{16,24},{18,... | collective-permute-start | bytes 196616 | tf_op jit(solution)/shard_map/ppermute | solution.py:278
  10.8 5.9 %collective-permute-start.5 = (bf16[256,256]{1,0:T(8,128)(2,1)S(1)}, bf16[256,256]{1,0:T(8,128)(2,1)S(1)}, u32[]{:S(2)}, u32[]{:S(2)}) collective-permute-start(bf16[256,256]{1,0:T(8,128)(2,1)S(1)} %pad_maximum_fusion.3), channel_id=1, source_target_pairs={{0,2},{2,0},{4,6},{6,4},{8,10},{10,8},{12,14},{14,12},{16,18},{18,... | collective-permute-start | bytes 393224 | tf_op jit(solution)/shard_map/ppermute | solution.py:278
  10.9 8.8 %collective-permute-start.7 = (bf16[128,256]{1,0:T(8,128)(2,1)S(1)}, bf16[128,256]{1,0:T(8,128)(2,1)S(1)}, u32[]{:S(2)}, u32[]{:S(2)}) collective-permute-start(bf16[128,256]{1,0:T(8,128)(2,1)S(1)} %collective-permute-done), channel_id=1, source_target_pairs={{0,8},{2,10},{4,12},{6,14},{8,0},{10,2},{12,4},{14,6},{16,24},{18,... | collective-permute-start | bytes 196616 | tf_op jit(solution)/shard_map/ppermute | solution.py:278
  12.5 7.2 %collective-permute-start.6 = (bf16[128,256]{1,0:T(8,128)(2,1)S(1)}, bf16[128,256]{1,0:T(8,128)(2,1)S(1)}, u32[]{:S(2)}, u32[]{:S(2)}) collective-permute-start(bf16[128,256]{1,0:T(8,128)(2,1)S(1)} %collective-permute-done), channel_id=1, source_target_pairs={{0,12},{2,14},{4,8},{6,10},{8,4},{10,6},{12,0},{14,2},{16,28},{18,... | collective-permute-start | bytes 196616 | tf_op jit(solution)/shard_map/ppermute | solution.py:278
  15.2 4.5 %collective-permute-start.8 = (bf16[128,256]{1,0:T(8,128)(2,1)S(1)}, bf16[128,256]{1,0:T(8,128)(2,1)S(1)}, u32[]{:S(2)}, u32[]{:S(2)}) collective-permute-start(bf16[128,256]{1,0:T(8,128)(2,1)S(1)} %collective-permute-done), channel_id=1, source_target_pairs={{0,4},{2,6},{4,0},{6,2},{8,12},{10,14},{12,8},{14,10},{16,20},{18,... | collective-permute-start | bytes 196616 | tf_op jit(solution)/shard_map/ppermute | solution.py:278
  16.8 3.6 %collective-permute-start.10 = (bf16[384,256]{1,0:T(8,128)(2,1)S(1)}, bf16[384,256]{1,0:T(8,128)(2,1)S(1)}, u32[]{:S(2)}, u32[]{:S(2)}) collective-permute-start(bf16[384,256]{1,0:T(8,128)(2,1)S(1)} %pad_maximum_fusion.1), channel_id=1, source_target_pairs={{0,2},{2,0},{4,6},{6,4},{8,10},{10,8},{12,14},{14,12},{16,18},{18,... | collective-permute-start | bytes 589832 | tf_op jit(solution)/shard_map/ppermute | solution.py:278
  19.8 2.1 %collective-permute-start.9 = (bf16[384,256]{1,0:T(8,128)(2,1)S(1)}, bf16[384,256]{1,0:T(8,128)(2,1)S(1)}, u32[]{:S(2)}, u32[]{:S(2)}) collective-permute-start(bf16[384,256]{1,0:T(8,128)(2,1)S(1)} %pad_maximum_fusion.2), channel_id=1, source_target_pairs={{0,2},{2,0},{4,6},{6,4},{8,10},{10,8},{12,14},{14,12},{16,18},{18,... | collective-permute-start | bytes 589832 | tf_op jit(solution)/shard_map/ppermute | solution.py:278
  25.6 1.8 %collective-permute-start.11 = (bf16[512,256]{1,0:T(8,128)(2,1)S(1)}, bf16[512,256]{1,0:T(8,128)(2,1)S(1)}, u32[]{:S(2)}, u32[]{:S(2)}) collective-permute-start(bf16[512,256]{1,0:T(8,128)(2,1)S(1)} %get-tuple-element.63), channel_id=1, source_target_pairs={{0,2},{2,0},{4,6},{6,4},{8,10},{10,8},{12,14},{14,12},{16,18},{18,... | collective-permute-start | bytes 786440 | tf_op jit(solution)/shard_map/ppermute | solution.py:278
  25.7 5.4 %collective-permute-start.15 = (bf16[384,256]{1,0:T(8,128)(2,1)S(1)}, bf16[384,256]{1,0:T(8,128)(2,1)S(1)}, u32[]{:S(2)}, u32[]{:S(2)}) collective-permute-start(bf16[384,256]{1,0:T(8,128)(2,1)S(1)} %get-tuple-element.73), channel_id=1, source_target_pairs={{0,2},{2,0},{4,6},{6,4},{8,10},{10,8},{12,14},{14,12},{16,18},{18,... | collective-permute-start | bytes 589832 | tf_op jit(solution)/shard_map/ppermute | solution.py:278
  27.6 6.4 %collective-permute-start.12 = (bf16[128,256]{1,0:T(8,128)(2,1)S(1)}, bf16[128,256]{1,0:T(8,128)(2,1)S(1)}, u32[]{:S(2)}, u32[]{:S(2)}) collective-permute-start(bf16[128,256]{1,0:T(8,128)(2,1)S(1)} %get-tuple-element.75), channel_id=1, source_target_pairs={{0,12},{2,14},{4,8},{6,10},{8,4},{10,6},{12,0},{14,2},{16,28},{18,... | collective-permute-start | bytes 196616 | tf_op jit(solution)/shard_map/ppermute | solution.py:278
  28.3 7.3 %collective-permute-start.14 = (bf16[128,256]{1,0:T(8,128)(2,1)S(1)}, bf16[128,256]{1,0:T(8,128)(2,1)S(1)}, u32[]{:S(2)}, u32[]{:S(2)}) collective-permute-start(bf16[128,256]{1,0:T(8,128)(2,1)S(1)} %get-tuple-element.76), channel_id=1, source_target_pairs={{0,4},{2,6},{4,0},{6,2},{8,12},{10,14},{12,8},{14,10},{16,20},{18,... | collective-permute-start | bytes 196616 | tf_op jit(solution)/shard_map/ppermute | solution.py:278
  29.5 6.1 %collective-permute-start.13 = (bf16[128,256]{1,0:T(8,128)(2,1)S(1)}, bf16[128,256]{1,0:T(8,128)(2,1)S(1)}, u32[]{:S(2)}, u32[]{:S(2)}) collective-permute-start(bf16[128,256]{1,0:T(8,128)(2,1)S(1)} %get-tuple-element.77), channel_id=1, source_target_pairs={{0,8},{2,10},{4,12},{6,14},{8,0},{10,2},{12,4},{14,6},{16,24},{18,... | collective-permute-start | bytes 196616 | tf_op jit(solution)/shard_map/ppermute | solution.py:278
  31.2 9.8 %collective-permute-start.16 = (bf16[128,256]{1,0:T(8,128)(2,1)S(1)}, bf16[128,256]{1,0:T(8,128)(2,1)S(1)}, u32[]{:S(2)}, u32[]{:S(2)}) collective-permute-start(bf16[128,256]{1,0:T(8,128)(2,1)S(1)} %get-tuple-element.78), channel_id=1, source_target_pairs={{0,13},{2,15},{4,9},{6,11},{8,4},{10,6},{12,0},{14,2},{16,29},{18,... | collective-permute-start | bytes 196616 | tf_op jit(solution)/shard_map/ppermute | solution.py:275
  32.9 8.0 %collective-permute-start.18 = (bf16[128,256]{1,0:T(8,128)(2,1)S(1)}, bf16[128,256]{1,0:T(8,128)(2,1)S(1)}, u32[]{:S(2)}, u32[]{:S(2)}) collective-permute-start(bf16[128,256]{1,0:T(8,128)(2,1)S(1)} %get-tuple-element.79), channel_id=1, source_target_pairs={{0,5},{2,7},{4,0},{6,2},{8,13},{10,15},{12,8},{14,10},{16,21},{18,... | collective-permute-start | bytes 196616 | tf_op jit(solution)/shard_map/ppermute | solution.py:275
  34.0 7.0 %collective-permute-start.17 = (bf16[128,256]{1,0:T(8,128)(2,1)S(1)}, bf16[128,256]{1,0:T(8,128)(2,1)S(1)}, u32[]{:S(2)}, u32[]{:S(2)}) collective-permute-start(bf16[128,256]{1,0:T(8,128)(2,1)S(1)} %get-tuple-element.80), channel_id=1, source_target_pairs={{0,9},{2,11},{4,13},{6,15},{8,0},{10,2},{12,4},{14,6},{16,25},{18,... | collective-permute-start | bytes 196616 | tf_op jit(solution)/shard_map/ppermute | solution.py:275
  35.7 5.3 %collective-permute-start.19 = (bf16[128,256]{1,0:T(8,128)(2,1)S(1)}, bf16[128,256]{1,0:T(8,128)(2,1)S(1)}, u32[]{:S(2)}, u32[]{:S(2)}) collective-permute-start(bf16[128,256]{1,0:T(8,128)(2,1)S(1)} %get-tuple-element.74), channel_id=1, source_target_pairs={{0,3},{2,0},{4,7},{6,4},{8,11},{10,8},{12,15},{14,12},{16,19},{18,... | collective-permute-start | bytes 196616 | tf_op jit(solution)/shard_map/ppermute | solution.py:275
  35.7 6.7 %collective-permute-start.20 = (bf16[128,256]{1,0:T(8,128)(2,1)S(1)}, bf16[128,256]{1,0:T(8,128)(2,1)S(1)}, u32[]{:S(2)}, u32[]{:S(2)}) collective-permute-start(bf16[128,256]{1,0:T(8,128)(2,1)S(1)} %add_convert_fusion.4.unused_ref), channel_id=1, source_target_pairs={{0,17},{2,19},{4,21},{6,23},{8,25},{10,27},{12,29},{14,31},{16,0},... | collective-permute-start | bytes 196616 | tf_op jit(solution)/shard_map/ppermute | solution.py:265

commit v5 on v4

--- a/solution.py
+++ b/solution.py
@@ -14,7 +14,12 @@
 
 
 def strides(span):
-    return list(range(span // 2 - 2, 0, -2))
+    return list(range(2, span // 2, 2))
+
+
+def far_strides(span):
+    ways = strides(span)
+    return ways[-1:] + ways[:-1]
 
 
 def window_ids(at, span):
@@ -22,14 +27,13 @@
         return jnp.where(u < t, u, u - span)
 
     def same_core(t):
-        others = [t ^ d for d in strides(span)]
-        return [nearest(t, u) for u in others], [u - span // 2 for u in others]
+        near = [nearest(t, t ^ d) for d in strides(span)]
+        return near, [(t ^ d) - span // 2 for d in far_strides(span)]
 
     near, far = same_core(at)
     twin = at ^ 1
     twin_near, twin_far = same_core(twin)
-    early = [at, at - span // 2] + near + [nearest(at, twin), twin - span // 2]
-    return early, far + twin_near, twin_far
+    return [at, at - span // 2] + near, far + [nearest(at, twin), twin - span // 2] + twin_near, twin_far
 
 
 def pack_kernel(k_hbm, v_hbm, kv_ref, arrived):
@@ -133,7 +137,7 @@
         width, block_len, qt_ref, gt_ref, kv_ref, bias_ref, span - steps, *late, vt_ref, s_ref
     )
     nt = (((1,), (1,)), ((), ()))
-    twins = ((steps + 2, 2), (steps, steps), (0, steps))
+    twins = ((0, 0), (steps, steps + 2), (0, steps))
     homes = [(first_ref, 0), (twin_far_ref, steps)]
     homes += [(twin_near_ref, i) for i in range(steps)] + [(twin_far_ref, i) for i in range(steps)]
     state = {}
@@ -168,6 +172,8 @@
         place = 0
         for (p_ref, dp_ref, _, _), ds_ref, (sq, sg), (first, count) in zip(groups, ds_refs, scaled, twins):
             ds_ref[:, lanes] = (p_ref[:, lanes].astype(F32) * (dp_ref[:, lanes] - delta)).astype(LOW)
+            if not count:
+                continue
             rows, kept = rows_of(first, count), rows_of(place, count)
             dv = lax.dot_general(p_ref[rows, lanes], sg, nt, preferred_element_type=F32)
             dk = lax.dot_general(ds_ref[rows, lanes], sq, nt, preferred_element_type=F32)
@@ -255,7 +261,7 @@
     inner_at = lax.axis_index("inner")
     outer_at = lax.axis_index("outer")
     at = outer_at * inner_count + inner_at
-    ways = strides(span)
+    ways, far_ways = strides(span), far_strides(span)
 
     def place(t):
         return (t % inner_count) * outer_count + t // inner_count
@@ -295,11 +301,12 @@
     prior = grouped(own, 1)
     far = moved(own, half)
     nears = [swapped(jnp.where(above(d), prior, own), d) for d in ways]
-    fars = [swapped(far, d) for d in ways[:-1]]
-    nears, later_far = lax.optimization_barrier((jnp.concatenate(nears, axis=0), far))
-    fars.append(swapped(later_far, ways[-1]))
-    twin_first = swapped(jnp.concatenate([jnp.where(above(1), prior, own), far], axis=0), 1)
-    early = jnp.concatenate([own, far, nears, twin_first], axis=0)
+    fars = [swapped(far, d) for d in far_ways[:-1]]
+    nears[1], later_far = lax.optimization_barrier((nears[1], far))
+    nears = jnp.concatenate(nears, axis=0)
+    fars.append(swapped(later_far, far_ways[-1]))
+    early = jnp.concatenate([own, far, nears], axis=0)
+    for_twin = jnp.concatenate([jnp.where(above(1), prior, own), far, nears], axis=0)
 
     steps = len(ways)
     heads = queries.shape[1] // width
@@ -330,20 +337,20 @@
             pltpu.SemaphoreType.DMA((3,)),
             *scratch_of(early),
         ],
-        40 * work * (steps + 4),
+        40 * work * (steps + 2),
         *(in_hbm(doc_blocks), at.reshape(1), in_hbm(queries), in_hbm(grad_output), early),
     )
     *fars, early_sums[-1] = lax.optimization_barrier((*fars, early_sums[-1]))
     fars = jnp.concatenate(fars, axis=0)
-    twin_nears, late = swapped(nears, 1), swapped(fars, 1)
-    middle = jnp.concatenate([fars, twin_nears], axis=0)
+    from_twin, late = swapped(for_twin, 1), swapped(fars, 1)
+    middle = jnp.concatenate([fars, from_twin], axis=0)
     middle_sums = call(
-        functools.partial(middle_kernel, steps + 4, width, block_len),
+        functools.partial(middle_kernel, steps + 2, width, block_len),
         "middle",
         [VMEM] * 4,
         sums_of(middle),
         scratch_of(middle),
-        40 * work * (2 * steps),
+        40 * work * (2 * steps + 2),
         *(bias, qt, gt, middle),
     )
     groups = (early, middle, late)
@@ -382,13 +389,14 @@
 
     from_twin_far = swapped(twin_far, 1)
     from_twin_near = swapped(twin_near, 1)
-    far_back = [swapped(added(block(far_parts, i), block(from_twin_far, i)), d) for i, d in enumerate(ways)]
+    far_sums = [added(block(far_parts, i), block(from_twin_far, i)) for i in range(steps)]
+    far_back = [swapped(far_sums[far_ways.index(d)], d) for d in reversed(ways)]
     near_sums = [added(block(near_parts, i), block(from_twin_near, i)) for i in range(steps)]
     far_sum = far_part.astype(F32) + block(from_twin_far, steps).astype(F32)
     for one in far_back:
         far_sum = far_sum + one.astype(F32)
     far_sum = far_sum.astype(LOW)
-    near_home = [returned(one, d) for one, d in zip(near_sums, ways)]
+    near_home = [returned(near_sums[ways.index(d)], d) for d in reversed(ways)]
     far_sum, first_part = lax.optimization_barrier((far_sum, first_part))
     far_home = moved(far_sum, -half)
     first_home = returned(first_part, 1)

time: 43.3 us -> 41.5 us (0.958)
  starting transfers between devices: 27.7 us -> 25.8 us
    ppermute x14 -> x13, starting transfers between devices: 14 us -> 11.9 us  [swapped(): return lax.ppermute(x, 'inner', [(i, i ^ d) for i in range(inner_count)])]
    ppermute x2, waiting for transfers between devices: 1.69 us -> 0.83 us  [moved(): return lax.ppermute(x, ('inner', 'outer'), route)]
    ppermute x14 -> x13, waiting for transfers between devices: 0.2 us -> 1.02 us  [swapped(): return lax.ppermute(x, 'inner', [(i, i ^ d) for i in range(inner_count)])]
  transfers between devices with their start and end apart: 21 -> 20, of which waited for: 3 -> 4; matrix products, arithmetic and copies ran while one was open for 1% -> 1% of each run, Pallas kernels for 17% -> 18%
where the time goes in v5:
time: 41.5 us; the launch traced here: 41.3 us
  starting transfers between devices  25.8 us (62%)
  Pallas kernels  11.8 us (28%)
  waiting for transfers between devices  1.86 us (4%)
  between operations  0.84 us (2%)
  local copies, waits for them, and re-layouts  0.72 us (2%)
    ppermute x13, starting transfers between devices, swapped(): return lax.ppermute(x, 'inner', [(i, i ^ d) for i in range(inner_count)])  11.9 us
    pallas_call x6, Pallas kernels, call(): pl.pallas_call(body, out_shape=tuple((jax.ShapeDtypeStruct(shape, kind) f...  11.8 us
    ppermute x2, starting transfers between devices, moved(): return lax.ppermute(x, ('inner', 'outer'), route)  6.45 us
    ppermute x4, starting transfers between devices, returned(): return lax.ppermute(x, ('inner', 'outer'), route)  4.5 us
    ppermute x1, starting transfers between devices, grouped(): lax.ppermute(x, 'outer', [(i, (i + distance) % outer_count) for i in rang...  3 us
    ppermute x13, waiting for transfers between devices, swapped(): return lax.ppermute(x, 'inner', [(i, i ^ d) for i in range(inner_count)])  1.02 us
    ppermute x2, waiting for transfers between devices, moved(): return lax.ppermute(x, ('inner', 'outer'), route)  0.83 us
  transfers between devices with their start and end apart: 20, of which 4 were waited for; matrix products, arithmetic and copies ran while one was open for 1% of the time, Pallas kernels for 18%

profile of v5, /device:TPU:0, one launch (start us, length us, event | category | flops | bytes accessed | tf_op | source)
XLA Modules:
  0.0 41.3 jit_solution(12556905798415019792)
XLA Ops:
  0.6 0.8 %pack.1 = bf16[128,256]{1,0:T(8,128)(2,1)S(1)} custom-call(bf16[128,128]{1,0:T(8,128)(2,1)} %k_hbm.1, bf16[128,128]{1,0:T(8,128)(2,1)} %v_hbm.1), custom_call_target="tpu_custom_call" | custom-call | bytes 65536 | tf_op jit(solution)/shard_map/pack/pallas_call | solution.py:243
  1.4 3.0 %collective-permute-start.1 = (bf16[128,256]{1,0:T(8,128)(2,1)S(1)}, bf16[128,256]{1,0:T(8,128)(2,1)S(1)}, u32[]{:S(2)}, u32[]{:S(2)}) collective-permute-start(bf16[128,256]{1,0:T(8,128)(2,1)S(1)} %pack.1), channel_id=1, source_target_pairs={{0,1},{1,0},{2,3},{3,2},{4,5},{5,4},{6,7},{7,6},{8,9},{9,8},{10,11... | collective-permute-start | bytes 196616 | tf_op jit(solution)/shard_map/ppermute | solution.py:274
  4.4 2.6 %collective-permute-start = (bf16[128,256]{1,0:T(8,128)(2,1)S(1)}, bf16[128,256]{1,0:T(8,128)(2,1)S(1)}, u32[]{:S(2)}, u32[]{:S(2)}) collective-permute-start(bf16[128,256]{1,0:T(8,128)(2,1)S(1)} %pack.1), channel_id=1, source_target_pairs={{0,16},{2,18},{4,20},{6,22},{8,24},{10,26},{12,28},{14,30},{16,1},... | collective-permute-start | bytes 196616 | tf_op jit(solution)/shard_map/ppermute | solution.py:271
  7.1 2.8 %collective-permute-start.4 = (bf16[128,256]{1,0:T(8,128)(2,1)S(1)}, bf16[128,256]{1,0:T(8,128)(2,1)S(1)}, u32[]{:S(2)}, u32[]{:S(2)}) collective-permute-start(bf16[128,256]{1,0:T(8,128)(2,1)S(1)} %get-tuple-element.82), channel_id=1, source_target_pairs={{0,12},{2,14},{4,8},{6,10},{8,4},{10,6},{12,0},{14,2},{16,28},{18,... | collective-permute-start | bytes 196616 | tf_op jit(solution)/shard_map/ppermute | solution.py:284
  9.9 0.4 %collective-permute-start.3 = (bf16[128,256]{1,0:T(8,128)(2,1)S(1)}, bf16[128,256]{1,0:T(8,128)(2,1)S(1)}, u32[]{:S(2)}, u32[]{:S(2)}) collective-permute-start(bf16[128,256]{1,0:T(8,128)(2,1)S(1)} %get-tuple-element.83), channel_id=1, source_target_pairs={{0,8},{2,10},{4,12},{6,14},{8,0},{10,2},{12,4},{14,6},{16,24},{18,... | collective-permute-start | bytes 196616 | tf_op jit(solution)/shard_map/ppermute | solution.py:284
  10.3 0.3 collective-permute-start.2
  10.6 0.2 collective-permute-done
  10.8 1.6 %collective-permute-start.6 = (bf16[128,256]{1,0:T(8,128)(2,1)S(1)}, bf16[128,256]{1,0:T(8,128)(2,1)S(1)}, u32[]{:S(2)}, u32[]{:S(2)}) collective-permute-start(bf16[128,256]{1,0:T(8,128)(2,1)S(1)} %collective-permute-done), channel_id=1, source_target_pairs={{0,4},{2,6},{4,0},{6,2},{8,12},{10,14},{12,8},{14,10},{16,20},{18,... | collective-permute-start | bytes 196616 | tf_op jit(solution)/shard_map/ppermute | solution.py:284
  12.4 1.4 %collective-permute-start.5 = (bf16[128,256]{1,0:T(8,128)(2,1)S(1)}, bf16[128,256]{1,0:T(8,128)(2,1)S(1)}, u32[]{:S(2)}, u32[]{:S(2)}) collective-permute-start(bf16[128,256]{1,0:T(8,128)(2,1)S(1)} %collective-permute-done), channel_id=1, source_target_pairs={{0,12},{2,14},{4,8},{6,10},{8,4},{10,6},{12,0},{14,2},{16,28},{18,... | collective-permute-start | bytes 196616 | tf_op jit(solution)/shard_map/ppermute | solution.py:284
  13.9 0.4 collective-permute-done.3
  14.2 1.0 %collective-permute-start.7 = (bf16[128,256]{1,0:T(8,128)(2,1)S(1)}, bf16[128,256]{1,0:T(8,128)(2,1)S(1)}, u32[]{:S(2)}, u32[]{:S(2)}) collective-permute-start(bf16[128,256]{1,0:T(8,128)(2,1)S(1)} %collective-permute-done), channel_id=1, source_target_pairs={{0,8},{2,10},{4,12},{6,14},{8,0},{10,2},{12,4},{14,6},{16,24},{18,... | collective-permute-start | bytes 196616 | tf_op jit(solution)/shard_map/ppermute | solution.py:284
  15.3 0.1 collective-permute-start.9
  15.4 2.5 %early.1 = (bf16[128,1024]{1,0:T(8,128)(2,1)S(1)}, bf16[128,1024]{1,0:T(8,128)(2,1)S(1)}, f32[128,256]{1,0:T(8,128)S(1)}, bf16[640,1024]{1,0:T(8,128)(2,1)S(1)},...) custom-call(s32[32]{0:T(128)} %doc_hbm.1, s32[1]{0:T(128)} %bitcast.at_ref, ...), custom_call_target="tpu_custom_call" | custom-call | flops 6710886400 | bytes 65536 | tf_op jit(solution)/shard_map/early/pallas_call | solution.py:243
  17.9 0.6 %collective-permute-done.7 = bf16[128,256]{1,0:T(8,128)(2,1)S(1)} collective-permute-done((bf16[128,256]{1,0:T(8,128)(2,1)S(1)}, bf16[128,256]{1,0:T(8,128)(2,1)S(1)}, u32[]{:S(2)}, u32[]{:S(2)}) %collective-permute-start.7) | collective-permute-done | bytes 65568 | tf_op jit(solution)/shard_map/ppermute | solution.py:284
  18.5 0.1 collective-permute-start.8
  18.7 1.9 %middle.1 = (bf16[1024,1024]{1,0:T(8,128)(2,1)S(1)}, f32[1024,1024]{1,0:T(8,128)S(1)}, f32[144,1024]{1,0:T(8,128)S(1)}, f32[8,1024]{1,0:T(8,128)S(1)}) custom-call(f32[128,256]{1,0:T(8,128)S(1)} %get-tuple-element.41.bias_ref.refs_0_, bf16[128,1024]{1,0:T(8,128)(2,1)S(1)} %get-tuple-element.42.qt_ref.refs_1_, ...), custom_call_target="tpu_custom_call" | custom-call | flops 10737418240 | bytes 65536 | tf_op jit(solution)/shard_map/middle/pallas_call | solution.py:243
  20.6 3.7 %main.1 = (bf16[128,256]{1,0:T(8,128)(2,1)S(1)}, bf16[384,256]{1,0:T(8,128)(2,1)S(1)}, bf16[512,256]{1,0:T(8,128)(2,1)S(1)}, bf16[640,1024]{1,0:T(8,128)(2,1)S(1...) custom-call(f32[128,256]{1,0:T(8,128)S(1)} %get-tuple-element.41.bia, ...), custom_call_target="tpu_custom_call" | custom-call | flops 3221225472 | bytes 65536 | tf_op jit(solution)/shard_map/main/pallas_call | solution.py:243
  24.3 0.5 %collective-permute-start.10 = (bf16[512,256]{1,0:T(8,128)(2,1)S(1)}, bf16[512,256]{1,0:T(8,128)(2,1)S(1)}, u32[]{:S(2)}, u32[]{:S(2)}) collective-permute-start(bf16[512,256]{1,0:T(8,128)(2,1)S(1)} %get-tuple-element.63), channel_id=1, source_target_pairs={{0,2},{2,0},{4,6},{6,4},{8,10},{10,8},{12,14},{14,12},{16,18},{18,... | collective-permute-start | bytes 786440 | tf_op jit(solution)/shard_map/ppermute | solution.py:284
  24.9 0.1 collective-permute-start.14
  24.9 1.2 %kept.1 = (bf16[128,256]{1,0:T(8,128)(2,1)S(1)}, bf16[128,256]{1,0:T(8,128)(2,1)S(1)}, bf16[384,256]{1,0:T(8,128)(2,1)S(1)}, bf16[384,256]{1,0:T(8,128)(2,1)S(1)}) custom-call(bf16[640,1024]{1,0:T(8,128)(2,1)S(1)} %get-tuple-element.40.refs_4_.refs_0_, bf16[640,1024]{1,0:T(8,128)(2,1)S(1)} %get-tuple-element.56.refs_1_.refs_0_, ...), custom_call_target="tpu_custom_call" | custom-call | flops 536870912 | bytes 65536 | tf_op jit(solution)/shard_map/kept/pallas_call | solution.py:243
  26.3 1.7 %collective-permute-start.11 = (bf16[128,256]{1,0:T(8,128)(2,1)S(1)}, bf16[128,256]{1,0:T(8,128)(2,1)S(1)}, u32[]{:S(2)}, u32[]{:S(2)}) collective-permute-start(bf16[128,256]{1,0:T(8,128)(2,1)S(1)} %get-tuple-element.75), channel_id=1, source_target_pairs={{0,12},{2,14},{4,8},{6,10},{8,4},{10,6},{12,0},{14,2},{16,28},{18,... | collective-permute-start | bytes 196616 | tf_op jit(solution)/shard_map/ppermute | solution.py:284
  27.9 1.2 %collective-permute-start.13 = (bf16[128,256]{1,0:T(8,128)(2,1)S(1)}, bf16[128,256]{1,0:T(8,128)(2,1)S(1)}, u32[]{:S(2)}, u32[]{:S(2)}) collective-permute-start(bf16[128,256]{1,0:T(8,128)(2,1)S(1)} %get-tuple-element.76), channel_id=1, source_target_pairs={{0,4},{2,6},{4,0},{6,2},{8,12},{10,14},{12,8},{14,10},{16,20},{18,... | collective-permute-start | bytes 196616 | tf_op jit(solution)/shard_map/ppermute | solution.py:284
  29.2 0.6 %collective-permute-start.12 = (bf16[128,256]{1,0:T(8,128)(2,1)S(1)}, bf16[128,256]{1,0:T(8,128)(2,1)S(1)}, u32[]{:S(2)}, u32[]{:S(2)}) collective-permute-start(bf16[128,256]{1,0:T(8,128)(2,1)S(1)} %get-tuple-element.77), channel_id=1, source_target_pairs={{0,8},{2,10},{4,12},{6,14},{8,0},{10,2},{12,4},{14,6},{16,24},{18,... | collective-permute-start | bytes 196616 | tf_op jit(solution)/shard_map/ppermute | solution.py:284
  29.9 2.5 %collective-permute-start.15 = (bf16[128,256]{1,0:T(8,128)(2,1)S(1)}, bf16[128,256]{1,0:T(8,128)(2,1)S(1)}, u32[]{:S(2)}, u32[]{:S(2)}) collective-permute-start(bf16[128,256]{1,0:T(8,128)(2,1)S(1)} %get-tuple-element.78), channel_id=1, source_target_pairs={{0,13},{2,15},{4,9},{6,11},{8,4},{10,6},{12,0},{14,2},{16,29},{18,... | collective-permute-start | bytes 196616 | tf_op jit(solution)/shard_map/ppermute | solution.py:281
  32.4 1.3 %collective-permute-start.17 = (bf16[128,256]{1,0:T(8,128)(2,1)S(1)}, bf16[128,256]{1,0:T(8,128)(2,1)S(1)}, u32[]{:S(2)}, u32[]{:S(2)}) collective-permute-start(bf16[128,256]{1,0:T(8,128)(2,1)S(1)} %get-tuple-element.79), channel_id=1, source_target_pairs={{0,5},{2,7},{4,0},{6,2},{8,13},{10,15},{12,8},{14,10},{16,21},{18,... | collective-permute-start | bytes 196616 | tf_op jit(solution)/shard_map/ppermute | solution.py:281
  33.7 0.6 %collective-permute-start.16 = (bf16[128,256]{1,0:T(8,128)(2,1)S(1)}, bf16[128,256]{1,0:T(8,128)(2,1)S(1)}, u32[]{:S(2)}, u32[]{:S(2)}) collective-permute-start(bf16[128,256]{1,0:T(8,128)(2,1)S(1)} %get-tuple-element.80), channel_id=1, source_target_pairs={{0,9},{2,11},{4,13},{6,15},{8,0},{10,2},{12,4},{14,6},{16,25},{18,... | collective-permute-start | bytes 196616 | tf_op jit(solution)/shard_map/ppermute | solution.py:281
  34.4 0.1 collective-permute-start.18
  34.4 3.9 %collective-permute-start.19 = (bf16[128,256]{1,0:T(8,128)(2,1)S(1)}, bf16[128,256]{1,0:T(8,128)(2,1)S(1)}, u32[]{:S(2)}, u32[]{:S(2)}) collective-permute-start(bf16[128,256]{1,0:T(8,128)(2,1)S(1)} %add_convert_fusion.4.unused_ref), channel_id=1, source_target_pairs={{0,17},{2,19},{4,21},{6,23},{8,25},{10,27},{12,29},{14,31},{16,0},... | collective-permute-start | bytes 196616 | tf_op jit(solution)/shard_map/ppermute | solution.py:271
  38.3 1.6 %query.1 = bf16[128,1024]{1,0:T(8,128)(2,1)} custom-call(bf16[128,256]{1,0:T(8,128)(2,1)S(1)} %add_convert_fusion.4.unused_ref, bf16[640,1024]{1,0:T(8,128)(2,1)S(1)} %get-tuple-element.56.refs_1_.refs_0_, bf16[1024,1024]{1,0:T(8,128)(2,1)S(1)} %get-tuple-element.59.refs_5_.refs_1_, bf16[384,1024]{1,0:T(8,128)(2,1)S(1)} %get-tuple-element.67.refs_2_, ...), custom_call_target="tpu_custom_call" | custom-call | flops 536870912 | bytes 65536 | tf_op jit(solution)/shard_map/query/pallas_call | solution.py:243
  39.9 0.6 %collective-permute-done.19 = bf16[128,256]{1,0:T(8,128)(2,1)S(1)} collective-permute-done((bf16[128,256]{1,0:T(8,128)(2,1)S(1)}, bf16[128,256]{1,0:T(8,128)(2,1)S(1)}, u32[]{:S(2)}, u32[]{:S(2)}) %collective-permute-start.19) | collective-permute-done | bytes 65568 | tf_op jit(solution)/shard_map/ppermute | solution.py:271
  40.6 0.1 add_convert_fusion
  40.6 0.6 %fusion = (bf16[128,128]{1,0:T(8,128)(2,1)}, bf16[128,128]{1,0:T(8,128)(2,1)}) fusion(bf16[128,256]{1,0:T(8,128)(2,1)S(1)} %add_convert_fusion), kind=kLoop, calls=%fused_computation.26 | loop fusion | bytes 131072 | tf_op jit(solution)/shard_map/slice | solution.py:416
  (29 shorter events, 0.3 us)
Async XLA Ops:
  1.4 5.6 %collective-permute-start.1 = (bf16[128,256]{1,0:T(8,128)(2,1)S(1)}, bf16[128,256]{1,0:T(8,128)(2,1)S(1)}, u32[]{:S(2)}, u32[]{:S(2)}) collective-permute-start(bf16[128,256]{1,0:T(8,128)(2,1)S(1)} %pack.1), channel_id=1, source_target_pairs={{0,1},{1,0},{2,3},{3,2},{4,5},{5,4},{6,7},{7,6},{8,9},{9,8},{10,11... | collective-permute-start | bytes 196616 | tf_op jit(solution)/shard_map/ppermute | solution.py:274
  4.4 6.4 %collective-permute-start = (bf16[128,256]{1,0:T(8,128)(2,1)S(1)}, bf16[128,256]{1,0:T(8,128)(2,1)S(1)}, u32[]{:S(2)}, u32[]{:S(2)}) collective-permute-start(bf16[128,256]{1,0:T(8,128)(2,1)S(1)} %pack.1), channel_id=1, source_target_pairs={{0,16},{2,18},{4,20},{6,22},{8,24},{10,26},{12,28},{14,30},{16,1},... | collective-permute-start | bytes 196616 | tf_op jit(solution)/shard_map/ppermute | solution.py:271
  7.1 8.2 %collective-permute-start.4 = (bf16[128,256]{1,0:T(8,128)(2,1)S(1)}, bf16[128,256]{1,0:T(8,128)(2,1)S(1)}, u32[]{:S(2)}, u32[]{:S(2)}) collective-permute-start(bf16[128,256]{1,0:T(8,128)(2,1)S(1)} %get-tuple-element.82), channel_id=1, source_target_pairs={{0,12},{2,14},{4,8},{6,10},{8,4},{10,6},{12,0},{14,2},{16,28},{18,... | collective-permute-start | bytes 196616 | tf_op jit(solution)/shard_map/ppermute | solution.py:284
  9.9 4.4 %collective-permute-start.3 = (bf16[128,256]{1,0:T(8,128)(2,1)S(1)}, bf16[128,256]{1,0:T(8,128)(2,1)S(1)}, u32[]{:S(2)}, u32[]{:S(2)}) collective-permute-start(bf16[128,256]{1,0:T(8,128)(2,1)S(1)} %get-tuple-element.83), channel_id=1, source_target_pairs={{0,8},{2,10},{4,12},{6,14},{8,0},{10,2},{12,4},{14,6},{16,24},{18,... | collective-permute-start | bytes 196616 | tf_op jit(solution)/shard_map/ppermute | solution.py:284
  10.3 4.9 %collective-permute-start.2 = (bf16[128,256]{1,0:T(8,128)(2,1)S(1)}, bf16[128,256]{1,0:T(8,128)(2,1)S(1)}, u32[]{:S(2)}, u32[]{:S(2)}) collective-permute-start(bf16[128,256]{1,0:T(8,128)(2,1)S(1)} %get-tuple-element.84), channel_id=1, source_target_pairs={{0,4},{2,6},{4,0},{6,2},{8,12},{10,14},{12,8},{14,10},{16,20},{18,... | collective-permute-start | bytes 196616 | tf_op jit(solution)/shard_map/ppermute | solution.py:284
  10.8 7.1 %collective-permute-start.6 = (bf16[128,256]{1,0:T(8,128)(2,1)S(1)}, bf16[128,256]{1,0:T(8,128)(2,1)S(1)}, u32[]{:S(2)}, u32[]{:S(2)}) collective-permute-start(bf16[128,256]{1,0:T(8,128)(2,1)S(1)} %collective-permute-done), channel_id=1, source_target_pairs={{0,4},{2,6},{4,0},{6,2},{8,12},{10,14},{12,8},{14,10},{16,20},{18,... | collective-permute-start | bytes 196616 | tf_op jit(solution)/shard_map/ppermute | solution.py:284
  12.4 5.5 %collective-permute-start.5 = (bf16[128,256]{1,0:T(8,128)(2,1)S(1)}, bf16[128,256]{1,0:T(8,128)(2,1)S(1)}, u32[]{:S(2)}, u32[]{:S(2)}) collective-permute-start(bf16[128,256]{1,0:T(8,128)(2,1)S(1)} %collective-permute-done), channel_id=1, source_target_pairs={{0,12},{2,14},{4,8},{6,10},{8,4},{10,6},{12,0},{14,2},{16,28},{18,... | collective-permute-start | bytes 196616 | tf_op jit(solution)/shard_map/ppermute | solution.py:284
  14.2 4.3 %collective-permute-start.7 = (bf16[128,256]{1,0:T(8,128)(2,1)S(1)}, bf16[128,256]{1,0:T(8,128)(2,1)S(1)}, u32[]{:S(2)}, u32[]{:S(2)}) collective-permute-start(bf16[128,256]{1,0:T(8,128)(2,1)S(1)} %collective-permute-done), channel_id=1, source_target_pairs={{0,8},{2,10},{4,12},{6,14},{8,0},{10,2},{12,4},{14,6},{16,24},{18,... | collective-permute-start | bytes 196616 | tf_op jit(solution)/shard_map/ppermute | solution.py:284
  15.3 3.4 %collective-permute-start.9 = (bf16[640,256]{1,0:T(8,128)(2,1)S(1)}, bf16[640,256]{1,0:T(8,128)(2,1)S(1)}, u32[]{:S(2)}, u32[]{:S(2)}) collective-permute-start(bf16[640,256]{1,0:T(8,128)(2,1)S(1)} %get-tuple-element.87), channel_id=1, source_target_pairs={{0,2},{2,0},{4,6},{6,4},{8,10},{10,8},{12,14},{14,12},{16,18},{18,... | collective-permute-start | bytes 983048 | tf_op jit(solution)/shard_map/ppermute | solution.py:284
  18.5 2.1 %collective-permute-start.8 = (bf16[384,256]{1,0:T(8,128)(2,1)S(1)}, bf16[384,256]{1,0:T(8,128)(2,1)S(1)}, u32[]{:S(2)}, u32[]{:S(2)}) collective-permute-start(bf16[384,256]{1,0:T(8,128)(2,1)S(1)} %pad_maximum_fusion), channel_id=1, source_target_pairs={{0,2},{2,0},{4,6},{6,4},{8,10},{10,8},{12,14},{14,12},{16,18},{18,... | collective-permute-start | bytes 589832 | tf_op jit(solution)/shard_map/ppermute | solution.py:284
  24.3 1.9 %collective-permute-start.10 = (bf16[512,256]{1,0:T(8,128)(2,1)S(1)}, bf16[512,256]{1,0:T(8,128)(2,1)S(1)}, u32[]{:S(2)}, u32[]{:S(2)}) collective-permute-start(bf16[512,256]{1,0:T(8,128)(2,1)S(1)} %get-tuple-element.63), channel_id=1, source_target_pairs={{0,2},{2,0},{4,6},{6,4},{8,10},{10,8},{12,14},{14,12},{16,18},{18,... | collective-permute-start | bytes 786440 | tf_op jit(solution)/shard_map/ppermute | solution.py:284
  24.9 5.0 %collective-permute-start.14 = (bf16[384,256]{1,0:T(8,128)(2,1)S(1)}, bf16[384,256]{1,0:T(8,128)(2,1)S(1)}, u32[]{:S(2)}, u32[]{:S(2)}) collective-permute-start(bf16[384,256]{1,0:T(8,128)(2,1)S(1)} %get-tuple-element.73), channel_id=1, source_target_pairs={{0,2},{2,0},{4,6},{6,4},{8,10},{10,8},{12,14},{14,12},{16,18},{18,... | collective-permute-start | bytes 589832 | tf_op jit(solution)/shard_map/ppermute | solution.py:284
  26.3 7.4 %collective-permute-start.11 = (bf16[128,256]{1,0:T(8,128)(2,1)S(1)}, bf16[128,256]{1,0:T(8,128)(2,1)S(1)}, u32[]{:S(2)}, u32[]{:S(2)}) collective-permute-start(bf16[128,256]{1,0:T(8,128)(2,1)S(1)} %get-tuple-element.75), channel_id=1, source_target_pairs={{0,12},{2,14},{4,8},{6,10},{8,4},{10,6},{12,0},{14,2},{16,28},{18,... | collective-permute-start | bytes 196616 | tf_op jit(solution)/shard_map/ppermute | solution.py:284
  27.9 6.4 %collective-permute-start.13 = (bf16[128,256]{1,0:T(8,128)(2,1)S(1)}, bf16[128,256]{1,0:T(8,128)(2,1)S(1)}, u32[]{:S(2)}, u32[]{:S(2)}) collective-permute-start(bf16[128,256]{1,0:T(8,128)(2,1)S(1)} %get-tuple-element.76), channel_id=1, source_target_pairs={{0,4},{2,6},{4,0},{6,2},{8,12},{10,14},{12,8},{14,10},{16,20},{18,... | collective-permute-start | bytes 196616 | tf_op jit(solution)/shard_map/ppermute | solution.py:284
  29.2 5.1 %collective-permute-start.12 = (bf16[128,256]{1,0:T(8,128)(2,1)S(1)}, bf16[128,256]{1,0:T(8,128)(2,1)S(1)}, u32[]{:S(2)}, u32[]{:S(2)}) collective-permute-start(bf16[128,256]{1,0:T(8,128)(2,1)S(1)} %get-tuple-element.77), channel_id=1, source_target_pairs={{0,8},{2,10},{4,12},{6,14},{8,0},{10,2},{12,4},{14,6},{16,24},{18,... | collective-permute-start | bytes 196616 | tf_op jit(solution)/shard_map/ppermute | solution.py:284
  29.9 10.0 %collective-permute-start.15 = (bf16[128,256]{1,0:T(8,128)(2,1)S(1)}, bf16[128,256]{1,0:T(8,128)(2,1)S(1)}, u32[]{:S(2)}, u32[]{:S(2)}) collective-permute-start(bf16[128,256]{1,0:T(8,128)(2,1)S(1)} %get-tuple-element.78), channel_id=1, source_target_pairs={{0,13},{2,15},{4,9},{6,11},{8,4},{10,6},{12,0},{14,2},{16,29},{18,... | collective-permute-start | bytes 196616 | tf_op jit(solution)/shard_map/ppermute | solution.py:281
  32.4 7.5 %collective-permute-start.17 = (bf16[128,256]{1,0:T(8,128)(2,1)S(1)}, bf16[128,256]{1,0:T(8,128)(2,1)S(1)}, u32[]{:S(2)}, u32[]{:S(2)}) collective-permute-start(bf16[128,256]{1,0:T(8,128)(2,1)S(1)} %get-tuple-element.79), channel_id=1, source_target_pairs={{0,5},{2,7},{4,0},{6,2},{8,13},{10,15},{12,8},{14,10},{16,21},{18,... | collective-permute-start | bytes 196616 | tf_op jit(solution)/shard_map/ppermute | solution.py:281
  33.7 6.2 %collective-permute-start.16 = (bf16[128,256]{1,0:T(8,128)(2,1)S(1)}, bf16[128,256]{1,0:T(8,128)(2,1)S(1)}, u32[]{:S(2)}, u32[]{:S(2)}) collective-permute-start(bf16[128,256]{1,0:T(8,128)(2,1)S(1)} %get-tuple-element.80), channel_id=1, source_target_pairs={{0,9},{2,11},{4,13},{6,15},{8,0},{10,2},{12,4},{14,6},{16,25},{18,... | collective-permute-start | bytes 196616 | tf_op jit(solution)/shard_map/ppermute | solution.py:281
  34.4 5.6 %collective-permute-start.18 = (bf16[128,256]{1,0:T(8,128)(2,1)S(1)}, bf16[128,256]{1,0:T(8,128)(2,1)S(1)}, u32[]{:S(2)}, u32[]{:S(2)}) collective-permute-start(bf16[128,256]{1,0:T(8,128)(2,1)S(1)} %get-tuple-element.74), channel_id=1, source_target_pairs={{0,3},{2,0},{4,7},{6,4},{8,11},{10,8},{12,15},{14,12},{16,19},{18,... | collective-permute-start | bytes 196616 | tf_op jit(solution)/shard_map/ppermute | solution.py:281
  34.4 6.1 %collective-permute-start.19 = (bf16[128,256]{1,0:T(8,128)(2,1)S(1)}, bf16[128,256]{1,0:T(8,128)(2,1)S(1)}, u32[]{:S(2)}, u32[]{:S(2)}) collective-permute-start(bf16[128,256]{1,0:T(8,128)(2,1)S(1)} %add_convert_fusion.4.unused_ref), channel_id=1, source_target_pairs={{0,17},{2,19},{4,21},{6,23},{8,25},{10,27},{12,29},{14,31},{16,0},... | collective-permute-start | bytes 196616 | tf_op jit(solution)/shard_map/ppermute | solution.py:271

commit v6 on v5

--- a/solution.py
+++ b/solution.py
@@ -407,7 +407,7 @@
         [(queries.shape, LOW)],
         [],
         work * span,
-        *(far_sum, *ds, *factors, *groups),
+        *(first_part, *ds, *factors, *groups),
     )
     mine = own_part.astype(F32)
     for one in near_home + [first_home, far_home]:

time: 41.5 us -> 41.1 us (level)
  no operation moved by 1% of the time
where the time goes in v6:
time: 41.1 us; the launch traced here: 40.8 us
  starting transfers between devices  25.8 us (63%)
  Pallas kernels  11.8 us (29%)
  waiting for transfers between devices  1.52 us (4%)
  between operations  0.83 us (2%)
  local copies, waits for them, and re-layouts  0.72 us (2%)
    ppermute x13, starting transfers between devices, swapped(): return lax.ppermute(x, 'inner', [(i, i ^ d) for i in range(inner_count)])  11.9 us
    pallas_call x6, Pallas kernels, call(): pl.pallas_call(body, out_shape=tuple((jax.ShapeDtypeStruct(shape, kind) f...  11.8 us
    ppermute x2, starting transfers between devices, moved(): return lax.ppermute(x, ('inner', 'outer'), route)  6.45 us
    ppermute x4, starting transfers between devices, returned(): return lax.ppermute(x, ('inner', 'outer'), route)  4.44 us
    ppermute x1, starting transfers between devices, grouped(): lax.ppermute(x, 'outer', [(i, (i + distance) % outer_count) for i in rang...  3 us
    ppermute x13, waiting for transfers between devices, swapped(): return lax.ppermute(x, 'inner', [(i, i ^ d) for i in range(inner_count)])  1.02 us
  transfers between devices with their start and end apart: 20, of which 4 were waited for; matrix products, arithmetic and copies ran while one was open for 1% of the time, Pallas kernels for 18%

profile of v6, /device:TPU:0, one launch (start us, length us, event | category | flops | bytes accessed | tf_op | source)
XLA Modules:
  0.0 40.8 jit_solution(10730515415004371762)
XLA Ops:
  0.6 0.8 %pack.1 = bf16[128,256]{1,0:T(8,128)(2,1)S(1)} custom-call(bf16[128,128]{1,0:T(8,128)(2,1)} %k_hbm.1, bf16[128,128]{1,0:T(8,128)(2,1)} %v_hbm.1), custom_call_target="tpu_custom_call" | custom-call | bytes 65536 | tf_op jit(solution)/shard_map/pack/pallas_call | solution.py:243
  1.4 3.0 %collective-permute-start.1 = (bf16[128,256]{1,0:T(8,128)(2,1)S(1)}, bf16[128,256]{1,0:T(8,128)(2,1)S(1)}, u32[]{:S(2)}, u32[]{:S(2)}) collective-permute-start(bf16[128,256]{1,0:T(8,128)(2,1)S(1)} %pack.1), channel_id=1, source_target_pairs={{0,1},{1,0},{2,3},{3,2},{4,5},{5,4},{6,7},{7,6},{8,9},{9,8},{10,11... | collective-permute-start | bytes 196616 | tf_op jit(solution)/shard_map/ppermute | solution.py:274
  4.4 2.6 %collective-permute-start = (bf16[128,256]{1,0:T(8,128)(2,1)S(1)}, bf16[128,256]{1,0:T(8,128)(2,1)S(1)}, u32[]{:S(2)}, u32[]{:S(2)}) collective-permute-start(bf16[128,256]{1,0:T(8,128)(2,1)S(1)} %pack.1), channel_id=1, source_target_pairs={{0,16},{2,18},{4,20},{6,22},{8,24},{10,26},{12,28},{14,30},{16,1},... | collective-permute-start | bytes 196616 | tf_op jit(solution)/shard_map/ppermute | solution.py:271
  7.0 0.0 collective-permute-done.1
  7.1 2.8 %collective-permute-start.4 = (bf16[128,256]{1,0:T(8,128)(2,1)S(1)}, bf16[128,256]{1,0:T(8,128)(2,1)S(1)}, u32[]{:S(2)}, u32[]{:S(2)}) collective-permute-start(bf16[128,256]{1,0:T(8,128)(2,1)S(1)} %get-tuple-element.82), channel_id=1, source_target_pairs={{0,12},{2,14},{4,8},{6,10},{8,4},{10,6},{12,0},{14,2},{16,28},{18,... | collective-permute-start | bytes 196616 | tf_op jit(solution)/shard_map/ppermute | solution.py:284
  9.9 0.4 %collective-permute-start.3 = (bf16[128,256]{1,0:T(8,128)(2,1)S(1)}, bf16[128,256]{1,0:T(8,128)(2,1)S(1)}, u32[]{:S(2)}, u32[]{:S(2)}) collective-permute-start(bf16[128,256]{1,0:T(8,128)(2,1)S(1)} %get-tuple-element.83), channel_id=1, source_target_pairs={{0,8},{2,10},{4,12},{6,14},{8,0},{10,2},{12,4},{14,6},{16,24},{18,... | collective-permute-start | bytes 196616 | tf_op jit(solution)/shard_map/ppermute | solution.py:284
  10.3 0.3 collective-permute-start.2
  10.6 0.2 collective-permute-done
  10.8 1.6 %collective-permute-start.6 = (bf16[128,256]{1,0:T(8,128)(2,1)S(1)}, bf16[128,256]{1,0:T(8,128)(2,1)S(1)}, u32[]{:S(2)}, u32[]{:S(2)}) collective-permute-start(bf16[128,256]{1,0:T(8,128)(2,1)S(1)} %collective-permute-done), channel_id=1, source_target_pairs={{0,4},{2,6},{4,0},{6,2},{8,12},{10,14},{12,8},{14,10},{16,20},{18,... | collective-permute-start | bytes 196616 | tf_op jit(solution)/shard_map/ppermute | solution.py:284
  12.4 1.4 %collective-permute-start.5 = (bf16[128,256]{1,0:T(8,128)(2,1)S(1)}, bf16[128,256]{1,0:T(8,128)(2,1)S(1)}, u32[]{:S(2)}, u32[]{:S(2)}) collective-permute-start(bf16[128,256]{1,0:T(8,128)(2,1)S(1)} %collective-permute-done), channel_id=1, source_target_pairs={{0,12},{2,14},{4,8},{6,10},{8,4},{10,6},{12,0},{14,2},{16,28},{18,... | collective-permute-start | bytes 196616 | tf_op jit(solution)/shard_map/ppermute | solution.py:284
  13.9 0.4 collective-permute-done.3
  14.2 1.0 %collective-permute-start.7 = (bf16[128,256]{1,0:T(8,128)(2,1)S(1)}, bf16[128,256]{1,0:T(8,128)(2,1)S(1)}, u32[]{:S(2)}, u32[]{:S(2)}) collective-permute-start(bf16[128,256]{1,0:T(8,128)(2,1)S(1)} %collective-permute-done), channel_id=1, source_target_pairs={{0,8},{2,10},{4,12},{6,14},{8,0},{10,2},{12,4},{14,6},{16,24},{18,... | collective-permute-start | bytes 196616 | tf_op jit(solution)/shard_map/ppermute | solution.py:284
  15.3 0.1 collective-permute-start.9
  15.4 2.5 %early.1 = (bf16[128,1024]{1,0:T(8,128)(2,1)S(1)}, bf16[128,1024]{1,0:T(8,128)(2,1)S(1)}, f32[128,256]{1,0:T(8,128)S(1)}, bf16[640,1024]{1,0:T(8,128)(2,1)S(1)},...) custom-call(s32[32]{0:T(128)} %doc_hbm.1, s32[1]{0:T(128)} %bitcast.at_ref, ...), custom_call_target="tpu_custom_call" | custom-call | flops 6710886400 | bytes 65536 | tf_op jit(solution)/shard_map/early/pallas_call | solution.py:243
  17.9 0.6 %collective-permute-done.7 = bf16[128,256]{1,0:T(8,128)(2,1)S(1)} collective-permute-done((bf16[128,256]{1,0:T(8,128)(2,1)S(1)}, bf16[128,256]{1,0:T(8,128)(2,1)S(1)}, u32[]{:S(2)}, u32[]{:S(2)}) %collective-permute-start.7) | collective-permute-done | bytes 65568 | tf_op jit(solution)/shard_map/ppermute | solution.py:284
  18.5 0.1 collective-permute-start.8
  18.7 1.9 %middle.1 = (bf16[1024,1024]{1,0:T(8,128)(2,1)S(1)}, f32[1024,1024]{1,0:T(8,128)S(1)}, f32[144,1024]{1,0:T(8,128)S(1)}, f32[8,1024]{1,0:T(8,128)S(1)}) custom-call(f32[128,256]{1,0:T(8,128)S(1)} %get-tuple-element.41.bias_ref.refs_0_, bf16[128,1024]{1,0:T(8,128)(2,1)S(1)} %get-tuple-element.42.qt_ref.refs_1_, ...), custom_call_target="tpu_custom_call" | custom-call | flops 10737418240 | bytes 65536 | tf_op jit(solution)/shard_map/middle/pallas_call | solution.py:243
  20.6 3.7 %main.1 = (bf16[128,256]{1,0:T(8,128)(2,1)S(1)}, bf16[384,256]{1,0:T(8,128)(2,1)S(1)}, bf16[512,256]{1,0:T(8,128)(2,1)S(1)}, bf16[640,1024]{1,0:T(8,128)(2,1)S(1...) custom-call(f32[128,256]{1,0:T(8,128)S(1)} %get-tuple-element.41.bia, ...), custom_call_target="tpu_custom_call" | custom-call | flops 3221225472 | bytes 65536 | tf_op jit(solution)/shard_map/main/pallas_call | solution.py:243
  24.3 0.5 %collective-permute-start.10 = (bf16[512,256]{1,0:T(8,128)(2,1)S(1)}, bf16[512,256]{1,0:T(8,128)(2,1)S(1)}, u32[]{:S(2)}, u32[]{:S(2)}) collective-permute-start(bf16[512,256]{1,0:T(8,128)(2,1)S(1)} %get-tuple-element.63), channel_id=1, source_target_pairs={{0,2},{2,0},{4,6},{6,4},{8,10},{10,8},{12,14},{14,12},{16,18},{18,... | collective-permute-start | bytes 786440 | tf_op jit(solution)/shard_map/ppermute | solution.py:284
  24.9 0.1 collective-permute-start.14
  24.9 1.2 %kept.1 = (bf16[128,256]{1,0:T(8,128)(2,1)S(1)}, bf16[128,256]{1,0:T(8,128)(2,1)S(1)}, bf16[384,256]{1,0:T(8,128)(2,1)S(1)}, bf16[384,256]{1,0:T(8,128)(2,1)S(1)}) custom-call(bf16[640,1024]{1,0:T(8,128)(2,1)S(1)} %get-tuple-element.40.refs_4_.refs_0_, bf16[640,1024]{1,0:T(8,128)(2,1)S(1)} %get-tuple-element.56.refs_1_.refs_0_, ...), custom_call_target="tpu_custom_call" | custom-call | flops 536870912 | bytes 65536 | tf_op jit(solution)/shard_map/kept/pallas_call | solution.py:243
  26.3 1.7 %collective-permute-start.11 = (bf16[128,256]{1,0:T(8,128)(2,1)S(1)}, bf16[128,256]{1,0:T(8,128)(2,1)S(1)}, u32[]{:S(2)}, u32[]{:S(2)}) collective-permute-start(bf16[128,256]{1,0:T(8,128)(2,1)S(1)} %get-tuple-element.75), channel_id=1, source_target_pairs={{0,12},{2,14},{4,8},{6,10},{8,4},{10,6},{12,0},{14,2},{16,28},{18,... | collective-permute-start | bytes 196616 | tf_op jit(solution)/shard_map/ppermute | solution.py:284
  27.9 1.2 %collective-permute-start.13 = (bf16[128,256]{1,0:T(8,128)(2,1)S(1)}, bf16[128,256]{1,0:T(8,128)(2,1)S(1)}, u32[]{:S(2)}, u32[]{:S(2)}) collective-permute-start(bf16[128,256]{1,0:T(8,128)(2,1)S(1)} %get-tuple-element.76), channel_id=1, source_target_pairs={{0,4},{2,6},{4,0},{6,2},{8,12},{10,14},{12,8},{14,10},{16,20},{18,... | collective-permute-start | bytes 196616 | tf_op jit(solution)/shard_map/ppermute | solution.py:284
  29.2 0.6 %collective-permute-start.12 = (bf16[128,256]{1,0:T(8,128)(2,1)S(1)}, bf16[128,256]{1,0:T(8,128)(2,1)S(1)}, u32[]{:S(2)}, u32[]{:S(2)}) collective-permute-start(bf16[128,256]{1,0:T(8,128)(2,1)S(1)} %get-tuple-element.77), channel_id=1, source_target_pairs={{0,8},{2,10},{4,12},{6,14},{8,0},{10,2},{12,4},{14,6},{16,24},{18,... | collective-permute-start | bytes 196616 | tf_op jit(solution)/shard_map/ppermute | solution.py:284
  29.9 2.5 %collective-permute-start.15 = (bf16[128,256]{1,0:T(8,128)(2,1)S(1)}, bf16[128,256]{1,0:T(8,128)(2,1)S(1)}, u32[]{:S(2)}, u32[]{:S(2)}) collective-permute-start(bf16[128,256]{1,0:T(8,128)(2,1)S(1)} %get-tuple-element.78), channel_id=1, source_target_pairs={{0,13},{2,15},{4,9},{6,11},{8,4},{10,6},{12,0},{14,2},{16,29},{18,... | collective-permute-start | bytes 196616 | tf_op jit(solution)/shard_map/ppermute | solution.py:281
  32.4 1.3 %collective-permute-start.17 = (bf16[128,256]{1,0:T(8,128)(2,1)S(1)}, bf16[128,256]{1,0:T(8,128)(2,1)S(1)}, u32[]{:S(2)}, u32[]{:S(2)}) collective-permute-start(bf16[128,256]{1,0:T(8,128)(2,1)S(1)} %get-tuple-element.79), channel_id=1, source_target_pairs={{0,5},{2,7},{4,0},{6,2},{8,13},{10,15},{12,8},{14,10},{16,21},{18,... | collective-permute-start | bytes 196616 | tf_op jit(solution)/shard_map/ppermute | solution.py:281
  33.7 0.6 %collective-permute-start.16 = (bf16[128,256]{1,0:T(8,128)(2,1)S(1)}, bf16[128,256]{1,0:T(8,128)(2,1)S(1)}, u32[]{:S(2)}, u32[]{:S(2)}) collective-permute-start(bf16[128,256]{1,0:T(8,128)(2,1)S(1)} %get-tuple-element.80), channel_id=1, source_target_pairs={{0,9},{2,11},{4,13},{6,15},{8,0},{10,2},{12,4},{14,6},{16,25},{18,... | collective-permute-start | bytes 196616 | tf_op jit(solution)/shard_map/ppermute | solution.py:281
  34.4 3.9 %collective-permute-start.19 = (bf16[128,256]{1,0:T(8,128)(2,1)S(1)}, bf16[128,256]{1,0:T(8,128)(2,1)S(1)}, u32[]{:S(2)}, u32[]{:S(2)}) collective-permute-start(bf16[128,256]{1,0:T(8,128)(2,1)S(1)} %add_convert_fusion.4), channel_id=1, source_target_pairs={{0,17},{2,19},{4,21},{6,23},{8,25},{10,27},{12,29},{14,31},{16,0},... | collective-permute-start | bytes 196616 | tf_op jit(solution)/shard_map/ppermute | solution.py:271
  38.2 1.6 %query.1 = bf16[128,1024]{1,0:T(8,128)(2,1)} custom-call(bf16[128,256]{1,0:T(8,128)(2,1)S(1)} %get-tuple-element.66.unused_ref, bf16[640,1024]{1,0:T(8,128)(2,1)S(1)} %get-tuple-element.56.refs_1_.refs_0_, bf16[1024,1024]{1,0:T(8,128)(2,1)S(1)} %get-tuple-element.59.refs_5_.refs_1_, bf16[384,1024]{1,0:T(8,128)(2,1)S(1)} %get-tuple-element.67.refs_2_, ...), custom_call_target="tpu_custom_call" | custom-call | flops 536870912 | bytes 65536 | tf_op jit(solution)/shard_map/query/pallas_call | solution.py:243
  39.9 0.3 collective-permute-done.19
  40.2 0.1 add_convert_fusion
  40.2 0.6 %fusion = (bf16[128,128]{1,0:T(8,128)(2,1)}, bf16[128,128]{1,0:T(8,128)(2,1)}) fusion(bf16[128,256]{1,0:T(8,128)(2,1)S(1)} %add_convert_fusion), kind=kLoop, calls=%fused_computation.26 | loop fusion | bytes 131072 | tf_op jit(solution)/shard_map/slice | solution.py:416
  (29 shorter events, 0.3 us)
Async XLA Ops:
  1.4 5.6 %collective-permute-start.1 = (bf16[128,256]{1,0:T(8,128)(2,1)S(1)}, bf16[128,256]{1,0:T(8,128)(2,1)S(1)}, u32[]{:S(2)}, u32[]{:S(2)}) collective-permute-start(bf16[128,256]{1,0:T(8,128)(2,1)S(1)} %pack.1), channel_id=1, source_target_pairs={{0,1},{1,0},{2,3},{3,2},{4,5},{5,4},{6,7},{7,6},{8,9},{9,8},{10,11... | collective-permute-start | bytes 196616 | tf_op jit(solution)/shard_map/ppermute | solution.py:274
  4.4 6.4 %collective-permute-start = (bf16[128,256]{1,0:T(8,128)(2,1)S(1)}, bf16[128,256]{1,0:T(8,128)(2,1)S(1)}, u32[]{:S(2)}, u32[]{:S(2)}) collective-permute-start(bf16[128,256]{1,0:T(8,128)(2,1)S(1)} %pack.1), channel_id=1, source_target_pairs={{0,16},{2,18},{4,20},{6,22},{8,24},{10,26},{12,28},{14,30},{16,1},... | collective-permute-start | bytes 196616 | tf_op jit(solution)/shard_map/ppermute | solution.py:271
  7.1 8.2 %collective-permute-start.4 = (bf16[128,256]{1,0:T(8,128)(2,1)S(1)}, bf16[128,256]{1,0:T(8,128)(2,1)S(1)}, u32[]{:S(2)}, u32[]{:S(2)}) collective-permute-start(bf16[128,256]{1,0:T(8,128)(2,1)S(1)} %get-tuple-element.82), channel_id=1, source_target_pairs={{0,12},{2,14},{4,8},{6,10},{8,4},{10,6},{12,0},{14,2},{16,28},{18,... | collective-permute-start | bytes 196616 | tf_op jit(solution)/shard_map/ppermute | solution.py:284
  9.9 4.4 %collective-permute-start.3 = (bf16[128,256]{1,0:T(8,128)(2,1)S(1)}, bf16[128,256]{1,0:T(8,128)(2,1)S(1)}, u32[]{:S(2)}, u32[]{:S(2)}) collective-permute-start(bf16[128,256]{1,0:T(8,128)(2,1)S(1)} %get-tuple-element.83), channel_id=1, source_target_pairs={{0,8},{2,10},{4,12},{6,14},{8,0},{10,2},{12,4},{14,6},{16,24},{18,... | collective-permute-start | bytes 196616 | tf_op jit(solution)/shard_map/ppermute | solution.py:284
  10.3 4.9 %collective-permute-start.2 = (bf16[128,256]{1,0:T(8,128)(2,1)S(1)}, bf16[128,256]{1,0:T(8,128)(2,1)S(1)}, u32[]{:S(2)}, u32[]{:S(2)}) collective-permute-start(bf16[128,256]{1,0:T(8,128)(2,1)S(1)} %get-tuple-element.84), channel_id=1, source_target_pairs={{0,4},{2,6},{4,0},{6,2},{8,12},{10,14},{12,8},{14,10},{16,20},{18,... | collective-permute-start | bytes 196616 | tf_op jit(solution)/shard_map/ppermute | solution.py:284
  10.8 7.1 %collective-permute-start.6 = (bf16[128,256]{1,0:T(8,128)(2,1)S(1)}, bf16[128,256]{1,0:T(8,128)(2,1)S(1)}, u32[]{:S(2)}, u32[]{:S(2)}) collective-permute-start(bf16[128,256]{1,0:T(8,128)(2,1)S(1)} %collective-permute-done), channel_id=1, source_target_pairs={{0,4},{2,6},{4,0},{6,2},{8,12},{10,14},{12,8},{14,10},{16,20},{18,... | collective-permute-start | bytes 196616 | tf_op jit(solution)/shard_map/ppermute | solution.py:284
  12.4 5.5 %collective-permute-start.5 = (bf16[128,256]{1,0:T(8,128)(2,1)S(1)}, bf16[128,256]{1,0:T(8,128)(2,1)S(1)}, u32[]{:S(2)}, u32[]{:S(2)}) collective-permute-start(bf16[128,256]{1,0:T(8,128)(2,1)S(1)} %collective-permute-done), channel_id=1, source_target_pairs={{0,12},{2,14},{4,8},{6,10},{8,4},{10,6},{12,0},{14,2},{16,28},{18,... | collective-permute-start | bytes 196616 | tf_op jit(solution)/shard_map/ppermute | solution.py:284
  14.2 4.3 %collective-permute-start.7 = (bf16[128,256]{1,0:T(8,128)(2,1)S(1)}, bf16[128,256]{1,0:T(8,128)(2,1)S(1)}, u32[]{:S(2)}, u32[]{:S(2)}) collective-permute-start(bf16[128,256]{1,0:T(8,128)(2,1)S(1)} %collective-permute-done), channel_id=1, source_target_pairs={{0,8},{2,10},{4,12},{6,14},{8,0},{10,2},{12,4},{14,6},{16,24},{18,... | collective-permute-start | bytes 196616 | tf_op jit(solution)/shard_map/ppermute | solution.py:284
  15.3 3.4 %collective-permute-start.9 = (bf16[640,256]{1,0:T(8,128)(2,1)S(1)}, bf16[640,256]{1,0:T(8,128)(2,1)S(1)}, u32[]{:S(2)}, u32[]{:S(2)}) collective-permute-start(bf16[640,256]{1,0:T(8,128)(2,1)S(1)} %get-tuple-element.87), channel_id=1, source_target_pairs={{0,2},{2,0},{4,6},{6,4},{8,10},{10,8},{12,14},{14,12},{16,18},{18,... | collective-permute-start | bytes 983048 | tf_op jit(solution)/shard_map/ppermute | solution.py:284
  18.5 2.1 %collective-permute-start.8 = (bf16[384,256]{1,0:T(8,128)(2,1)S(1)}, bf16[384,256]{1,0:T(8,128)(2,1)S(1)}, u32[]{:S(2)}, u32[]{:S(2)}) collective-permute-start(bf16[384,256]{1,0:T(8,128)(2,1)S(1)} %pad_maximum_fusion), channel_id=1, source_target_pairs={{0,2},{2,0},{4,6},{6,4},{8,10},{10,8},{12,14},{14,12},{16,18},{18,... | collective-permute-start | bytes 589832 | tf_op jit(solution)/shard_map/ppermute | solution.py:284
  24.3 1.9 %collective-permute-start.10 = (bf16[512,256]{1,0:T(8,128)(2,1)S(1)}, bf16[512,256]{1,0:T(8,128)(2,1)S(1)}, u32[]{:S(2)}, u32[]{:S(2)}) collective-permute-start(bf16[512,256]{1,0:T(8,128)(2,1)S(1)} %get-tuple-element.63), channel_id=1, source_target_pairs={{0,2},{2,0},{4,6},{6,4},{8,10},{10,8},{12,14},{14,12},{16,18},{18,... | collective-permute-start | bytes 786440 | tf_op jit(solution)/shard_map/ppermute | solution.py:284
  24.9 5.0 %collective-permute-start.14 = (bf16[384,256]{1,0:T(8,128)(2,1)S(1)}, bf16[384,256]{1,0:T(8,128)(2,1)S(1)}, u32[]{:S(2)}, u32[]{:S(2)}) collective-permute-start(bf16[384,256]{1,0:T(8,128)(2,1)S(1)} %get-tuple-element.73), channel_id=1, source_target_pairs={{0,2},{2,0},{4,6},{6,4},{8,10},{10,8},{12,14},{14,12},{16,18},{18,... | collective-permute-start | bytes 589832 | tf_op jit(solution)/shard_map/ppermute | solution.py:284
  26.3 7.4 %collective-permute-start.11 = (bf16[128,256]{1,0:T(8,128)(2,1)S(1)}, bf16[128,256]{1,0:T(8,128)(2,1)S(1)}, u32[]{:S(2)}, u32[]{:S(2)}) collective-permute-start(bf16[128,256]{1,0:T(8,128)(2,1)S(1)} %get-tuple-element.75), channel_id=1, source_target_pairs={{0,12},{2,14},{4,8},{6,10},{8,4},{10,6},{12,0},{14,2},{16,28},{18,... | collective-permute-start | bytes 196616 | tf_op jit(solution)/shard_map/ppermute | solution.py:284
  27.9 6.4 %collective-permute-start.13 = (bf16[128,256]{1,0:T(8,128)(2,1)S(1)}, bf16[128,256]{1,0:T(8,128)(2,1)S(1)}, u32[]{:S(2)}, u32[]{:S(2)}) collective-permute-start(bf16[128,256]{1,0:T(8,128)(2,1)S(1)} %get-tuple-element.76), channel_id=1, source_target_pairs={{0,4},{2,6},{4,0},{6,2},{8,12},{10,14},{12,8},{14,10},{16,20},{18,... | collective-permute-start | bytes 196616 | tf_op jit(solution)/shard_map/ppermute | solution.py:284
  29.2 5.1 %collective-permute-start.12 = (bf16[128,256]{1,0:T(8,128)(2,1)S(1)}, bf16[128,256]{1,0:T(8,128)(2,1)S(1)}, u32[]{:S(2)}, u32[]{:S(2)}) collective-permute-start(bf16[128,256]{1,0:T(8,128)(2,1)S(1)} %get-tuple-element.77), channel_id=1, source_target_pairs={{0,8},{2,10},{4,12},{6,14},{8,0},{10,2},{12,4},{14,6},{16,24},{18,... | collective-permute-start | bytes 196616 | tf_op jit(solution)/shard_map/ppermute | solution.py:284
  29.9 10.0 %collective-permute-start.15 = (bf16[128,256]{1,0:T(8,128)(2,1)S(1)}, bf16[128,256]{1,0:T(8,128)(2,1)S(1)}, u32[]{:S(2)}, u32[]{:S(2)}) collective-permute-start(bf16[128,256]{1,0:T(8,128)(2,1)S(1)} %get-tuple-element.78), channel_id=1, source_target_pairs={{0,13},{2,15},{4,9},{6,11},{8,4},{10,6},{12,0},{14,2},{16,29},{18,... | collective-permute-start | bytes 196616 | tf_op jit(solution)/shard_map/ppermute | solution.py:281
  32.4 7.5 %collective-permute-start.17 = (bf16[128,256]{1,0:T(8,128)(2,1)S(1)}, bf16[128,256]{1,0:T(8,128)(2,1)S(1)}, u32[]{:S(2)}, u32[]{:S(2)}) collective-permute-start(bf16[128,256]{1,0:T(8,128)(2,1)S(1)} %get-tuple-element.79), channel_id=1, source_target_pairs={{0,5},{2,7},{4,0},{6,2},{8,13},{10,15},{12,8},{14,10},{16,21},{18,... | collective-permute-start | bytes 196616 | tf_op jit(solution)/shard_map/ppermute | solution.py:281
  33.7 6.2 %collective-permute-start.16 = (bf16[128,256]{1,0:T(8,128)(2,1)S(1)}, bf16[128,256]{1,0:T(8,128)(2,1)S(1)}, u32[]{:S(2)}, u32[]{:S(2)}) collective-permute-start(bf16[128,256]{1,0:T(8,128)(2,1)S(1)} %get-tuple-element.80), channel_id=1, source_target_pairs={{0,9},{2,11},{4,13},{6,15},{8,0},{10,2},{12,4},{14,6},{16,25},{18,... | collective-permute-start | bytes 196616 | tf_op jit(solution)/shard_map/ppermute | solution.py:281
  34.4 5.8 %collective-permute-start.19 = (bf16[128,256]{1,0:T(8,128)(2,1)S(1)}, bf16[128,256]{1,0:T(8,128)(2,1)S(1)}, u32[]{:S(2)}, u32[]{:S(2)}) collective-permute-start(bf16[128,256]{1,0:T(8,128)(2,1)S(1)} %add_convert_fusion.4), channel_id=1, source_target_pairs={{0,17},{2,19},{4,21},{6,23},{8,25},{10,27},{12,29},{14,31},{16,0},... | collective-permute-start | bytes 196616 | tf_op jit(solution)/shard_map/ppermute | solution.py:271
  38.2 1.9 %collective-permute-start.18 = (bf16[128,256]{1,0:T(8,128)(2,1)S(1)}, bf16[128,256]{1,0:T(8,128)(2,1)S(1)}, u32[]{:S(2)}, u32[]{:S(2)}) collective-permute-start(bf16[128,256]{1,0:T(8,128)(2,1)S(1)} %get-tuple-element.66.unused_ref), channel_id=1, source_target_pairs={{0,3},{2,0},{4,7},{6,4},{8,11},{10,8},{12,15},{14,12},{16,19},{18,... | collective-permute-start | bytes 196616 | tf_op jit(solution)/shard_map/ppermute | solution.py:281

commit v7 on v6

--- a/solution.py
+++ b/solution.py
@@ -192,12 +192,11 @@
             place += count
 
     for hp in range(-2, pairs):
-        if hp >= 0:
-            settle(hp)
         if hp + 2 < pairs:
             score(hp + 2)
         if 0 <= hp + 1 < pairs:
             weigh(hp + 1)
+            settle(hp + 1)
         if hp >= 0:
             spread(hp)
 

time: 41.1 us -> 41.1 us (level)
  no operation moved by 1% of the time
where the time goes in v7:
time: 41.1 us; the launch traced here: 40.8 us
  starting transfers between devices  25.8 us (63%)
  Pallas kernels  11.8 us (29%)
  waiting for transfers between devices  1.52 us (4%)
  between operations  0.83 us (2%)
  local copies, waits for them, and re-layouts  0.72 us (2%)
    ppermute x13, starting transfers between devices, swapped(): return lax.ppermute(x, 'inner', [(i, i ^ d) for i in range(inner_count)])  11.9 us
    pallas_call x6, Pallas kernels, call(): pl.pallas_call(body, out_shape=tuple((jax.ShapeDtypeStruct(shape, kind) f...  11.8 us
    ppermute x2, starting transfers between devices, moved(): return lax.ppermute(x, ('inner', 'outer'), route)  6.45 us
    ppermute x4, starting transfers between devices, returned(): return lax.ppermute(x, ('inner', 'outer'), route)  4.44 us
    ppermute x1, starting transfers between devices, grouped(): lax.ppermute(x, 'outer', [(i, (i + distance) % outer_count) for i in rang...  3 us
    ppermute x13, waiting for transfers between devices, swapped(): return lax.ppermute(x, 'inner', [(i, i ^ d) for i in range(inner_count)])  1.02 us
  transfers between devices with their start and end apart: 20, of which 4 were waited for; matrix products, arithmetic and copies ran while one was open for 1% of the time, Pallas kernels for 18%

profile of v7, /device:TPU:0, one launch (start us, length us, event | category | flops | bytes accessed | tf_op | source)
XLA Modules:
  0.0 40.8 jit_solution(10730515415004371762)
XLA Ops:
  0.6 0.8 %pack.1 = bf16[128,256]{1,0:T(8,128)(2,1)S(1)} custom-call(bf16[128,128]{1,0:T(8,128)(2,1)} %k_hbm.1, bf16[128,128]{1,0:T(8,128)(2,1)} %v_hbm.1), custom_call_target="tpu_custom_call" | custom-call | bytes 65536 | tf_op jit(solution)/shard_map/pack/pallas_call | solution.py:242
  1.4 3.0 %collective-permute-start.1 = (bf16[128,256]{1,0:T(8,128)(2,1)S(1)}, bf16[128,256]{1,0:T(8,128)(2,1)S(1)}, u32[]{:S(2)}, u32[]{:S(2)}) collective-permute-start(bf16[128,256]{1,0:T(8,128)(2,1)S(1)} %pack.1), channel_id=1, source_target_pairs={{0,1},{1,0},{2,3},{3,2},{4,5},{5,4},{6,7},{7,6},{8,9},{9,8},{10,11... | collective-permute-start | bytes 196616 | tf_op jit(solution)/shard_map/ppermute | solution.py:273
  4.4 2.6 %collective-permute-start = (bf16[128,256]{1,0:T(8,128)(2,1)S(1)}, bf16[128,256]{1,0:T(8,128)(2,1)S(1)}, u32[]{:S(2)}, u32[]{:S(2)}) collective-permute-start(bf16[128,256]{1,0:T(8,128)(2,1)S(1)} %pack.1), channel_id=1, source_target_pairs={{0,16},{2,18},{4,20},{6,22},{8,24},{10,26},{12,28},{14,30},{16,1},... | collective-permute-start | bytes 196616 | tf_op jit(solution)/shard_map/ppermute | solution.py:270
  7.0 0.0 collective-permute-done.1
  7.1 2.8 %collective-permute-start.4 = (bf16[128,256]{1,0:T(8,128)(2,1)S(1)}, bf16[128,256]{1,0:T(8,128)(2,1)S(1)}, u32[]{:S(2)}, u32[]{:S(2)}) collective-permute-start(bf16[128,256]{1,0:T(8,128)(2,1)S(1)} %get-tuple-element.82), channel_id=1, source_target_pairs={{0,12},{2,14},{4,8},{6,10},{8,4},{10,6},{12,0},{14,2},{16,28},{18,... | collective-permute-start | bytes 196616 | tf_op jit(solution)/shard_map/ppermute | solution.py:283
  9.9 0.4 %collective-permute-start.3 = (bf16[128,256]{1,0:T(8,128)(2,1)S(1)}, bf16[128,256]{1,0:T(8,128)(2,1)S(1)}, u32[]{:S(2)}, u32[]{:S(2)}) collective-permute-start(bf16[128,256]{1,0:T(8,128)(2,1)S(1)} %get-tuple-element.83), channel_id=1, source_target_pairs={{0,8},{2,10},{4,12},{6,14},{8,0},{10,2},{12,4},{14,6},{16,24},{18,... | collective-permute-start | bytes 196616 | tf_op jit(solution)/shard_map/ppermute | solution.py:283
  10.3 0.3 collective-permute-start.2
  10.6 0.2 collective-permute-done
  10.8 1.6 %collective-permute-start.6 = (bf16[128,256]{1,0:T(8,128)(2,1)S(1)}, bf16[128,256]{1,0:T(8,128)(2,1)S(1)}, u32[]{:S(2)}, u32[]{:S(2)}) collective-permute-start(bf16[128,256]{1,0:T(8,128)(2,1)S(1)} %collective-permute-done), channel_id=1, source_target_pairs={{0,4},{2,6},{4,0},{6,2},{8,12},{10,14},{12,8},{14,10},{16,20},{18,... | collective-permute-start | bytes 196616 | tf_op jit(solution)/shard_map/ppermute | solution.py:283
  12.4 1.4 %collective-permute-start.5 = (bf16[128,256]{1,0:T(8,128)(2,1)S(1)}, bf16[128,256]{1,0:T(8,128)(2,1)S(1)}, u32[]{:S(2)}, u32[]{:S(2)}) collective-permute-start(bf16[128,256]{1,0:T(8,128)(2,1)S(1)} %collective-permute-done), channel_id=1, source_target_pairs={{0,12},{2,14},{4,8},{6,10},{8,4},{10,6},{12,0},{14,2},{16,28},{18,... | collective-permute-start | bytes 196616 | tf_op jit(solution)/shard_map/ppermute | solution.py:283
  13.9 0.4 collective-permute-done.3
  14.2 1.0 %collective-permute-start.7 = (bf16[128,256]{1,0:T(8,128)(2,1)S(1)}, bf16[128,256]{1,0:T(8,128)(2,1)S(1)}, u32[]{:S(2)}, u32[]{:S(2)}) collective-permute-start(bf16[128,256]{1,0:T(8,128)(2,1)S(1)} %collective-permute-done), channel_id=1, source_target_pairs={{0,8},{2,10},{4,12},{6,14},{8,0},{10,2},{12,4},{14,6},{16,24},{18,... | collective-permute-start | bytes 196616 | tf_op jit(solution)/shard_map/ppermute | solution.py:283
  15.3 0.1 collective-permute-start.9
  15.4 2.5 %early.1 = (bf16[128,1024]{1,0:T(8,128)(2,1)S(1)}, bf16[128,1024]{1,0:T(8,128)(2,1)S(1)}, f32[128,256]{1,0:T(8,128)S(1)}, bf16[640,1024]{1,0:T(8,128)(2,1)S(1)},...) custom-call(s32[32]{0:T(128)} %doc_hbm.1, s32[1]{0:T(128)} %bitcast.at_ref, ...), custom_call_target="tpu_custom_call" | custom-call | flops 6710886400 | bytes 65536 | tf_op jit(solution)/shard_map/early/pallas_call | solution.py:242
  17.9 0.6 %collective-permute-done.7 = bf16[128,256]{1,0:T(8,128)(2,1)S(1)} collective-permute-done((bf16[128,256]{1,0:T(8,128)(2,1)S(1)}, bf16[128,256]{1,0:T(8,128)(2,1)S(1)}, u32[]{:S(2)}, u32[]{:S(2)}) %collective-permute-start.7) | collective-permute-done | bytes 65568 | tf_op jit(solution)/shard_map/ppermute | solution.py:283
  18.5 0.1 collective-permute-start.8
  18.7 1.9 %middle.1 = (bf16[1024,1024]{1,0:T(8,128)(2,1)S(1)}, f32[1024,1024]{1,0:T(8,128)S(1)}, f32[144,1024]{1,0:T(8,128)S(1)}, f32[8,1024]{1,0:T(8,128)S(1)}) custom-call(f32[128,256]{1,0:T(8,128)S(1)} %get-tuple-element.41.bias_ref.refs_0_, bf16[128,1024]{1,0:T(8,128)(2,1)S(1)} %get-tuple-element.42.qt_ref.refs_1_, ...), custom_call_target="tpu_custom_call" | custom-call | flops 10737418240 | bytes 65536 | tf_op jit(solution)/shard_map/middle/pallas_call | solution.py:242
  20.6 3.7 %main.1 = (bf16[128,256]{1,0:T(8,128)(2,1)S(1)}, bf16[384,256]{1,0:T(8,128)(2,1)S(1)}, bf16[512,256]{1,0:T(8,128)(2,1)S(1)}, bf16[640,1024]{1,0:T(8,128)(2,1)S(1...) custom-call(f32[128,256]{1,0:T(8,128)S(1)} %get-tuple-element.41.bia, ...), custom_call_target="tpu_custom_call" | custom-call | flops 3221225472 | bytes 65536 | tf_op jit(solution)/shard_map/main/pallas_call | solution.py:242
  24.3 0.5 %collective-permute-start.10 = (bf16[512,256]{1,0:T(8,128)(2,1)S(1)}, bf16[512,256]{1,0:T(8,128)(2,1)S(1)}, u32[]{:S(2)}, u32[]{:S(2)}) collective-permute-start(bf16[512,256]{1,0:T(8,128)(2,1)S(1)} %get-tuple-element.63), channel_id=1, source_target_pairs={{0,2},{2,0},{4,6},{6,4},{8,10},{10,8},{12,14},{14,12},{16,18},{18,... | collective-permute-start | bytes 786440 | tf_op jit(solution)/shard_map/ppermute | solution.py:283
  24.9 0.1 collective-permute-start.14
  24.9 1.2 %kept.1 = (bf16[128,256]{1,0:T(8,128)(2,1)S(1)}, bf16[128,256]{1,0:T(8,128)(2,1)S(1)}, bf16[384,256]{1,0:T(8,128)(2,1)S(1)}, bf16[384,256]{1,0:T(8,128)(2,1)S(1)}) custom-call(bf16[640,1024]{1,0:T(8,128)(2,1)S(1)} %get-tuple-element.40.refs_4_.refs_0_, bf16[640,1024]{1,0:T(8,128)(2,1)S(1)} %get-tuple-element.56.refs_1_.refs_0_, ...), custom_call_target="tpu_custom_call" | custom-call | flops 536870912 | bytes 65536 | tf_op jit(solution)/shard_map/kept/pallas_call | solution.py:242
  26.3 1.7 %collective-permute-start.11 = (bf16[128,256]{1,0:T(8,128)(2,1)S(1)}, bf16[128,256]{1,0:T(8,128)(2,1)S(1)}, u32[]{:S(2)}, u32[]{:S(2)}) collective-permute-start(bf16[128,256]{1,0:T(8,128)(2,1)S(1)} %get-tuple-element.75), channel_id=1, source_target_pairs={{0,12},{2,14},{4,8},{6,10},{8,4},{10,6},{12,0},{14,2},{16,28},{18,... | collective-permute-start | bytes 196616 | tf_op jit(solution)/shard_map/ppermute | solution.py:283
  27.9 1.2 %collective-permute-start.13 = (bf16[128,256]{1,0:T(8,128)(2,1)S(1)}, bf16[128,256]{1,0:T(8,128)(2,1)S(1)}, u32[]{:S(2)}, u32[]{:S(2)}) collective-permute-start(bf16[128,256]{1,0:T(8,128)(2,1)S(1)} %get-tuple-element.76), channel_id=1, source_target_pairs={{0,4},{2,6},{4,0},{6,2},{8,12},{10,14},{12,8},{14,10},{16,20},{18,... | collective-permute-start | bytes 196616 | tf_op jit(solution)/shard_map/ppermute | solution.py:283
  29.2 0.6 %collective-permute-start.12 = (bf16[128,256]{1,0:T(8,128)(2,1)S(1)}, bf16[128,256]{1,0:T(8,128)(2,1)S(1)}, u32[]{:S(2)}, u32[]{:S(2)}) collective-permute-start(bf16[128,256]{1,0:T(8,128)(2,1)S(1)} %get-tuple-element.77), channel_id=1, source_target_pairs={{0,8},{2,10},{4,12},{6,14},{8,0},{10,2},{12,4},{14,6},{16,24},{18,... | collective-permute-start | bytes 196616 | tf_op jit(solution)/shard_map/ppermute | solution.py:283
  29.9 2.5 %collective-permute-start.15 = (bf16[128,256]{1,0:T(8,128)(2,1)S(1)}, bf16[128,256]{1,0:T(8,128)(2,1)S(1)}, u32[]{:S(2)}, u32[]{:S(2)}) collective-permute-start(bf16[128,256]{1,0:T(8,128)(2,1)S(1)} %get-tuple-element.78), channel_id=1, source_target_pairs={{0,13},{2,15},{4,9},{6,11},{8,4},{10,6},{12,0},{14,2},{16,29},{18,... | collective-permute-start | bytes 196616 | tf_op jit(solution)/shard_map/ppermute | solution.py:280
  32.4 1.3 %collective-permute-start.17 = (bf16[128,256]{1,0:T(8,128)(2,1)S(1)}, bf16[128,256]{1,0:T(8,128)(2,1)S(1)}, u32[]{:S(2)}, u32[]{:S(2)}) collective-permute-start(bf16[128,256]{1,0:T(8,128)(2,1)S(1)} %get-tuple-element.79), channel_id=1, source_target_pairs={{0,5},{2,7},{4,0},{6,2},{8,13},{10,15},{12,8},{14,10},{16,21},{18,... | collective-permute-start | bytes 196616 | tf_op jit(solution)/shard_map/ppermute | solution.py:280
  33.7 0.6 %collective-permute-start.16 = (bf16[128,256]{1,0:T(8,128)(2,1)S(1)}, bf16[128,256]{1,0:T(8,128)(2,1)S(1)}, u32[]{:S(2)}, u32[]{:S(2)}) collective-permute-start(bf16[128,256]{1,0:T(8,128)(2,1)S(1)} %get-tuple-element.80), channel_id=1, source_target_pairs={{0,9},{2,11},{4,13},{6,15},{8,0},{10,2},{12,4},{14,6},{16,25},{18,... | collective-permute-start | bytes 196616 | tf_op jit(solution)/shard_map/ppermute | solution.py:280
  34.4 3.9 %collective-permute-start.19 = (bf16[128,256]{1,0:T(8,128)(2,1)S(1)}, bf16[128,256]{1,0:T(8,128)(2,1)S(1)}, u32[]{:S(2)}, u32[]{:S(2)}) collective-permute-start(bf16[128,256]{1,0:T(8,128)(2,1)S(1)} %add_convert_fusion.4), channel_id=1, source_target_pairs={{0,17},{2,19},{4,21},{6,23},{8,25},{10,27},{12,29},{14,31},{16,0},... | collective-permute-start | bytes 196616 | tf_op jit(solution)/shard_map/ppermute | solution.py:270
  38.2 1.6 %query.1 = bf16[128,1024]{1,0:T(8,128)(2,1)} custom-call(bf16[128,256]{1,0:T(8,128)(2,1)S(1)} %get-tuple-element.66.unused_ref, bf16[640,1024]{1,0:T(8,128)(2,1)S(1)} %get-tuple-element.56.refs_1_.refs_0_, bf16[1024,1024]{1,0:T(8,128)(2,1)S(1)} %get-tuple-element.59.refs_5_.refs_1_, bf16[384,1024]{1,0:T(8,128)(2,1)S(1)} %get-tuple-element.67.refs_2_, ...), custom_call_target="tpu_custom_call" | custom-call | flops 536870912 | bytes 65536 | tf_op jit(solution)/shard_map/query/pallas_call | solution.py:242
  39.9 0.3 collective-permute-done.19
  40.2 0.1 add_convert_fusion
  40.2 0.6 %fusion = (bf16[128,128]{1,0:T(8,128)(2,1)}, bf16[128,128]{1,0:T(8,128)(2,1)}) fusion(bf16[128,256]{1,0:T(8,128)(2,1)S(1)} %add_convert_fusion), kind=kLoop, calls=%fused_computation.26 | loop fusion | bytes 131072 | tf_op jit(solution)/shard_map/slice | solution.py:415
  (29 shorter events, 0.3 us)
Async XLA Ops:
  1.4 5.6 %collective-permute-start.1 = (bf16[128,256]{1,0:T(8,128)(2,1)S(1)}, bf16[128,256]{1,0:T(8,128)(2,1)S(1)}, u32[]{:S(2)}, u32[]{:S(2)}) collective-permute-start(bf16[128,256]{1,0:T(8,128)(2,1)S(1)} %pack.1), channel_id=1, source_target_pairs={{0,1},{1,0},{2,3},{3,2},{4,5},{5,4},{6,7},{7,6},{8,9},{9,8},{10,11... | collective-permute-start | bytes 196616 | tf_op jit(solution)/shard_map/ppermute | solution.py:273
  4.4 6.4 %collective-permute-start = (bf16[128,256]{1,0:T(8,128)(2,1)S(1)}, bf16[128,256]{1,0:T(8,128)(2,1)S(1)}, u32[]{:S(2)}, u32[]{:S(2)}) collective-permute-start(bf16[128,256]{1,0:T(8,128)(2,1)S(1)} %pack.1), channel_id=1, source_target_pairs={{0,16},{2,18},{4,20},{6,22},{8,24},{10,26},{12,28},{14,30},{16,1},... | collective-permute-start | bytes 196616 | tf_op jit(solution)/shard_map/ppermute | solution.py:270
  7.1 8.2 %collective-permute-start.4 = (bf16[128,256]{1,0:T(8,128)(2,1)S(1)}, bf16[128,256]{1,0:T(8,128)(2,1)S(1)}, u32[]{:S(2)}, u32[]{:S(2)}) collective-permute-start(bf16[128,256]{1,0:T(8,128)(2,1)S(1)} %get-tuple-element.82), channel_id=1, source_target_pairs={{0,12},{2,14},{4,8},{6,10},{8,4},{10,6},{12,0},{14,2},{16,28},{18,... | collective-permute-start | bytes 196616 | tf_op jit(solution)/shard_map/ppermute | solution.py:283
  9.9 4.4 %collective-permute-start.3 = (bf16[128,256]{1,0:T(8,128)(2,1)S(1)}, bf16[128,256]{1,0:T(8,128)(2,1)S(1)}, u32[]{:S(2)}, u32[]{:S(2)}) collective-permute-start(bf16[128,256]{1,0:T(8,128)(2,1)S(1)} %get-tuple-element.83), channel_id=1, source_target_pairs={{0,8},{2,10},{4,12},{6,14},{8,0},{10,2},{12,4},{14,6},{16,24},{18,... | collective-permute-start | bytes 196616 | tf_op jit(solution)/shard_map/ppermute | solution.py:283
  10.3 4.9 %collective-permute-start.2 = (bf16[128,256]{1,0:T(8,128)(2,1)S(1)}, bf16[128,256]{1,0:T(8,128)(2,1)S(1)}, u32[]{:S(2)}, u32[]{:S(2)}) collective-permute-start(bf16[128,256]{1,0:T(8,128)(2,1)S(1)} %get-tuple-element.84), channel_id=1, source_target_pairs={{0,4},{2,6},{4,0},{6,2},{8,12},{10,14},{12,8},{14,10},{16,20},{18,... | collective-permute-start | bytes 196616 | tf_op jit(solution)/shard_map/ppermute | solution.py:283
  10.8 7.1 %collective-permute-start.6 = (bf16[128,256]{1,0:T(8,128)(2,1)S(1)}, bf16[128,256]{1,0:T(8,128)(2,1)S(1)}, u32[]{:S(2)}, u32[]{:S(2)}) collective-permute-start(bf16[128,256]{1,0:T(8,128)(2,1)S(1)} %collective-permute-done), channel_id=1, source_target_pairs={{0,4},{2,6},{4,0},{6,2},{8,12},{10,14},{12,8},{14,10},{16,20},{18,... | collective-permute-start | bytes 196616 | tf_op jit(solution)/shard_map/ppermute | solution.py:283
  12.4 5.5 %collective-permute-start.5 = (bf16[128,256]{1,0:T(8,128)(2,1)S(1)}, bf16[128,256]{1,0:T(8,128)(2,1)S(1)}, u32[]{:S(2)}, u32[]{:S(2)}) collective-permute-start(bf16[128,256]{1,0:T(8,128)(2,1)S(1)} %collective-permute-done), channel_id=1, source_target_pairs={{0,12},{2,14},{4,8},{6,10},{8,4},{10,6},{12,0},{14,2},{16,28},{18,... | collective-permute-start | bytes 196616 | tf_op jit(solution)/shard_map/ppermute | solution.py:283
  14.2 4.3 %collective-permute-start.7 = (bf16[128,256]{1,0:T(8,128)(2,1)S(1)}, bf16[128,256]{1,0:T(8,128)(2,1)S(1)}, u32[]{:S(2)}, u32[]{:S(2)}) collective-permute-start(bf16[128,256]{1,0:T(8,128)(2,1)S(1)} %collective-permute-done), channel_id=1, source_target_pairs={{0,8},{2,10},{4,12},{6,14},{8,0},{10,2},{12,4},{14,6},{16,24},{18,... | collective-permute-start | bytes 196616 | tf_op jit(solution)/shard_map/ppermute | solution.py:283
  15.3 3.4 %collective-permute-start.9 = (bf16[640,256]{1,0:T(8,128)(2,1)S(1)}, bf16[640,256]{1,0:T(8,128)(2,1)S(1)}, u32[]{:S(2)}, u32[]{:S(2)}) collective-permute-start(bf16[640,256]{1,0:T(8,128)(2,1)S(1)} %get-tuple-element.87), channel_id=1, source_target_pairs={{0,2},{2,0},{4,6},{6,4},{8,10},{10,8},{12,14},{14,12},{16,18},{18,... | collective-permute-start | bytes 983048 | tf_op jit(solution)/shard_map/ppermute | solution.py:283
  18.5 2.1 %collective-permute-start.8 = (bf16[384,256]{1,0:T(8,128)(2,1)S(1)}, bf16[384,256]{1,0:T(8,128)(2,1)S(1)}, u32[]{:S(2)}, u32[]{:S(2)}) collective-permute-start(bf16[384,256]{1,0:T(8,128)(2,1)S(1)} %pad_maximum_fusion), channel_id=1, source_target_pairs={{0,2},{2,0},{4,6},{6,4},{8,10},{10,8},{12,14},{14,12},{16,18},{18,... | collective-permute-start | bytes 589832 | tf_op jit(solution)/shard_map/ppermute | solution.py:283
  24.3 1.9 %collective-permute-start.10 = (bf16[512,256]{1,0:T(8,128)(2,1)S(1)}, bf16[512,256]{1,0:T(8,128)(2,1)S(1)}, u32[]{:S(2)}, u32[]{:S(2)}) collective-permute-start(bf16[512,256]{1,0:T(8,128)(2,1)S(1)} %get-tuple-element.63), channel_id=1, source_target_pairs={{0,2},{2,0},{4,6},{6,4},{8,10},{10,8},{12,14},{14,12},{16,18},{18,... | collective-permute-start | bytes 786440 | tf_op jit(solution)/shard_map/ppermute | solution.py:283
  24.9 5.0 %collective-permute-start.14 = (bf16[384,256]{1,0:T(8,128)(2,1)S(1)}, bf16[384,256]{1,0:T(8,128)(2,1)S(1)}, u32[]{:S(2)}, u32[]{:S(2)}) collective-permute-start(bf16[384,256]{1,0:T(8,128)(2,1)S(1)} %get-tuple-element.73), channel_id=1, source_target_pairs={{0,2},{2,0},{4,6},{6,4},{8,10},{10,8},{12,14},{14,12},{16,18},{18,... | collective-permute-start | bytes 589832 | tf_op jit(solution)/shard_map/ppermute | solution.py:283
  26.3 7.4 %collective-permute-start.11 = (bf16[128,256]{1,0:T(8,128)(2,1)S(1)}, bf16[128,256]{1,0:T(8,128)(2,1)S(1)}, u32[]{:S(2)}, u32[]{:S(2)}) collective-permute-start(bf16[128,256]{1,0:T(8,128)(2,1)S(1)} %get-tuple-element.75), channel_id=1, source_target_pairs={{0,12},{2,14},{4,8},{6,10},{8,4},{10,6},{12,0},{14,2},{16,28},{18,... | collective-permute-start | bytes 196616 | tf_op jit(solution)/shard_map/ppermute | solution.py:283
  27.9 6.4 %collective-permute-start.13 = (bf16[128,256]{1,0:T(8,128)(2,1)S(1)}, bf16[128,256]{1,0:T(8,128)(2,1)S(1)}, u32[]{:S(2)}, u32[]{:S(2)}) collective-permute-start(bf16[128,256]{1,0:T(8,128)(2,1)S(1)} %get-tuple-element.76), channel_id=1, source_target_pairs={{0,4},{2,6},{4,0},{6,2},{8,12},{10,14},{12,8},{14,10},{16,20},{18,... | collective-permute-start | bytes 196616 | tf_op jit(solution)/shard_map/ppermute | solution.py:283
  29.2 5.1 %collective-permute-start.12 = (bf16[128,256]{1,0:T(8,128)(2,1)S(1)}, bf16[128,256]{1,0:T(8,128)(2,1)S(1)}, u32[]{:S(2)}, u32[]{:S(2)}) collective-permute-start(bf16[128,256]{1,0:T(8,128)(2,1)S(1)} %get-tuple-element.77), channel_id=1, source_target_pairs={{0,8},{2,10},{4,12},{6,14},{8,0},{10,2},{12,4},{14,6},{16,24},{18,... | collective-permute-start | bytes 196616 | tf_op jit(solution)/shard_map/ppermute | solution.py:283
  29.9 10.0 %collective-permute-start.15 = (bf16[128,256]{1,0:T(8,128)(2,1)S(1)}, bf16[128,256]{1,0:T(8,128)(2,1)S(1)}, u32[]{:S(2)}, u32[]{:S(2)}) collective-permute-start(bf16[128,256]{1,0:T(8,128)(2,1)S(1)} %get-tuple-element.78), channel_id=1, source_target_pairs={{0,13},{2,15},{4,9},{6,11},{8,4},{10,6},{12,0},{14,2},{16,29},{18,... | collective-permute-start | bytes 196616 | tf_op jit(solution)/shard_map/ppermute | solution.py:280
  32.4 7.5 %collective-permute-start.17 = (bf16[128,256]{1,0:T(8,128)(2,1)S(1)}, bf16[128,256]{1,0:T(8,128)(2,1)S(1)}, u32[]{:S(2)}, u32[]{:S(2)}) collective-permute-start(bf16[128,256]{1,0:T(8,128)(2,1)S(1)} %get-tuple-element.79), channel_id=1, source_target_pairs={{0,5},{2,7},{4,0},{6,2},{8,13},{10,15},{12,8},{14,10},{16,21},{18,... | collective-permute-start | bytes 196616 | tf_op jit(solution)/shard_map/ppermute | solution.py:280
  33.7 6.2 %collective-permute-start.16 = (bf16[128,256]{1,0:T(8,128)(2,1)S(1)}, bf16[128,256]{1,0:T(8,128)(2,1)S(1)}, u32[]{:S(2)}, u32[]{:S(2)}) collective-permute-start(bf16[128,256]{1,0:T(8,128)(2,1)S(1)} %get-tuple-element.80), channel_id=1, source_target_pairs={{0,9},{2,11},{4,13},{6,15},{8,0},{10,2},{12,4},{14,6},{16,25},{18,... | collective-permute-start | bytes 196616 | tf_op jit(solution)/shard_map/ppermute | solution.py:280
  34.4 5.8 %collective-permute-start.19 = (bf16[128,256]{1,0:T(8,128)(2,1)S(1)}, bf16[128,256]{1,0:T(8,128)(2,1)S(1)}, u32[]{:S(2)}, u32[]{:S(2)}) collective-permute-start(bf16[128,256]{1,0:T(8,128)(2,1)S(1)} %add_convert_fusion.4), channel_id=1, source_target_pairs={{0,17},{2,19},{4,21},{6,23},{8,25},{10,27},{12,29},{14,31},{16,0},... | collective-permute-start | bytes 196616 | tf_op jit(solution)/shard_map/ppermute | solution.py:270
  38.2 1.9 %collective-permute-start.18 = (bf16[128,256]{1,0:T(8,128)(2,1)S(1)}, bf16[128,256]{1,0:T(8,128)(2,1)S(1)}, u32[]{:S(2)}, u32[]{:S(2)}) collective-permute-start(bf16[128,256]{1,0:T(8,128)(2,1)S(1)} %get-tuple-element.66.unused_ref), channel_id=1, source_target_pairs={{0,3},{2,0},{4,7},{6,4},{8,11},{10,8},{12,15},{14,12},{16,19},{18,... | collective-permute-start | bytes 196616 | tf_op jit(solution)/shard_map/ppermute | solution.py:280
